TPU v7x, 32 devices: a whole 2x2x4 slice. The times are simulated.
32 devices in a mesh: dp: 4 (over z), ctx: 4 (over y, x), tp: 2 (over core).
Axes of the slice: x: 2, y: 2, z: 4, core: 2. Of those that a mesh axis runs over, the one named last changes fastest.
Arguments:
- activations: bfloat16 [4, 2048, 2048], P('dp', 'ctx'), may hold values from -6 to 6
- seg_ids: int32 [4, 2048], P('dp', 'ctx'), may hold values from 0 to 7, never falling along the last dimension, each value on 1 to 1024 neighbouring positions
- cotangent: bfloat16 [4, 2048, 2048], P('dp', 'ctx'), may hold values from -6 to 6
- q_weight: bfloat16 [2048, 256], P(('dp', 'ctx'), 'tp'), may hold values from -0.125 to 0.125
- k_weight: bfloat16 [2048, 256], P(('dp', 'ctx'), 'tp'), may hold values from -0.125 to 0.125
- v_weight: bfloat16 [2048, 2048], P(('dp', 'ctx'), 'tp'), may hold values from -0.125 to 0.125
- o_weight: bfloat16 [2048, 2048], P(('dp', 'ctx'), 'tp'), may hold values from -2 to 2
- gate_weight: bfloat16 [2048, 5632], P(('dp', 'ctx'), 'tp'), may hold values from -0.125 to 0.125
- up_weight: bfloat16 [2048, 5632], P(('dp', 'ctx'), 'tp'), may hold values from -0.125 to 0.125
- down_weight: bfloat16 [2048, 5632], P(('dp', 'ctx'), 'tp'), may hold values from -0.078125 to 0.078125
- attn_gain: bfloat16 [2048], P(('dp', 'ctx')), may hold values from 0.5 to 1.5
- mlp_gain: bfloat16 [2048], P(('dp', 'ctx')), may hold values from 0.5 to 1.5
Outputs:
- out_activations: bfloat16 [4, 2048, 2048], P('dp', 'ctx')
- grad_activations: float32 [4, 2048, 2048], P('dp', 'ctx')
- grad_q_weight: float32 [2048, 256], P(('dp', 'ctx'), 'tp')
- grad_k_weight: float32 [2048, 256], P(('dp', 'ctx'), 'tp')
- grad_v_weight: float32 [2048, 2048], P(('dp', 'ctx'), 'tp')
- grad_o_weight: float32 [2048, 2048], P(('dp', 'ctx'), 'tp')
- grad_gate_weight: float32 [2048, 5632], P(('dp', 'ctx'), 'tp')
- grad_up_weight: float32 [2048, 5632], P(('dp', 'ctx'), 'tp')
- grad_down_weight: float32 [2048, 5632], P(('dp', 'ctx'), 'tp')
- grad_attn_gain: float32 [2048], P(('dp', 'ctx'))
- grad_mlp_gain: float32 [2048], P(('dp', 'ctx'))
Inputs may be any that keep to these rules, and one draw needn't show every extreme that they name: `seg_ids`: along each sequence the document ids never fall; a document holds 1 to 1024 tokens and one holds exactly 1024.
All inputs are finite; a program needn't handle non-finite values.
Results may differ from a plain program's by a relative error of at most 0.017.
Values may be sent and summed in bfloat16 or wider, within the bound.
A program may use at most 256 MiB of HBM per device.

v0:
```python
import jax
import jax.numpy as jnp
from jax import lax
from jax.sharding import PartitionSpec as P

F = 16
DV = 128


EPSILON = 1e-05
PRECISE = lax.Precision.HIGHEST


def prefix(x, axis, join, neutral, backward):
    count = lax.axis_size(axis)
    place = lax.axis_index(axis)
    ahead = count - 1 - place if backward else place
    gathered = jax.tree.map(
        lambda a, kind: lax.all_gather(a.astype(kind), axis),
        x,
        (jnp.bfloat16, jnp.bfloat16, jnp.bfloat16),
    )
    state = jax.tree.map(lambda a, e: jnp.zeros_like(a) + jnp.asarray(e, a.dtype), x, neutral)

    def one(lap, state):
        source = count - 1 - lap if backward else lap
        return join(
            state,
            jax.tree.map(
                lambda a, own: lax.dynamic_index_in_dim(a, source, 0, False).astype(own.dtype),
                gathered,
                x,
            ),
        )

    return lax.fori_loop(0, ahead, one, state)


def taylor(features_in):
    feature_count = features_in.shape[-1]
    products = (features_in[..., :, None] * features_in[..., None, :]).reshape(
        features_in.shape[:-1] + (feature_count * feature_count,)
    )
    constant = jnp.ones(features_in.shape[:-1] + (1,), jnp.float32)
    return jnp.concatenate(
        [
            constant,
            features_in * feature_count ** (-0.25),
            products * (2.0 * feature_count) ** (-0.5),
        ],
        axis=-1,
    )


def taylor_back(features_in, incoming_gradient):
    feature_count = features_in.shape[-1]
    linear = incoming_gradient[..., 1 : 1 + feature_count] * feature_count ** (-0.25)
    square = incoming_gradient[..., 1 + feature_count :].reshape(
        incoming_gradient.shape[:-1] + (feature_count, feature_count)
    )
    paired = jnp.einsum(
        "...ab,...b->...a", square + jnp.swapaxes(square, -1, -2), features_in, precision=PRECISE
    )
    return linear + paired * (2.0 * feature_count) ** (-0.5)


def norm_backward_step(incoming_gradient, unit_normalized_rows, multiplier_term, gain_vector_row):
    rescaled_rows = incoming_gradient * gain_vector_row
    return multiplier_term * (
        rescaled_rows
        - unit_normalized_rows
        * jnp.mean(rescaled_rows * unit_normalized_rows, axis=1, keepdims=True)
    )


def join_states(earlier, later_part):
    is_empty = later_part[2] < 0.0
    retain = jnp.where(is_empty | (earlier[2] == later_part[2]), 1.0, 0.0).astype(jnp.float32)
    return (
        later_part[0] + retain * earlier[0],
        later_part[1] + retain * earlier[1],
        jnp.where(is_empty, earlier[2], later_part[2]),
    )


def shards(
    activations,
    seg_ids,
    cotangent,
    q_weight,
    k_weight,
    v_weight,
    o_weight,
    gate_weight,
    up_weight,
    down_weight,
    attn_gain,
    mlp_gain,
):
    layer_input_rows = activations[0].astype(jnp.float32)
    segment = seg_ids[0].astype(jnp.float32)
    tokens = layer_input_rows.shape[0]
    head_count = q_weight.shape[1] // F
    w_query, w_key, w_value, w_out, first_norm_gain = (
        lax.all_gather(q_weight, ("dp", "ctx"), axis=0, tiled=True),
        lax.all_gather(k_weight, ("dp", "ctx"), axis=0, tiled=True),
        lax.all_gather(v_weight, ("dp", "ctx"), axis=0, tiled=True),
        lax.all_gather(o_weight, ("dp", "ctx"), axis=0, tiled=True),
        lax.all_gather(attn_gain, ("dp", "ctx"), axis=0, tiled=True),
    )
    first_inverse_scale = lax.rsqrt(
        jnp.mean(layer_input_rows * layer_input_rows, axis=1, keepdims=True) + EPSILON
    )
    first_unit_rows = layer_input_rows * first_inverse_scale
    first_normalized = (first_unit_rows * first_norm_gain.astype(jnp.float32)).astype(jnp.bfloat16)
    queries = (
        jnp.dot(first_normalized, w_query, preferred_element_type=jnp.float32)
        .astype(jnp.bfloat16)
        .reshape(tokens, head_count, F)
    )
    key_heads = (
        jnp.dot(first_normalized, w_key, preferred_element_type=jnp.float32)
        .astype(jnp.bfloat16)
        .reshape(tokens, head_count, F)
    )
    value_heads = (
        jnp.dot(first_normalized, w_value, preferred_element_type=jnp.float32)
        .astype(jnp.bfloat16)
        .reshape(tokens, head_count, DV)
    )
    w_gate, w_up, w_down, second_norm_gain = (
        lax.all_gather(gate_weight, ("dp", "ctx"), axis=0, tiled=True),
        lax.all_gather(up_weight, ("dp", "ctx"), axis=0, tiled=True),
        lax.all_gather(down_weight, ("dp", "ctx"), axis=0, tiled=True),
        lax.all_gather(mlp_gain, ("dp", "ctx"), axis=0, tiled=True),
    )
    scores = jnp.einsum(
        "thf,shf->hts", queries, key_heads, preferred_element_type=jnp.float32
    ) * F ** (-0.5)
    places = jnp.arange(tokens)
    visible = (
        (places[:, None] >= places[None, :]) & (segment[:, None] == segment[None, :])
    ).astype(jnp.float32)
    weights = (visible * (1.0 + scores + 0.5 * scores * scores)).astype(jnp.bfloat16)
    query_float = queries.astype(jnp.float32)
    key_float = key_heads.astype(jnp.float32)
    value_float = value_heads.astype(jnp.float32)
    feat_q = taylor(query_float)
    feat_k = taylor(key_float)
    ending = segment[-1]
    owned = (segment == ending).astype(jnp.float32)[:, None, None]
    local_state = jnp.einsum("thf,thd->hfd", feat_k * owned, value_float, precision=PRECISE)
    local_total = jnp.sum(feat_k * owned, axis=0)
    empty_state = (jnp.zeros_like(local_state), jnp.zeros_like(local_total), jnp.float32(-1.0))
    prior_state, prior_total, before = prefix(
        (local_state, local_total, ending), "ctx", join_states, empty_state, False
    )
    inherit = (segment == before).astype(jnp.float32)
    numerator = jnp.einsum(
        "hts,shd->thd", weights, value_heads, preferred_element_type=jnp.float32
    ) + inherit[:, None, None] * jnp.einsum("thf,hfd->thd", feat_q, prior_state, precision=PRECISE)
    denominator = jnp.sum(weights.astype(jnp.float32), axis=2).T + inherit[:, None] * jnp.einsum(
        "thf,hf->th", feat_q, prior_total, precision=PRECISE
    )
    mixed_heads = numerator / denominator[:, :, None]
    heads_out = mixed_heads.reshape(tokens, head_count * DV).astype(jnp.bfloat16)
    attn_out = lax.psum(
        jnp.einsum("tc,dc->td", heads_out, w_out, preferred_element_type=jnp.float32), "tp"
    )
    residual_midpoint = layer_input_rows + attn_out
    second_inverse_scale = lax.rsqrt(
        jnp.mean(residual_midpoint * residual_midpoint, axis=1, keepdims=True) + EPSILON
    )
    second_unit_rows = residual_midpoint * second_inverse_scale
    second_normalized = (second_unit_rows * second_norm_gain.astype(jnp.float32)).astype(
        jnp.bfloat16
    )
    gate_value = jnp.dot(second_normalized, w_gate, preferred_element_type=jnp.float32)
    up_value = jnp.dot(second_normalized, w_up, preferred_element_type=jnp.float32)
    sigmoid_gate = jax.nn.sigmoid(gate_value)
    hidden = (gate_value * sigmoid_gate * up_value).astype(jnp.bfloat16)
    mlp_out = lax.psum(
        jnp.einsum("tc,dc->td", hidden, w_down, preferred_element_type=jnp.float32).astype(
            jnp.bfloat16
        ),
        "tp",
    ).astype(jnp.float32)
    final_out = residual_midpoint + mlp_out
    grad_out = cotangent[0].astype(jnp.float32)
    grad_branch_two = cotangent[0]
    grad_w_down = jnp.einsum(
        "td,tc->dc", grad_branch_two, hidden, preferred_element_type=jnp.float32
    )
    grad_hidden = jnp.dot(grad_branch_two, w_down, preferred_element_type=jnp.float32)
    grad_gate = (
        grad_hidden * up_value * sigmoid_gate * (1.0 + gate_value * (1.0 - sigmoid_gate))
    ).astype(jnp.bfloat16)
    grad_up = (grad_hidden * gate_value * sigmoid_gate).astype(jnp.bfloat16)
    grad_w_gate = jnp.einsum(
        "td,tc->dc", second_normalized, grad_gate, preferred_element_type=jnp.float32
    )
    grad_w_up = jnp.einsum(
        "td,tc->dc", second_normalized, grad_up, preferred_element_type=jnp.float32
    )
    grad_normed_part = jnp.einsum(
        "tc,dc->td", grad_gate, w_gate, preferred_element_type=jnp.float32
    ) + jnp.einsum("tc,dc->td", grad_up, w_up, preferred_element_type=jnp.float32)
    second_normalized_gradient = lax.psum(grad_normed_part.astype(jnp.bfloat16), "tp").astype(
        jnp.float32
    )
    second_gain_gradient = jnp.sum(second_normalized_gradient * second_unit_rows, axis=0)
    grad_middle = grad_out + norm_backward_step(
        second_normalized_gradient,
        second_unit_rows,
        second_inverse_scale,
        second_norm_gain.astype(jnp.float32),
    )
    mlp_grads = (
        lax.psum_scatter(grad_w_gate, ("dp", "ctx"), scatter_dimension=0, tiled=True),
        lax.psum_scatter(grad_w_up, ("dp", "ctx"), scatter_dimension=0, tiled=True),
        lax.psum_scatter(grad_w_down, ("dp", "ctx"), scatter_dimension=0, tiled=True),
        lax.psum_scatter(second_gain_gradient, ("dp", "ctx"), scatter_dimension=0, tiled=True),
    )
    grad_branch_one = grad_middle.astype(jnp.bfloat16)
    grad_w_out = jnp.einsum(
        "td,tc->dc", grad_branch_one, heads_out, preferred_element_type=jnp.float32
    )
    grad_heads_low = jnp.dot(grad_branch_one, w_out, preferred_element_type=jnp.float32).astype(
        jnp.bfloat16
    )
    grad_mixed = (
        lax.optimization_barrier(grad_heads_low).astype(jnp.float32).reshape(tokens, head_count, DV)
    )
    numer_low = (grad_mixed / denominator[:, :, None]).astype(jnp.bfloat16)
    grad_numer = lax.optimization_barrier(numer_low).astype(jnp.float32)
    grad_denom = -jnp.sum(grad_mixed * mixed_heads, axis=2) / denominator
    grad_weights = (
        jnp.einsum("thd,shd->hts", numer_low, value_heads, preferred_element_type=jnp.float32)
        + grad_denom.T[:, :, None]
    )
    grad_scores = (grad_weights * visible * (1.0 + scores)).astype(jnp.bfloat16)
    grad_value = jnp.einsum("hts,thd->shd", weights, numer_low, preferred_element_type=jnp.float32)
    grad_query = jnp.einsum(
        "hts,shf->thf", grad_scores, key_heads, preferred_element_type=jnp.float32
    ) * F ** (-0.5)
    grad_key = jnp.einsum(
        "hts,thf->shf", grad_scores, queries, preferred_element_type=jnp.float32
    ) * F ** (-0.5)
    grad_feat_q = inherit[:, None, None] * (
        jnp.einsum("thd,hfd->thf", grad_numer, prior_state, precision=PRECISE)
        + grad_denom[:, :, None] * prior_total[None]
    )
    carried_state = jnp.einsum(
        "thf,thd->hfd", feat_q * inherit[:, None, None], grad_numer, precision=PRECISE
    )
    carried_total = jnp.sum(feat_q * (inherit[:, None] * grad_denom)[:, :, None], axis=0)
    starting = segment[0]
    later_state, later_total, after_seg = prefix(
        (carried_state, carried_total, starting), "ctx", join_states, empty_state, True
    )
    reached = (segment == after_seg).astype(jnp.float32)[:, None, None]
    grad_feat_k = reached * (
        jnp.einsum("hfd,thd->thf", later_state, value_float, precision=PRECISE) + later_total[None]
    )
    grad_value = grad_value + reached * jnp.einsum(
        "thf,hfd->thd", feat_k, later_state, precision=PRECISE
    )
    grad_query = grad_query + taylor_back(query_float, grad_feat_q)
    grad_key = grad_key + taylor_back(key_float, grad_feat_k)
    grad_query_low = grad_query.reshape(tokens, head_count * F).astype(jnp.bfloat16)
    grad_key_low = grad_key.reshape(tokens, head_count * F).astype(jnp.bfloat16)
    grad_value_low = grad_value.reshape(tokens, head_count * DV).astype(jnp.bfloat16)
    grad_w_query = jnp.einsum(
        "td,tc->dc", first_normalized, grad_query_low, preferred_element_type=jnp.float32
    )
    grad_w_key = jnp.einsum(
        "td,tc->dc", first_normalized, grad_key_low, preferred_element_type=jnp.float32
    )
    grad_w_value = jnp.einsum(
        "td,tc->dc", first_normalized, grad_value_low, preferred_element_type=jnp.float32
    )
    grad_normed_sum = (
        jnp.einsum("tc,dc->td", grad_query_low, w_query, preferred_element_type=jnp.float32)
        + jnp.einsum("tc,dc->td", grad_key_low, w_key, preferred_element_type=jnp.float32)
        + jnp.einsum("tc,dc->td", grad_value_low, w_value, preferred_element_type=jnp.float32)
    )
    first_normalized_gradient = lax.psum(grad_normed_sum.astype(jnp.bfloat16), "tp").astype(
        jnp.float32
    )
    first_gain_gradient = jnp.sum(first_normalized_gradient * first_unit_rows, axis=0)
    grad_inputs = grad_middle + norm_backward_step(
        first_normalized_gradient,
        first_unit_rows,
        first_inverse_scale,
        first_norm_gain.astype(jnp.float32),
    )
    attn_grads = (
        lax.psum_scatter(grad_w_query, ("dp", "ctx"), scatter_dimension=0, tiled=True),
        lax.psum_scatter(grad_w_key, ("dp", "ctx"), scatter_dimension=0, tiled=True),
        lax.psum_scatter(grad_w_value, ("dp", "ctx"), scatter_dimension=0, tiled=True),
        lax.psum_scatter(grad_w_out, ("dp", "ctx"), scatter_dimension=0, tiled=True),
        lax.psum_scatter(first_gain_gradient, ("dp", "ctx"), scatter_dimension=0, tiled=True),
    )
    return (
        final_out.astype(jnp.bfloat16)[None],
        grad_inputs[None],
        attn_grads[0],
        attn_grads[1],
        attn_grads[2],
        attn_grads[3],
        mlp_grads[0],
        mlp_grads[1],
        mlp_grads[2],
        attn_grads[4],
        mlp_grads[3],
    )


def solution(mesh):
    placed = (
        P("dp", "ctx", None),
        P("dp", "ctx"),
        P("dp", "ctx", None),
        P(("dp", "ctx"), "tp"),
        P(("dp", "ctx"), "tp"),
        P(("dp", "ctx"), "tp"),
        P(("dp", "ctx"), "tp"),
        P(("dp", "ctx"), "tp"),
        P(("dp", "ctx"), "tp"),
        P(("dp", "ctx"), "tp"),
        P(("dp", "ctx")),
        P(("dp", "ctx")),
    )
    return jax.shard_map(
        shards,
        mesh=mesh,
        in_specs=placed,
        out_specs=(
            P("dp", "ctx", None),
            P("dp", "ctx", None),
            P(("dp", "ctx"), "tp"),
            P(("dp", "ctx"), "tp"),
            P(("dp", "ctx"), "tp"),
            P(("dp", "ctx"), "tp"),
            P(("dp", "ctx"), "tp"),
            P(("dp", "ctx"), "tp"),
            P(("dp", "ctx"), "tp"),
            P(("dp", "ctx")),
            P(("dp", "ctx")),
        ),
        check_vma=False,
    )
```

profile of v0, /device:TPU:0, one launch (start us, length us, event | category | flops | bytes accessed | tf_op | source)
XLA Modules:
  0.0 2840.1 jit_solution(801804439583956505)
XLA Ops:
  8.0 42.4 %all-gather.5 = bf16[16,1,128]{2,1,0:T(2,128)(2,1)S(1)} all-gather(bf16[1,1,128]{2,1,0:T(2,128)(2,1)} %bitcast.282), channel_id=1, replica_groups=mesh['dp'=4,'ctx'=4,'tp'=2] {'dp','ctx'}, dimensions={0}, use_global_device_ids=true | all-gather | bytes 4352 | tf_op jit(solution)/shard_map/all_gather | solution.py:109
  54.5 42.3 %all_gather.60 = bf16[2048,128]{1,0:T(8,128)(2,1)S(1)} all-gather(bf16[128,128]{1,0:T(8,128)(2,1)} %param.20), channel_id=1, replica_groups=mesh['dp'=4,'ctx'=4,'tp'=2] {'dp','ctx'}, dimensions={0}, use_global_device_ids=true | all-gather | bytes 557056 | tf_op jit(solution)/shard_map/all_gather | solution.py:106
  102.9 4.7 fusion.44
  116.1 10.2 all-reduce.5
  126.3 3.1 multiply_reduce_fusion.1
  129.4 8.3 all-gather.1
  137.7 40.2 %all_gather.59 = bf16[2048,128]{1,0:T(8,128)(2,1)S(1)} all-gather(bf16[128,128]{1,0:T(8,128)(2,1)S(1)} %copy-done.56), channel_id=1, replica_groups=mesh['dp'=4,'ctx'=4,'tp'=2] {'dp','ctx'}, dimensions={0}, use_global_device_ids=true | all-gather | bytes 557056 | tf_op jit(solution)/shard_map/all_gather | solution.py:105
  182.5 5.3 convert_reduce_fusion
  192.3 5.3 fusion.74
  197.6 7.0 fusion.89
  204.6 25.3 all-gather.17.cloned.1.call-done
  229.8 6.9 fusion.90
  238.7 38.4 %all-gather.6 = bf16[16,1,128]{2,1,0:T(2,128)(2,1)S(1)} all-gather(bf16[1,1,128]{2,1,0:T(2,128)(2,1)} %bitcast.283), channel_id=1, replica_groups=mesh['dp'=4,'ctx'=4,'tp'=2] {'dp','ctx'}, dimensions={0}, use_global_device_ids=true | all-gather | bytes 4352 | tf_op jit(solution)/shard_map/all_gather | solution.py:135
  277.7 2.9 multiply_reduce_fusion.2
  283.0 127.2 %all-gather.19.cloned.1.call-done = bf16[2048,2816]{1,0:T(8,128)(2,1)} async-done(((bf16[128,2816]{1,0:T(8,128)(2,1)}), bf16[2048,2816]{1,0:T(8,128)(2,1)}) %all-gather.19.cloned.1.call-update) | async-done | bytes 11534352 | tf_op jit(solution)/shard_map/all_gather | solution.py:132
  410.2 11.0 fusion.91
  421.3 132.3 %all-gather.21.cloned.1.call-done = bf16[2048,2816]{1,0:T(8,128)(2,1)} async-done(((bf16[128,2816]{1,0:T(8,128)(2,1)}), bf16[2048,2816]{1,0:T(8,128)(2,1)}) %all-gather.21.cloned.1.call-update) | async-done | bytes 11534352 | tf_op jit(solution)/shard_map/all_gather | solution.py:133
  553.6 12.5 fusion.92
  566.2 131.0 %all-gather.23.cloned.1.call-done = bf16[2048,2816]{1,0:T(8,128)(2,1)} async-done(((bf16[128,2816]{1,0:T(8,128)(2,1)}), bf16[2048,2816]{1,0:T(8,128)(2,1)}) %all-gather.23.cloned.1.call-update) | async-done | bytes 11534352 | tf_op jit(solution)/shard_map/all_gather | solution.py:134
  697.1 14.9 multiply_convert_fusion.2
  712.0 12.5 fusion.93
  724.6 9.1 add_convert_fusion.1
  733.7 11.1 convolution_convert_fusion
  744.8 8.4 all-reduce.13.cloned.1.call-done
  753.2 4.8 fusion.21
  761.3 3.3 convolution_convert_fusion.1
  767.4 5.1 fusion.45
  781.5 8.7 all-gather.4
  790.2 3.6 fusion.33
  804.2 7.0 all-gather.27.cloned.1.call-done
  811.3 12.1 while.31
  826.6 3.6 fusion.30
  831.5 4.4 add_convert_fusion.3
  842.3 13.7 convolution_bitcast_fusion
  861.7 8.2 fusion.62
  871.2 5.9 fusion.79
  877.1 14.2 fusion.97
  891.3 13.0 fusion.98
  906.2 2.9 fusion.24
  909.1 80.1 %all-reduce.4 = (f32[2048]{0:T(1024)S(1)}, f32[2048]{0:T(1024)S(1)}) all-reduce(f32[2048]{0:T(1024)S(1)} %get-tuple-element.208, f32[2048]{0:T(1024)S(1)} %copy-done.55), channel_id=14, replica_groups=mesh['dp'=4,'ctx'=4,'tp'=2] {'dp','ctx'}, use_global_device_ids=true, to_apply=%region_24.25.clone | all-reduce | flops 4096 | bytes 32768
  990.4 7.5 fusion.17
  997.9 351.6 %reduce-scatter.20.cloned.1.call-done = f32[128,2816]{0,1:T(8,128)} async-done(((f32[2048,2816]{0,1:T(8,128)}), f32[128,2816]{0,1:T(8,128)}) %reduce-scatter.20.cloned.1.call-update) | async-done | bytes 1441808 | tf_op jit(solution)/shard_map/reduce_scatter | solution.py:221
  1352.3 82.4 %reduce-scatter.8.cloned.1.call-done = f32[128,128]{1,0:T(8,128)} async-done(((f32[2048,128]{1,0:T(8,128)}), f32[128,128]{1,0:T(8,128)}) %reduce-scatter.8.cloned.1.call-update) | async-done | bytes 65552 | tf_op jit(solution)/shard_map/reduce_scatter | solution.py:298
  1434.8 77.0 %reduce-scatter.10.cloned.1.call-done = f32[128,128]{1,0:T(8,128)} async-done(((f32[2048,128]{1,0:T(8,128)}), f32[128,128]{1,0:T(8,128)}) %reduce-scatter.10.cloned.1.call-update) | async-done | bytes 65552 | tf_op jit(solution)/shard_map/reduce_scatter | solution.py:299
  1511.8 177.3 %reduce-scatter.14.cloned.1.call-done = f32[128,1024]{1,0:T(8,128)} async-done(((f32[2048,1024]{1,0:T(8,128)}), f32[128,1024]{1,0:T(8,128)}) %reduce-scatter.14.cloned.1.call-update) | async-done | bytes 524304 | tf_op jit(solution)/shard_map/reduce_scatter | solution.py:301
  1689.1 183.1 %reduce-scatter.12.cloned.1.call-done = f32[128,1024]{1,0:T(8,128)} async-done(((f32[2048,1024]{1,0:T(8,128)}), f32[128,1024]{1,0:T(8,128)}) %reduce-scatter.12.cloned.1.call-update) | async-done | bytes 524304 | tf_op jit(solution)/shard_map/reduce_scatter | solution.py:300
  1872.2 478.3 %reduce-scatter.16.cloned.1.call-done = f32[128,2816]{1,0:T(8,128)} async-done(((f32[2048,2816]{1,0:T(8,128)}), f32[128,2816]{1,0:T(8,128)}) %reduce-scatter.16.cloned.1.call-update) | async-done | bytes 1441808 | tf_op jit(solution)/shard_map/reduce_scatter | solution.py:219
  2350.5 482.6 %reduce-scatter.18.cloned.1.call-done = f32[128,2816]{1,0:T(8,128)} async-done(((f32[2048,2816]{1,0:T(8,128)}), f32[128,2816]{1,0:T(8,128)}) %reduce-scatter.18.cloned.1.call-update) | async-done | bytes 1441808 | tf_op jit(solution)/shard_map/reduce_scatter | solution.py:220
  (255 shorter events, 86.8 us)
Async XLA Ops:
  7.2 95.7 %all-gather.15.cloned.1.call-start = ((), (), s32[]{:S(2)}) async-start(), calls=%async_computation.7 | async-start | bytes 4456448 | tf_op jit(solution)/shard_map/all_gather | solution.py:107
  7.9 184.2 %all-gather.25.cloned.1.call-start = ((), (), s32[]{:S(2)}) async-start(), calls=%async_computation.21 | async-start | bytes 2795520 | tf_op jit(solution)/shard_map/all_gather | solution.py:19
  50.4 127.5 %copy-start.45 = (f32[16,1,128]{2,1,0:T(1,128)}, f32[16,1,128]{2,1,0:T(1,128)S(1)}, u32[]{:S(2)}) copy-start(f32[16,1,128]{2,1,0:T(1,128)S(1)} %convert_element_type.350) | copy-start | bytes 24580
  51.1 141.1 %copy-start.47 = (f32[1,512]{1,0:T(1,128)}, f32[1,512]{1,0:T(1,128)S(1)}, u32[]{:S(2)}) copy-start(f32[1,512]{1,0:T(1,128)S(1)} %convert_element_type.294) | copy-start | bytes 6148
  51.7 140.6 %copy-start.51 = (f32[273]{0:T(512)}, f32[273]{0:T(512)S(1)}, u32[]{:S(2)}) copy-start(f32[273]{0:T(512)S(1)} %pad.3.clone) | copy-start | bytes 3280
  53.8 124.2 %copy-start.57 = (f32[512]{0:T(512)}, f32[512]{0:T(512)S(1)}, u32[]{:S(2)}) copy-start(f32[512]{0:T(512)S(1)} %add_rsqrt_fusion.1) | copy-start | bytes 6148
  96.7 6.2 copy-start.9
  100.2 26.1 copy-start.24
  107.6 80.3 %copy-start.16 = (bf16[64,8,8,128]{3,2,1,0:T(8,128)(2,1)}, bf16[64,8,8,128]{3,2,1,0:T(8,128)(2,1)S(1)}, u32[]{:S(2)}) copy-start(bf16[64,8,8,128]{3,2,1,0:T(8,128)(2,1)S(1)} %fusion.44) | copy-start | bytes 3145732
  107.6 5.7 copy-start.63
  110.5 27.3 copy-start.56
  111.4 118.5 %all-gather.17.cloned.1.call-start = ((), (), s32[]{:S(2)}) async-start(), calls=%async_computation.8 | async-start | bytes 4456448 | tf_op jit(solution)/shard_map/all_gather | solution.py:108
  112.1 165.6 %all-reduce.11.cloned.1.call-start = ((), (), s32[]{:S(2)}) async-start(), calls=%async_computation.9 | async-start | bytes 8388608 | tf_op jit(solution)/shard_map/psum | solution.py:167
  178.9 9.0 copy-start.38
  179.8 8.1 copy-start.20
  192.2 5.3 copy-start.49
  192.2 5.3 copy-start.7
  192.2 5.3 copy-start.26
  236.7 173.5 %all-gather.19.cloned.1.call-start = ((), (), s32[]{:S(2)}) async-start(), calls=%async_computation.10 | async-start | bytes 12255232 | tf_op jit(solution)/shard_map/all_gather | solution.py:132
  237.3 316.3 %all-gather.21.cloned.1.call-start = ((), (), s32[]{:S(2)}) async-start(), calls=%async_computation.11 | async-start | bytes 12255232 | tf_op jit(solution)/shard_map/all_gather | solution.py:133
  237.9 459.2 %all-gather.23.cloned.1.call-start = ((), (), s32[]{:S(2)}) async-start(), calls=%async_computation.12 | async-start | bytes 12255232 | tf_op jit(solution)/shard_map/all_gather | solution.py:134
  238.6 514.6 %all-reduce.13.cloned.1.call-start = ((), (), s32[]{:S(2)}) async-start(), calls=%async_computation.13 | async-start | bytes 4194304 | tf_op jit(solution)/shard_map/psum | solution.py:208
  277.7 4.9 copy-start.43
  283.0 127.2 %copy-start.30 = (bf16[512,2048]{1,0:T(8,128)(2,1)}, bf16[512,2048]{1,0:T(8,128)(2,1)S(1)}, u32[]{:S(2)}) copy-start(bf16[512,2048]{1,0:T(8,128)(2,1)S(1)} %multiply_convert_fusion.5) | copy-start | bytes 6291460
  421.3 275.8 %copy-start.28 = (bf16[1,512,2048]{2,1,0:T(8,128)(2,1)S(1)}, bf16[1,512,2048]{2,1,0:T(8,128)(2,1)}, u32[]{:S(2)}) copy-start(bf16[1,512,2048]{2,1,0:T(8,128)(2,1)} %param.18) | copy-start | bytes 6291460
  697.1 27.4 slice-start.2
  697.1 27.4 slice-start.3
  712.0 12.5 copy-start.65
  712.0 12.5 copy-start.64
  712.0 12.5 slice-start.4
  733.6 77.6 %all-gather.27.cloned.1.call-start = ((), (), s32[]{:S(2)}) async-start(), calls=%async_computation.22 | async-start | bytes 2795520 | tf_op jit(solution)/shard_map/all_gather | solution.py:19
  773.4 132.8 %all-reduce.15.cloned.1.call-start = ((), (), s32[]{:S(2)}) async-start(), calls=%async_computation.23 | async-start | bytes 8388608 | tf_op jit(solution)/shard_map/psum | solution.py:182
  776.0 17.7 slice-start
  778.4 15.4 slice-start.1
  778.9 11.2 copy-start.50
  780.6 13.2 copy-start.17
  780.6 13.2 copy-start.21
  796.0 5.4 copy-start.12
  801.4 9.9 copy-start.62
  811.3 12.2 copy-start.48
  825.7 5.8 copy-start.18
  840.8 508.7 %reduce-scatter.20.cloned.1.call-start = ((), (), s32[]{:S(2)}) async-start(), calls=%async_computation.20 | async-start | bytes 24510464 | tf_op jit(solution)/shard_map/reduce_scatter | solution.py:221
  856.0 578.7 %reduce-scatter.8.cloned.1.call-start = ((), (), s32[]{:S(2)}) async-start(), calls=%async_computation.14 | async-start | bytes 1114112 | tf_op jit(solution)/shard_map/reduce_scatter | solution.py:298
  859.6 652.1 %reduce-scatter.10.cloned.1.call-start = ((), (), s32[]{:S(2)}) async-start(), calls=%async_computation.15 | async-start | bytes 1114112 | tf_op jit(solution)/shard_map/reduce_scatter | solution.py:299
  861.7 827.4 %reduce-scatter.14.cloned.1.call-start = ((), (), s32[]{:S(2)}) async-start(), calls=%async_computation.17 | async-start | bytes 8912896 | tf_op jit(solution)/shard_map/reduce_scatter | solution.py:301
  870.0 1002.2 %reduce-scatter.12.cloned.1.call-start = ((), (), s32[]{:S(2)}) async-start(), calls=%async_computation.16 | async-start | bytes 8912896 | tf_op jit(solution)/shard_map/reduce_scatter | solution.py:300
  877.1 1473.4 %reduce-scatter.16.cloned.1.call-start = ((), (), s32[]{:S(2)}) async-start(), calls=%async_computation.18 | async-start | bytes 24510464 | tf_op jit(solution)/shard_map/reduce_scatter | solution.py:219
  891.3 1941.8 %reduce-scatter.18.cloned.1.call-start = ((), (), s32[]{:S(2)}) async-start(), calls=%async_computation.19 | async-start | bytes 24510464 | tf_op jit(solution)/shard_map/reduce_scatter | solution.py:220
  (40 other events, 110.0 us)
Sparse Core Ops, SparseCore 0:
  10.8 83.8 all-gather.14
  111.5 37.9 all-gather.24
  152.3 77.5 all-gather.16
  236.9 27.0 all-reduce.10
  266.9 143.3 all-gather.18
  413.2 140.3 all-gather.20
  556.7 140.3 all-gather.22
  733.8 19.3 all-reduce.12
  773.5 37.6 all-gather.26
  840.9 27.6 all-reduce.14
  871.0 478.4 reduce-scatter.19
  1352.2 82.4 reduce-scatter.7
  1437.6 74.1 reduce-scatter.9
  1514.6 174.4 reduce-scatter.13
  1691.9 180.2 reduce-scatter.11
  1875.0 475.3 reduce-scatter.15
  2353.3 479.7 reduce-scatter.17
where the time goes:
time: 2850 us; the launch traced here: 2840 us
  waiting for transfers between devices  2270 us (80%)
  blocking collectives  271 us (10%)
  matrix products  199 us (7%)
  other arithmetic  44.8 us (2%)
  local copies, waits for them, and re-layouts  34.3 us (1%)
    reduce_scatter x1, waiting for transfers between devices, shards(): lax.psum_scatter(grad_w_up, ('dp', 'ctx'), scatter_dimension=0, tiled=True)  483 us
    reduce_scatter x1, waiting for transfers between devices, shards(): lax.psum_scatter(grad_w_gate, ('dp', 'ctx'), scatter_dimension=0, tiled=T...  478 us
    reduce_scatter x1, waiting for transfers between devices, shards(): lax.psum_scatter(grad_w_down, ('dp', 'ctx'), scatter_dimension=0, tiled=T...  352 us
    reduce_scatter x1, waiting for transfers between devices, shards(): lax.psum_scatter(grad_w_value, ('dp', 'ctx'), scatter_dimension=0, tiled=...  183 us
    reduce_scatter x1, waiting for transfers between devices, shards(): lax.psum_scatter(grad_w_out, ('dp', 'ctx'), scatter_dimension=0, tiled=True)  177 us
    all_gather x1, waiting for transfers between devices, shards(): lax.all_gather(up_weight, ('dp', 'ctx'), axis=0, tiled=True)  132 us
    all_gather x1, waiting for transfers between devices, shards(): lax.all_gather(down_weight, ('dp', 'ctx'), axis=0, tiled=True)  131 us
    all_gather x1, waiting for transfers between devices, shards(): lax.all_gather(gate_weight, ('dp', 'ctx'), axis=0, tiled=True)  127 us
  transfers between devices with their start and end apart: 17, of which 13 were waited for; matrix products, arithmetic and copies ran while one was open for 6% of the time, Pallas kernels for 0%

commit v1 on v0

--- a/solution.py
+++ b/solution.py
@@ -1,6 +1,8 @@
 import jax
 import jax.numpy as jnp
 from jax import lax
+from jax.experimental import pallas as pl
+from jax.experimental.pallas import tpu as pltpu
 from jax.sharding import PartitionSpec as P
 
 F = 16
@@ -9,6 +11,7 @@
 
 EPSILON = 1e-05
 PRECISE = lax.Precision.HIGHEST
+VMEM_MOST = 56 * 2**20
 
 
 def prefix(x, axis, join, neutral, backward):
@@ -316,6 +319,376 @@
     )
 
 
+BLOCK = 512
+
+
+def attention_forward(qkv, seg_rows, seg_cols, heads):
+    tokens = qkv.shape[0]
+    wide = heads * DV
+
+    def kernel(x_ref, row_ref, col_ref, mixed_ref, denom_ref, low_ref, ext_ref):
+        i = pl.program_id(0)
+
+        @pl.when(i == 0)
+        def _():
+            for h in range(heads):
+                ext_ref[:, 2 * h * DV : (2 * h + 1) * DV] = x_ref[:, h * DV : (h + 1) * DV]
+                ext_ref[:, (2 * h + 1) * DV : (2 * h + 2) * DV] = jnp.ones(
+                    (tokens, DV), jnp.bfloat16
+                )
+
+        base = pl.multiple_of(i * BLOCK, BLOCK)
+        own = row_ref[pl.ds(base, BLOCK), :]
+        place = lax.broadcasted_iota(jnp.int32, (BLOCK, BLOCK), 0) - lax.broadcasted_iota(
+            jnp.int32, (BLOCK, BLOCK), 1
+        )
+        queries = [
+            x_ref[pl.ds(base, BLOCK), wide + h * F : wide + (h + 1) * F] * jnp.bfloat16(F**-0.5)
+            for h in range(heads)
+        ]
+
+        def step(j, sums):
+            start = pl.multiple_of(j * BLOCK, BLOCK)
+            visible = (place >= start - base) & (own == col_ref[:, pl.ds(start, BLOCK)])
+            out = []
+            for h in range(heads):
+                keys = x_ref[
+                    pl.ds(start, BLOCK),
+                    wide + (heads + h) * F : wide + (heads + h + 1) * F,
+                ]
+                s = lax.dot_general(
+                    queries[h], keys, (((1,), (1,)), ((), ())), preferred_element_type=jnp.float32
+                )
+                a = jnp.where(visible, (0.5 * s + 1.0) * s + 1.0, 0.0).astype(jnp.bfloat16)
+                out.append(
+                    sums[h]
+                    + jnp.dot(
+                        a,
+                        ext_ref[pl.ds(start, BLOCK), 2 * h * DV : (2 * h + 2) * DV],
+                        preferred_element_type=jnp.float32,
+                    )
+                )
+            return tuple(out)
+
+        sums = lax.fori_loop(
+            0, i + 1, step, tuple(jnp.zeros((BLOCK, 2 * DV), jnp.float32) for _ in range(heads))
+        )
+        for h in range(heads):
+            denom = sums[h][:, DV:]
+            mixed = sums[h][:, :DV] / denom
+            mixed_ref[:, h * DV : (h + 1) * DV] = mixed
+            low_ref[:, h * DV : (h + 1) * DV] = mixed.astype(jnp.bfloat16)
+            denom_ref[:, h : h + 1] = denom[:, :1]
+
+    return pl.pallas_call(
+        kernel,
+        grid=(tokens // BLOCK,),
+        in_specs=[
+            pl.BlockSpec(qkv.shape, lambda i: (0, 0)),
+            pl.BlockSpec((tokens, 1), lambda i: (0, 0)),
+            pl.BlockSpec((1, tokens), lambda i: (0, 0)),
+        ],
+        out_specs=[
+            pl.BlockSpec((BLOCK, wide), lambda i: (i, 0)),
+            pl.BlockSpec((BLOCK, heads), lambda i: (i, 0)),
+            pl.BlockSpec((BLOCK, wide), lambda i: (i, 0)),
+        ],
+        out_shape=[
+            jax.ShapeDtypeStruct((tokens, wide), jnp.float32),
+            jax.ShapeDtypeStruct((tokens, heads), jnp.float32),
+            jax.ShapeDtypeStruct((tokens, wide), jnp.bfloat16),
+        ],
+        scratch_shapes=[pltpu.VMEM((tokens, 2 * wide), jnp.bfloat16)],
+        compiler_params=pltpu.CompilerParams(vmem_limit_bytes=VMEM_MOST),
+        cost_estimate=pl.CostEstimate(
+            flops=tokens * tokens * heads * 400, bytes_accessed=tokens * wide * 12, transcendentals=0
+        ),
+        name="attn_forward",
+    )(qkv, seg_rows, seg_cols)
+
+
+def attention_backward(qkv, g_mixed, mixed, denom, seg_rows, seg_cols, heads):
+    tokens = qkv.shape[0]
+    wide = heads * DV
+    blocks = tokens // BLOCK
+
+    def kernel(
+        x_ref, gm_ref, m_ref, d_ref, row_ref, col_ref, g_ref, gq_ref, numer_ref, gden_ref, key_ref
+    ):
+        j = pl.program_id(0)
+
+        @pl.when(j == 0)
+        def _():
+            gq_ref[...] = jnp.zeros_like(gq_ref)
+            for h in range(heads):
+                part = pl.ds(h * DV, DV)
+                gm = gm_ref[:, part].astype(jnp.float32)
+                inverse = 1.0 / d_ref[:, h : h + 1]
+                numer_ref[:, part] = (gm * inverse).astype(jnp.bfloat16)
+                down = -jnp.sum(gm * m_ref[:, part], axis=1, keepdims=True) * inverse
+                gden_ref[h : h + 1, :] = jnp.transpose(
+                    jnp.broadcast_to(down, (tokens, 128)), (1, 0)
+                )[:1, :]
+            key_ref[...] = jnp.transpose(
+                x_ref[:, wide : wide + 2 * heads * F].astype(jnp.float32), (1, 0)
+            ).astype(jnp.bfloat16)
+
+        start = pl.multiple_of(j * BLOCK, BLOCK)
+        own = row_ref[pl.ds(start, BLOCK), :]
+        place = lax.broadcasted_iota(jnp.int32, (BLOCK, BLOCK), 1) - lax.broadcasted_iota(
+            jnp.int32, (BLOCK, BLOCK), 0
+        )
+        values = [x_ref[pl.ds(start, BLOCK), h * DV : (h + 1) * DV] for h in range(heads)]
+        keys = [
+            x_ref[pl.ds(start, BLOCK), wide + (heads + h) * F : wide + (heads + h + 1) * F]
+            * jnp.bfloat16(F**-0.5)
+            for h in range(heads)
+        ]
+        across = [
+            key_ref[(heads + h) * F : (heads + h + 1) * F, pl.ds(start, BLOCK)]
+            * jnp.bfloat16(F**-0.5)
+            for h in range(heads)
+        ]
+
+        def step(i, sums):
+            base = pl.multiple_of(i * BLOCK, BLOCK)
+            visible = (place >= start - base) & (own == col_ref[:, pl.ds(base, BLOCK)])
+            out = []
+            for h in range(heads):
+                queries = x_ref[pl.ds(base, BLOCK), wide + h * F : wide + (h + 1) * F]
+                numer = numer_ref[pl.ds(base, BLOCK), h * DV : (h + 1) * DV]
+                s = lax.dot_general(
+                    keys[h], queries, (((1,), (1,)), ((), ())), preferred_element_type=jnp.float32
+                )
+                a = jnp.where(visible, (0.5 * s + 1.0) * s + 1.0, 0.0).astype(jnp.bfloat16)
+                ga = (
+                    lax.dot_general(
+                        values[h],
+                        numer,
+                        (((1,), (1,)), ((), ())),
+                        preferred_element_type=jnp.float32,
+                    )
+                    + gden_ref[h : h + 1, pl.ds(base, BLOCK)]
+                )
+                gs = jnp.where(visible, ga * (1.0 + s), 0.0).astype(jnp.bfloat16)
+                gv = sums[2 * h] + jnp.dot(a, numer, preferred_element_type=jnp.float32)
+                gk = sums[2 * h + 1] + jnp.dot(gs, queries, preferred_element_type=jnp.float32)
+                gq_ref[h * F : (h + 1) * F, pl.ds(base, BLOCK)] += jnp.dot(
+                    across[h], gs, preferred_element_type=jnp.float32
+                )
+                out += [gv, gk]
+            return tuple(out)
+
+        zeros = []
+        for h in range(heads):
+            zeros += [jnp.zeros((BLOCK, DV), jnp.float32), jnp.zeros((BLOCK, F), jnp.float32)]
+        sums = lax.fori_loop(j, blocks, step, tuple(zeros))
+        for h in range(heads):
+            g_ref[pl.ds(start, BLOCK), h * DV : (h + 1) * DV] = sums[2 * h].astype(jnp.bfloat16)
+            g_ref[
+                pl.ds(start, BLOCK), wide + (heads + h) * F : wide + (heads + h + 1) * F
+            ] = (sums[2 * h + 1] * F**-0.5).astype(jnp.bfloat16)
+
+        @pl.when(j == blocks - 1)
+        def _():
+            g_ref[:, wide : wide + heads * F] = jnp.transpose(gq_ref[...], (1, 0)).astype(
+                jnp.bfloat16
+            )
+
+    whole = lambda shape: pl.BlockSpec(shape, lambda j: (0, 0))
+    return pl.pallas_call(
+        kernel,
+        grid=(blocks,),
+        in_specs=[
+            whole(qkv.shape),
+            whole(g_mixed.shape),
+            whole(mixed.shape),
+            whole(denom.shape),
+            whole((tokens, 1)),
+            whole((1, tokens)),
+        ],
+        out_specs=whole(qkv.shape),
+        out_shape=jax.ShapeDtypeStruct(qkv.shape, jnp.bfloat16),
+        scratch_shapes=[
+            pltpu.VMEM((heads * F, tokens), jnp.float32),
+            pltpu.VMEM((tokens, wide), jnp.bfloat16),
+            pltpu.VMEM((8, tokens), jnp.float32),
+            pltpu.VMEM((2 * heads * F, tokens), jnp.bfloat16),
+        ],
+        compiler_params=pltpu.CompilerParams(vmem_limit_bytes=VMEM_MOST),
+        cost_estimate=pl.CostEstimate(
+            flops=tokens * tokens * heads * 800, bytes_accessed=tokens * wide * 12, transcendentals=0
+        ),
+        name="attn_backward",
+    )(qkv, g_mixed, mixed, denom, seg_rows, seg_cols)
+
+
+def by_columns(weight, parts):
+    rows, columns = weight.shape
+    return weight.reshape(rows, parts, columns // parts).transpose(1, 0, 2)
+
+
+def to_owner(packed):
+    summed = lax.psum_scatter(packed, "dp", scatter_dimension=0, tiled=True)
+    parts = lax.axis_size("ctx")
+    return lax.all_to_all(
+        summed.reshape(parts, -1, packed.shape[1]), "ctx", 0, 0, tiled=True
+    ).transpose(1, 0, 2)
+
+
+def plane_shards(
+    activations,
+    seg_ids,
+    cotangent,
+    q_weight,
+    k_weight,
+    v_weight,
+    o_weight,
+    gate_weight,
+    up_weight,
+    down_weight,
+    attn_gain,
+    mlp_gain,
+):
+    parts = lax.axis_size("ctx")
+    plane = ("ctx", "tp")
+    heads = q_weight.shape[1] // F // parts
+    wide = heads * DV
+    narrow = heads * F
+    units = gate_weight.shape[1] // parts
+    rows = activations.shape[1] // lax.axis_size("tp")
+    mine = lax.axis_index("tp") * rows
+    f32, bf16 = jnp.float32, jnp.bfloat16
+
+    def dot(a, b, ca, cb):
+        return lax.dot_general(a, b, (((ca,), (cb,)), ((), ())), preferred_element_type=f32)
+
+    def gather(own):
+        return lax.all_gather(own, plane, axis=0, tiled=True)
+
+    def scatter(partial):
+        return lax.psum_scatter(
+            partial.astype(bf16), plane, scatter_dimension=0, tiled=True
+        ).astype(f32)
+
+    def fetch(packed):
+        mixed = lax.all_to_all(packed, "ctx", 0, 0, tiled=True)
+        return lax.all_gather(mixed, "dp", axis=0, tiled=True).reshape(-1, packed.shape[2])
+
+    gain_one = attn_gain.astype(f32)[:, None]
+    gain_two = mlp_gain.astype(f32)[:, None]
+    scaled = lambda w, g: (w.astype(f32) * g).astype(bf16)
+    w_attn = fetch(
+        jnp.concatenate(
+            [
+                by_columns(scaled(v_weight, gain_one), parts),
+                by_columns(scaled(q_weight, gain_one), parts),
+                by_columns(scaled(k_weight, gain_one), parts),
+                by_columns(o_weight, parts),
+            ],
+            axis=2,
+        )
+    )
+    w_mlp = fetch(
+        jnp.concatenate(
+            [
+                by_columns(scaled(gate_weight, gain_two), parts),
+                by_columns(scaled(up_weight, gain_two), parts),
+                by_columns(down_weight, parts),
+            ],
+            axis=2,
+        )
+    )
+    w_qkv, w_out = w_attn[:, : wide + 2 * narrow], w_attn[:, wide + 2 * narrow :]
+    w_gate, w_up, w_down = w_mlp[:, :units], w_mlp[:, units : 2 * units], w_mlp[:, 2 * units :]
+
+    x_own = lax.dynamic_slice_in_dim(activations[0], mine, rows, 0).astype(f32)
+    r_one = lax.rsqrt(jnp.mean(x_own * x_own, axis=1, keepdims=True) + EPSILON)
+    hat_one = x_own * r_one
+    rows_one = gather(hat_one.astype(bf16))
+    cot_own = lax.dynamic_slice_in_dim(cotangent[0], mine, rows, 0)
+    cot = gather(cot_own)
+    segments = lax.all_gather(seg_ids[0], "ctx", axis=0, tiled=True)
+    seg_rows, seg_cols = segments[:, None], segments[None, :]
+
+    qkv = dot(rows_one, w_qkv, 1, 0).astype(bf16)
+    mixed, denom, heads_out = attention_forward(qkv, seg_rows, seg_cols, heads)
+    middle = x_own + scatter(dot(heads_out, w_out, 1, 1))
+    r_two = lax.rsqrt(jnp.mean(middle * middle, axis=1, keepdims=True) + EPSILON)
+    hat_two = middle * r_two
+    rows_two = gather(hat_two.astype(bf16))
+    gate = dot(rows_two, w_gate, 1, 0)
+    up = dot(rows_two, w_up, 1, 0)
+    sig = jax.nn.sigmoid(gate)
+    hidden = (gate * sig * up).astype(bf16)
+    out_own = (middle + scatter(dot(hidden, w_down, 1, 1))).astype(bf16)
+    out = lax.all_gather(out_own, "tp", axis=0, tiled=True)
+
+    g_hidden = dot(cot, w_down, 1, 0)
+    g_gate = (g_hidden * up * sig * (1.0 + gate * (1.0 - sig))).astype(bf16)
+    g_up = (g_hidden * gate * sig).astype(bf16)
+    e_two = scatter(dot(g_gate, w_gate, 1, 1) + dot(g_up, w_up, 1, 1))
+    g_middle = cot_own.astype(f32) + r_two * (
+        e_two - hat_two * jnp.mean(e_two * hat_two, axis=1, keepdims=True)
+    )
+    back_mlp = to_owner(
+        jnp.concatenate(
+            [dot(rows_two, g_gate, 0, 0), dot(rows_two, g_up, 0, 0), dot(cot, hidden, 0, 0)], axis=1
+        ).astype(bf16)
+    )
+    branch = gather(g_middle.astype(bf16))
+    g_mixed = dot(branch, w_out, 1, 0).astype(bf16)
+    g_qkv = attention_backward(qkv, g_mixed, mixed, denom, seg_rows, seg_cols, heads)
+    e_one = scatter(dot(g_qkv, w_qkv, 1, 1))
+    g_x = g_middle + r_one * (e_one - hat_one * jnp.mean(e_one * hat_one, axis=1, keepdims=True))
+    g_input = lax.all_gather(g_x, "tp", axis=0, tiled=True)
+    back_attn = to_owner(
+        jnp.concatenate([dot(rows_one, g_qkv, 0, 0), dot(branch, heads_out, 0, 0)], axis=1).astype(
+            bf16
+        )
+    )
+
+    def owned(back, start, width):
+        return back[:, :, start : start + width].reshape(back.shape[0], -1).astype(f32)
+
+    s_v = owned(back_attn, 0, wide)
+    s_q = owned(back_attn, wide, narrow)
+    s_k = owned(back_attn, wide + narrow, narrow)
+    s_o = owned(back_attn, wide + 2 * narrow, wide)
+    s_gate = owned(back_mlp, 0, units)
+    s_up = owned(back_mlp, units, units)
+    s_down = owned(back_mlp, 2 * units, units)
+    along = lambda s, w: jnp.sum(s * w.astype(f32), axis=1)
+    gains = lax.psum(
+        jnp.stack(
+            [
+                along(s_q, q_weight) + along(s_k, k_weight) + along(s_v, v_weight),
+                along(s_gate, gate_weight) + along(s_up, up_weight),
+            ]
+        ),
+        "tp",
+    )
+    return (
+        out[None],
+        g_input[None],
+        s_q * gain_one,
+        s_k * gain_one,
+        s_v * gain_one,
+        s_o,
+        s_gate * gain_two,
+        s_up * gain_two,
+        s_down,
+        gains[0],
+        gains[1],
+    )
+
+
+def layer(*arrays):
+    heads = arrays[3].shape[1] // F
+    plan = shards if heads % lax.axis_size("ctx") else plane_shards
+    return plan(*arrays)
+
+
 def solution(mesh):
     placed = (
         P("dp", "ctx", None),
@@ -332,7 +705,7 @@
         P(("dp", "ctx")),
     )
     return jax.shard_map(
-        shards,
+        layer,
         mesh=mesh,
         in_specs=placed,
         out_specs=(

time: 2850 us -> 1130 us (0.40)
  waiting for transfers between devices: 2270 us -> 758 us
  blocking collectives: 271 us -> 64.6 us
  matrix products: 199 us -> 151 us
  Pallas kernels: 0 us -> 42.4 us
    reduce_scatter x7 -> x6, waiting for transfers between devices: 1830 us -> 351 us  [the longest x4 192 us: scatter(): lax.psum_scatter(partial.astype(bf16), plane, scatter_dimension=0, tiled=...]
    all_gather x6 -> x1, blocking collectives: 180 us -> 7.29 us  [plane_shards(): segments = lax.all_gather(seg_ids[0], 'ctx', axis=0, tiled=True)]
    unnamed x2 -> x0, blocking collectives: 90.2 us -> none
    all_to_all x0 -> x2, blocking collectives: none -> 54.9 us  [fetch(): mixed = lax.all_to_all(packed, 'ctx', 0, 0, tiled=True)]
    dot_general x34 -> x15, matrix products: 199 us -> 151 us  [dot(): lax.dot_general(a, b, (((ca,), (cb,)), ((), ())), preferred_element_type=...]
    all_gather x7 -> x8, waiting for transfers between devices: 423 us -> 380 us  [the longest x2 189 us: fetch(): lax.all_gather(mixed, 'dp', axis=0, tiled=True).reshape(-1, packed.shape[2])]
    pallas_call x0 -> x2, Pallas kernels: none -> 42.4 us  [the longest x1 27 us: attention_backward(): pl.pallas_call(kernel, grid=(blocks,), in_specs=[whole(qkv.shape), whole(...]
  transfers between devices with their start and end apart: 17 -> 16, of which waited for: 13 -> 15; matrix products, arithmetic and copies ran while one was open for 6% -> 12% of each run, Pallas kernels for 0% -> 0%
where the time goes in v1:
time: 1130 us; the launch traced here: 1120 us
  waiting for transfers between devices  758 us (67%)
  matrix products  151 us (13%)
  blocking collectives  64.6 us (6%)
  local copies, waits for them, and re-layouts  52.4 us (5%)
  Pallas kernels  42.4 us (4%)
  other arithmetic  27.5 us (2%)
  between operations  14.6 us (1%)
    reduce_scatter x4, waiting for transfers between devices, scatter(): lax.psum_scatter(partial.astype(bf16), plane, scatter_dimension=0, tiled=...  192 us
    all_gather x2, waiting for transfers between devices, fetch(): lax.all_gather(mixed, 'dp', axis=0, tiled=True).reshape(-1, packed.shape[2])  189 us
    all_gather x4, waiting for transfers between devices, gather(): return lax.all_gather(own, plane, axis=0, tiled=True)  183 us
    reduce_scatter x2, waiting for transfers between devices, to_owner(): summed = lax.psum_scatter(packed, 'dp', scatter_dimension=0, tiled=True)  159 us
    dot_general x15, matrix products, dot(): lax.dot_general(a, b, (((ca,), (cb,)), ((), ())), preferred_element_type=...  151 us
    all_to_all x2, blocking collectives, fetch(): mixed = lax.all_to_all(packed, 'ctx', 0, 0, tiled=True)  54.9 us
    pallas_call x1, Pallas kernels, attention_backward(): pl.pallas_call(kernel, grid=(blocks,), in_specs=[whole(qkv.shape), whole(...  27 us
    all_to_all x2, waiting for transfers between devices, to_owner(): lax.all_to_all(summed.reshape(parts, -1, packed.shape[1]), 'ctx', 0, 0, t...  26.3 us
  transfers between devices with their start and end apart: 16, of which 15 were waited for; matrix products, arithmetic and copies ran while one was open for 12% of the time, Pallas kernels for 0%

profile of v1, /device:TPU:0, one launch (start us, length us, event | category | flops | bytes accessed | tf_op | source)
XLA Modules:
  0.0 1120.1 jit_solution(4306560687444805559)
XLA Ops:
  12.3 14.5 %all_to_all.20 = bf16[4,128,576]{1,2,0:T(8,128)(2,1)} all-to-all(bf16[4,128,576]{1,2,0:T(8,128)(2,1)S(1)} %pad_maximum_fusion.3), channel_id=1, replica_groups=mesh['dp'=4,'ctx'=4,'tp'=2] {'ctx'}, dimensions={0} | all-to-all | bytes 1179648 | tf_op jit(solution)/shard_map/all_to_all | solution.py:575
  29.0 7.3 all-gather.col_ref
  37.7 39.3 %all-gather.13.cloned.1.call-done = bf16[16,128,576]{1,2,0:T(8,128)(2,1)} async-done(((bf16[4,128,576]{1,2,0:T(8,128)(2,1)}), bf16[16,128,576]{1,2,0:T(8,128)(2,1)}) %all-gather.13.cloned.1.call-update) | async-done | bytes 2359312 | tf_op jit(solution)/shard_map/all_gather | solution.py:576
  76.9 3.4 copy_bitcast_fusion
  80.4 52.3 %all-gather.11.cloned.1.call-done = bf16[2048,2048]{1,0:T(8,128)(2,1)} async-done(((bf16[256,2048]{1,0:T(8,128)(2,1)}), bf16[2048,2048]{1,0:T(8,128)(2,1)}) %all-gather.11.cloned.1.call-update) | async-done | bytes 8388624 | tf_op jit(solution)/shard_map/all_gather | solution.py:567
  132.6 9.5 convolution_convert_fusion.5.x_ref
  142.2 15.4 %attn_forward.1 = (f32[2048,256]{1,0:T(8,128)}, f32[2048,2]{1,0:T(8,128)}, bf16[2048,256]{1,0:T(8,128)(2,1)}) custom-call(bf16[2048,320]{1,0:T(8,128)(2,1)} %convolution_convert_fusion.5.x_ref, s32[2048,1]{1,0:T(8,128)} %copy.60.row_ref, s32[1,2048]{1,0:T(1,128)} %copy-done.17), custom_call_target="tpu_custom_call" | custom-call | flops 3355443200 | bytes 6291456 | tf_op jit(solution)/shard_map/attn_forward/pallas_call | solution.py:383
  157.6 7.1 convolution_convert_fusion.2
  167.9 2.5 copy.63
  171.7 40.4 %all_to_all.21 = bf16[4,128,2112]{1,2,0:T(8,128)(2,1)} all-to-all(bf16[4,128,2112]{1,2,0:T(8,128)(2,1)S(1)} %pad_maximum_fusion.2), channel_id=1, replica_groups=mesh['dp'=4,'ctx'=4,'tp'=2] {'ctx'}, dimensions={0} | all-to-all | bytes 4325376 | tf_op jit(solution)/shard_map/all_to_all | solution.py:575
  212.1 33.5 %reduce-scatter.7.cloned.1.call-done = bf16[256,2048]{1,0:T(8,128)(2,1)} async-done(((bf16[2048,2048]{1,0:T(8,128)(2,1)}), bf16[256,2048]{1,0:T(8,128)(2,1)}) %reduce-scatter.7.cloned.1.call-update) | async-done | bytes 1048592 | tf_op jit(solution)/shard_map/reduce_scatter | solution.py:570
  248.8 2.3 constant_dynamic-slice_fusion
  251.2 149.9 %all-gather.17.cloned.1.call-done = bf16[16,128,2112]{1,2,0:T(8,128)(2,1)} async-done(((bf16[4,128,2112]{1,2,0:T(8,128)(2,1)}), bf16[16,128,2112]{1,2,0:T(8,128)(2,1)}) %all-gather.17.cloned.1.call-update) | async-done | bytes 8650768 | tf_op jit(solution)/shard_map/all_gather | solution.py:576
  401.1 12.0 %copy.64 = bf16[16,128,2112]{2,1,0:T(8,128)(2,1)} copy(bf16[16,128,2112]{1,2,0:T(8,128)(2,1)} %all-gather.17.cloned.1.call-done) | data formatting | bytes 17301504 | tf_op jit(solution)/shard_map/all_gather | solution.py:576
  413.1 43.1 %all-gather.15.cloned.1.call-done = bf16[2048,2048]{1,0:T(8,128)(2,1)} async-done(((bf16[256,2048]{1,0:T(8,128)(2,1)}), bf16[2048,2048]{1,0:T(8,128)(2,1)}) %all-gather.15.cloned.1.call-update) | async-done | bytes 8388624 | tf_op jit(solution)/shard_map/all_gather | solution.py:567
  456.2 12.9 %fusion.13 = f32[2048,704]{0,1:T(8,128)} fusion(bf16[2048,2048]{1,0:T(8,128)(2,1)} %all-gather.15.cloned.1.call-done, bf16[2048,2112]{1,0:T(8,128)(2,1)} %bitcast.124), kind=kOutput, calls=%fused_computation.26 | convolution fusion | flops 5905580032 | bytes 17301504 | tf_op jit(solution)/shard_map/dot_general | solution.py:564
  469.1 10.0 fusion.17
  479.1 33.4 %all-gather.25.cloned.1.call-done = bf16[1,2048,2048]{2,1,0:T(8,128)(2,1)} async-done(((bf16[1,256,2048]{2,1,0:T(8,128)(2,1)}), bf16[1,2048,2048]{2,1,0:T(8,128)(2,1)}) %all-gather.25.cloned.1.call-update) | async-done | bytes 8388624 | tf_op jit(solution)/shard_map/all_gather | solution.py:567
  512.5 16.2 %multiply_convert_fusion = (bf16[2048,704]{0,1:T(8,128)(2,1)S(1)}, bf16[2048,704]{0,1:T(8,128)(2,1)}, bf16[2048,704]{0,1:T(8,128)(2,1)}) fusion(f32[2048,704]{0,1:T(8,128)} %fusion.17, f32[2048,704]{0,1:T(8,128)} %fusion.13, bf16[2048,2112]{1,0:T(8,128)(2,1)} %bitcast.126, bf16[1,2048,2048]{2,1,0:T(8,128)(2,1)} %all-gather.25.cloned.1.call-done), kind=kOutput, calls=%fused_computation.9 | convolution fusion | flops 5928648704 | bytes 31719424 | tf_op jit(solution)/shard_map/dot_general | solution.py:564
  528.7 13.7 %fusion.15 = f32[2048,2048]{1,0:T(8,128)} fusion(bf16[2048,704]{0,1:T(8,128)(2,1)} %get-tuple-element.40, bf16[2048,2112]{1,0:T(8,128)(2,1)} %bitcast.127), kind=kOutput, calls=%fused_computation.28 | convolution fusion | flops 5905580032 | bytes 22806528 | tf_op jit(solution)/shard_map/dot_general | solution.py:564
  542.4 15.8 %add_convert_fusion = bf16[2048,2048]{1,0:T(8,128)(2,1)} fusion(f32[2048,2048]{1,0:T(8,128)} %fusion.15, bf16[2048,704]{0,1:T(8,128)(2,1)S(1)} %get-tuple-element.39, bf16[2048,2112]{1,0:T(8,128)(2,1)} %bitcast.128), kind=kOutput, calls=%fused_computation | convolution fusion | flops 5913968640 | bytes 31195136 | tf_op jit(solution)/shard_map/dot_general | solution.py:564
  558.3 71.4 %reduce-scatter.11.cloned.1.call-done = bf16[256,2048]{1,0:T(8,128)(2,1)} async-done(((bf16[2048,2048]{1,0:T(8,128)(2,1)}), bf16[256,2048]{1,0:T(8,128)(2,1)}) %reduce-scatter.11.cloned.1.call-update) | async-done | bytes 1048592 | tf_op jit(solution)/shard_map/reduce_scatter | solution.py:570
  633.8 54.5 %all-gather.21.cloned.1.call-done = bf16[2048,2048]{1,0:T(8,128)(2,1)} async-done(((bf16[256,2048]{1,0:T(8,128)(2,1)}), bf16[2048,2048]{1,0:T(8,128)(2,1)}) %all-gather.21.cloned.1.call-update) | async-done | bytes 8388624 | tf_op jit(solution)/shard_map/all_gather | solution.py:567
  688.3 7.0 convolution_convert_fusion.8.gm_ref
  695.3 27.0 %attn_backward.1 = bf16[2048,320]{1,0:T(8,128)(2,1)} custom-call(bf16[2048,320]{1,0:T(8,128)(2,1)} %convolution_convert_fusion.5.x_ref, bf16[2048,256]{1,0:T(8,128)(2,1)} %convolution_convert_fusion.8.gm_ref, f32[2048,256]{1,0:T(8,128)} %get-tuple-element.15.m_ref, f32[2048,2]{1,0:T(8,128)} %get-tuple-element.16.d_ref, s32[2048,1]{1,0:T(8,128)} %copy.60.row_ref, ...), custom_call_target="tpu_custom_call" | custom-call | flops 6710886400 | bytes 6291456 | tf_op jit(solution)/shard_map/attn_backward/pallas_call | solution.py:499
  722.3 8.2 convolution_convert_fusion
  730.6 11.6 %convolution_convert_fusion.1 = bf16[2048,2048]{1,0:T(8,128)(2,1)} fusion(bf16[2048,704]{0,1:T(8,128)(2,1)} %get-tuple-element.41, bf16[2048,2112]{1,0:T(8,128)(2,1)} %bitcast.129), kind=kOutput, calls=%fused_computation.7 | convolution fusion | flops 5909774336 | bytes 14417920 | tf_op jit(solution)/shard_map/dot_general | solution.py:564
  742.3 11.4 %fusion.4 = bf16[2048,704]{0,1:T(8,128)(2,1)S(1)} fusion(bf16[2048,704]{0,1:T(8,128)(2,1)} %get-tuple-element.41, bf16[1,2048,2048]{2,1,0:T(8,128)(2,1)} %all-gather.25.cloned.1.call-done), kind=kOutput, calls=%fused_computation.15 | convolution fusion | flops 5907021824 | bytes 14155776 | tf_op jit(solution)/shard_map/dot_general | solution.py:564
  753.8 9.0 convolution_convert_fusion.3
  762.9 6.3 convolution_convert_fusion.4
  769.2 4.1 pad_maximum_fusion
  773.6 6.2 convolution_convert_fusion.7
  779.8 6.5 convolution_convert_fusion.6
  787.9 14.0 %reduce-scatter.13.cloned.1.call-done = bf16[256,2048]{1,0:T(8,128)(2,1)} async-done(((bf16[2048,2048]{1,0:T(8,128)(2,1)}), bf16[256,2048]{1,0:T(8,128)(2,1)}) %reduce-scatter.13.cloned.1.call-update) | async-done | bytes 1048592 | tf_op jit(solution)/shard_map/reduce_scatter | solution.py:570
  803.7 73.3 %reduce-scatter.9.cloned.1.call-done = bf16[256,2048]{1,0:T(8,128)(2,1)} async-done(((bf16[2048,2048]{1,0:T(8,128)(2,1)}), bf16[256,2048]{1,0:T(8,128)(2,1)}) %reduce-scatter.9.cloned.1.call-update) | async-done | bytes 1048592 | tf_op jit(solution)/shard_map/reduce_scatter | solution.py:570
  877.0 5.3 fusion.23
  882.3 145.7 %reduce-scatter.17.cloned.1.call-done = bf16[512,2112]{0,1:T(8,128)(2,1)} async-done(((bf16[2048,2112]{0,1:T(8,128)(2,1)}), bf16[512,2112]{0,1:T(8,128)(2,1)}) %reduce-scatter.17.cloned.1.call-update) | async-done | bytes 2162704 | tf_op jit(solution)/shard_map/reduce_scatter | solution.py:532
  1028.0 3.4 copy_bitcast_fusion.1
  1031.4 4.5 all-to-all-start.3
  1036.5 25.2 %all-to-all-done.3 = bf16[4,128,2112]{1,2,0:T(8,128)(2,1)} async-done(((bf16[4,128,2112]{1,2,0:T(8,128)(2,1)}), bf16[4,128,2112]{1,2,0:T(8,128)(2,1)}, u32[]{:S(2)}, u32[]{:S(2)}) %all-to-all-start.3) | async-done | bytes 2162720 | tf_op jit(solution)/shard_map/all_to_all | solution.py:534
  1061.6 2.8 fusion.43
  1066.2 13.4 %reduce-scatter.15.cloned.1.call-done = bf16[512,576]{0,1:T(8,128)(2,1)} async-done(((bf16[2048,576]{0,1:T(8,128)(2,1)}), bf16[512,576]{0,1:T(8,128)(2,1)}) %reduce-scatter.15.cloned.1.call-update) | async-done | bytes 589840 | tf_op jit(solution)/shard_map/reduce_scatter | solution.py:532
  1081.6 3.6 all-to-all-start.2
  1085.2 3.0 fusion.30
  1088.2 3.0 copy.73
  1097.7 2.5 psum.7
  1100.7 7.4 all-gather.23.cloned.1.call-done
  1108.1 3.3 copy.85
  (142 shorter events, 37.3 us)
Async XLA Ops:
  7.2 19.6 %copy-start = (bf16[1,512,2048]{2,1,0:T(8,128)(2,1)S(1)}, bf16[1,512,2048]{2,1,0:T(8,128)(2,1)}, u32[]{:S(2)}) copy-start(bf16[1,512,2048]{2,1,0:T(8,128)(2,1)} %param.12) | copy-start | bytes 6291460
  7.2 69.8 %all-gather.13.cloned.1.call-start = ((), (), s32[]{:S(2)}) async-start(), calls=%async_computation.11 | async-start | bytes 2949120 | tf_op jit(solution)/shard_map/all_gather | solution.py:576
  8.0 19.1 %copy-start.20 = (f32[128]{0:T(128)}, f32[128]{0:T(128)S(1)}, u32[]{:S(2)}) copy-start(f32[128]{0:T(128)S(1)} %convert_element_type.149) | copy-start | bytes 1540
  8.9 18.2 %copy-start.13 = (bf16[128,128]{0,1:T(8,128)(2,1)}, bf16[128,128]{0,1:T(8,128)(2,1)S(1)}, u32[]{:S(2)}) copy-start(bf16[128,128]{0,1:T(8,128)(2,1)S(1)} %copy.55) | copy-start | bytes 98308
  9.8 17.3 %copy-start.15 = (bf16[128,128]{0,1:T(8,128)(2,1)}, bf16[128,128]{0,1:T(8,128)(2,1)S(1)}, u32[]{:S(2)}) copy-start(bf16[128,128]{0,1:T(8,128)(2,1)S(1)} %copy.56) | copy-start | bytes 98308
  26.7 2.3 copy-start.24
  26.8 105.9 %all-gather.11.cloned.1.call-start = ((), (), s32[]{:S(2)}) async-start(), calls=%async_computation.10 | async-start | bytes 9437184 | tf_op jit(solution)/shard_map/all_gather | solution.py:567
  29.0 216.7 %reduce-scatter.7.cloned.1.call-start = ((), (), s32[]{:S(2)}) async-start(), calls=%async_computation.12 | async-start | bytes 9437184 | tf_op jit(solution)/shard_map/reduce_scatter | solution.py:570
  36.3 44.1 %copy-start.17 = (s32[1,2048]{1,0:T(1,128)}, s32[1,2048]{1,0:T(1,128)S(1)}, u32[]{:S(2)}) copy-start(s32[1,2048]{1,0:T(1,128)S(1)} %all-gather.col_ref) | copy-start | bytes 24580
  164.7 0.7 copy-start.26
  164.7 1.1 copy-start.12
  164.7 236.4 %all-gather.17.cloned.1.call-start = ((), (), s32[]{:S(2)}) async-start(), calls=%async_computation.14 | async-start | bytes 10813440 | tf_op jit(solution)/shard_map/all_gather | solution.py:576
  165.8 4.9 copy-start.22
  166.1 4.5 copy-start.3
  167.9 3.8 copy-start.5
  170.4 1.1 copy-start.10
  212.1 244.1 %all-gather.15.cloned.1.call-start = ((), (), s32[]{:S(2)}) async-start(), calls=%async_computation.13 | async-start | bytes 9437184 | tf_op jit(solution)/shard_map/all_gather | solution.py:567
  245.6 1.7 copy-start.1
  248.7 263.8 %all-gather.25.cloned.1.call-start = ((), (), s32[]{:S(2)}) async-start(), calls=%async_computation.23 | async-start | bytes 9437184 | tf_op jit(solution)/shard_map/all_gather | solution.py:567
  251.1 378.6 %reduce-scatter.11.cloned.1.call-start = ((), (), s32[]{:S(2)}) async-start(), calls=%async_computation.17 | async-start | bytes 9437184 | tf_op jit(solution)/shard_map/reduce_scatter | solution.py:570
  456.2 12.9 %copy-start.25 = (bf16[2048,2048]{1,0:T(8,128)(2,1)S(1)}, bf16[2048,2048]{1,0:T(8,128)(2,1)}, u32[]{:S(2)}) copy-start(bf16[2048,2048]{1,0:T(8,128)(2,1)} %all-gather.15.cloned.1.call-done) | copy-start | bytes 25165828
  528.7 13.7 %copy-start.28 = (bf16[2048,704]{0,1:T(8,128)(2,1)}, bf16[2048,704]{0,1:T(8,128)(2,1)S(1)}, u32[]{:S(2)}) copy-start(bf16[2048,704]{0,1:T(8,128)(2,1)S(1)} %get-tuple-element.39) | copy-start | bytes 8650756
  558.3 130.0 %all-gather.21.cloned.1.call-start = ((), (), s32[]{:S(2)}) async-start(), calls=%async_computation.18 | async-start | bytes 9437184 | tf_op jit(solution)/shard_map/all_gather | solution.py:567
  629.7 2.0 copy-start.2
  629.7 2.2 copy-start.8
  633.8 168.2 %reduce-scatter.13.cloned.1.call-start = ((), (), s32[]{:S(2)}) async-start(), calls=%async_computation.19 | async-start | bytes 9437184 | tf_op jit(solution)/shard_map/reduce_scatter | solution.py:570
  695.3 27.0 %copy-start.7 = (bf16[2048,576]{0,1:T(8,128)(2,1)S(1)}, bf16[2048,576]{0,1:T(8,128)(2,1)}, u32[]{:S(2)}) copy-start(bf16[2048,576]{0,1:T(8,128)(2,1)} %copy_bitcast_fusion) | copy-start | bytes 7077892
  730.5 146.4 %reduce-scatter.9.cloned.1.call-start = ((), (), s32[]{:S(2)}) async-start(), calls=%async_computation.15 | async-start | bytes 9437184 | tf_op jit(solution)/shard_map/reduce_scatter | solution.py:570
  742.3 285.7 %reduce-scatter.17.cloned.1.call-start = ((), (), s32[]{:S(2)}) async-start(), calls=%async_computation.22 | async-start | bytes 10813440 | tf_op jit(solution)/shard_map/reduce_scatter | solution.py:532
  742.3 11.4 %copy-start.29 = (bf16[2048,704]{0,1:T(8,128)(2,1)S(1)}, bf16[2048,704]{0,1:T(8,128)(2,1)}, u32[]{:S(2)}) copy-start(bf16[2048,704]{0,1:T(8,128)(2,1)} %copy-done.28) | copy-start | bytes 8650756
  742.3 20.5 %slice-start = ((s8[8388608]{0:T(1024)(128)(4,1)}), s8[4194304]{0:T(1024)(128)(4,1)S(1)}, s32[]{:S(2)}) async-start(s8[8388608]{0:T(1024)(128)(4,1)} %bitcast.142), calls=%async_computation.24 | async-start | bytes 8388608
  753.8 9.1 slice-start.1
  753.8 9.1 copy-start.30
  773.3 306.3 %reduce-scatter.15.cloned.1.call-start = ((), (), s32[]{:S(2)}) async-start(), calls=%async_computation.21 | async-start | bytes 2949120 | tf_op jit(solution)/shard_map/reduce_scatter | solution.py:532
  773.6 6.2 copy-start.27
  786.2 15.7 %copy-start.19 = (f32[256]{0:T(256)S(1)}, f32[256]{0:T(256)}, u32[]{:S(2)}) copy-start(f32[256]{0:T(256)} %copy-done.18) | copy-start | bytes 3076
  787.8 312.8 %all-gather.19.cloned.1.call-start = ((), (), s32[]{:S(2)}) async-start(), calls=%async_computation.16 | async-start | bytes 3145728 | tf_op jit(solution)/shard_map/all_gather | solution.py:625
  1031.4 30.2 %all-to-all-start.3 = ((bf16[4,128,2112]{1,2,0:T(8,128)(2,1)}), bf16[4,128,2112]{1,2,0:T(8,128)(2,1)}, u32[]{:S(2)}, u32[]{:S(2)}) async-start(bf16[4,128,2112]{1,2,0:T(8,128)(2,1)} %copy_bitcast_fusion.1), calls=%async_computation.9 | async-start | bytes 4325376 | tf_op jit(solution)/shard_map/all_to_all | solution.py:534
  1035.9 72.2 %all-gather.23.cloned.1.call-start = ((), (), s32[]{:S(2)}) async-start(), calls=%async_computation.20 | async-start | bytes 6291456 | tf_op jit(solution)/shard_map/all_gather | solution.py:644
  1064.6 20.6 %copy-start.4 = (bf16[128,2816]{0,1:T(8,128)(2,1)S(1)}, bf16[128,2816]{0,1:T(8,128)(2,1)}, u32[]{:S(2)}) copy-start(bf16[128,2816]{0,1:T(8,128)(2,1)} %copy-done.3) | copy-start | bytes 2162692
  1064.6 20.6 %copy-start.6 = (bf16[128,2816]{0,1:T(8,128)(2,1)S(1)}, bf16[128,2816]{0,1:T(8,128)(2,1)}, u32[]{:S(2)}) copy-start(bf16[128,2816]{0,1:T(8,128)(2,1)} %copy-done.5) | copy-start | bytes 2162692
  1064.6 20.6 %copy-start.23 = (f32[128]{0:T(128)S(1)}, f32[128]{0:T(128)}, u32[]{:S(2)}) copy-start(f32[128]{0:T(128)} %copy-done.22) | copy-start | bytes 1540
  1081.6 12.3 %all-to-all-start.2 = ((bf16[4,128,576]{1,2,0:T(8,128)(2,1)}), bf16[4,128,576]{1,2,0:T(8,128)(2,1)S(1)}, u32[]{:S(2)}, u32[]{:S(2)}) async-start(bf16[4,128,576]{1,2,0:T(8,128)(2,1)} %copy_bitcast_fusion.2), calls=%async_computation.7 | async-start | bytes 1179648 | tf_op jit(solution)/shard_map/all_to_all | solution.py:534
  1088.2 5.7 copy-start.14
  1088.2 5.7 copy-start.16
  1088.2 5.7 copy-start.21
  1093.9 2.9 copy-start.11
  1108.1 3.3 copy-start.9
  (1 other events, 0.6 us)
Sparse Core Ops, SparseCore 0:
  26.9 50.0 all-gather.12
  79.4 53.1 all-gather.10
  164.8 80.7 reduce-scatter.6
  247.1 153.8 all-gather.16
  403.5 52.6 all-gather.14
  458.1 54.3 all-gather.24
  558.4 71.2 reduce-scatter.10
  633.9 54.3 all-gather.20
  730.7 71.2 reduce-scatter.12
  805.6 71.2 reduce-scatter.8
  879.3 148.5 reduce-scatter.16
  1030.7 48.8 reduce-scatter.14
  1081.1 10.0 all-gather.18
  1093.2 14.8 all-gather.22

commit v2 on v1

--- a/solution.py
+++ b/solution.py
@@ -523,6 +523,597 @@
     )(qkv, g_mixed, mixed, denom, seg_rows, seg_cols)
 
 
+MESH = pl.DeviceIdType.MESH
+BF16, F32 = jnp.bfloat16, jnp.float32
+
+
+def dot(a, b, ca, cb):
+    return lax.dot_general(a, b, (((ca,), (cb,)), ((), ())), preferred_element_type=F32)
+
+
+def place_of():
+    return lax.axis_index("dp"), lax.axis_index("ctx"), lax.axis_index("tp")
+
+
+def beside(c, across):
+    x, y = lax.rem(c, 2), lax.div(c, 2)
+    return lax.rem(x + across % 2, 2) + 2 * lax.rem(y + across // 2, 2)
+
+
+def greet(devices):
+    barrier = pltpu.get_barrier_semaphore()
+    for device in devices:
+        pl.semaphore_signal(barrier, inc=1, device_id=device, device_id_type=MESH)
+    pl.semaphore_wait(barrier, len(devices))
+
+
+def remote(source, target, send, receive, k, device):
+    return pltpu.make_async_remote_copy(
+        src_ref=source,
+        dst_ref=target,
+        send_sem=send.at[k],
+        recv_sem=receive.at[k],
+        device_id=device,
+        device_id_type=MESH,
+    )
+
+
+def gather_rows(buf, send, receive, piece=None, early=None):
+    d, c, t = place_of()
+    own = buf.shape[0] // 8
+    half = own // 2
+    to_x, to_y, to_t = (d, beside(c, 1), t), (d, beside(c, 2), t), (d, c, 1 - t)
+    started = []
+
+    def part(across, core, h):
+        block = c if across == 0 else beside(c, across)
+        start = (2 * block + core) * own + h * half
+        return buf.at[pl.ds(pl.multiple_of(start, half), half)]
+
+    def put(k, across, h, device):
+        ref = part(across, t, h)
+        copy = remote(ref, ref, send, receive, k, device)
+        copy.start()
+        started.append(copy)
+
+    def got(k, across, core, h):
+        ref = part(across, core, h)
+        remote(ref, ref, send, receive, k, to_t).wait_recv()
+
+    def work(across, core):
+        if piece is not None:
+            block = c if across == 0 else beside(c, across)
+            piece(pl.multiple_of((2 * block + core) * own, own))
+
+    put(0, 0, 0, to_x)
+    put(1, 0, 1, to_y)
+    put(2, 0, 1, to_x)
+    put(3, 0, 0, to_y)
+    put(6, 0, 0, to_t)
+    put(7, 0, 1, to_t)
+    if early is not None:
+        early()
+    work(0, t)
+    got(6, 0, 1 - t, 0)
+    got(7, 0, 1 - t, 1)
+    work(0, 1 - t)
+    got(0, 1, t, 0)
+    put(4, 1, 0, to_y)
+    put(8, 1, 0, to_t)
+    got(1, 2, t, 1)
+    put(5, 2, 1, to_x)
+    put(9, 2, 1, to_t)
+    got(2, 1, t, 1)
+    put(10, 1, 1, to_t)
+    got(3, 2, t, 0)
+    put(11, 2, 0, to_t)
+    work(1, t)
+    work(2, t)
+    got(8, 1, 1 - t, 0)
+    got(10, 1, 1 - t, 1)
+    work(1, 1 - t)
+    got(9, 2, 1 - t, 1)
+    got(11, 2, 1 - t, 0)
+    work(2, 1 - t)
+    got(4, 3, t, 0)
+    put(12, 3, 0, to_t)
+    got(5, 3, t, 1)
+    put(13, 3, 1, to_t)
+    work(3, t)
+    got(12, 3, 1 - t, 0)
+    got(13, 3, 1 - t, 1)
+    work(3, 1 - t)
+    for copy in started:
+        copy.wait_send()
+
+
+GATHER_COPIES = 14
+
+
+def scatter_rows(piece, bufs, send, receive):
+    to_core, from_core, kept, over, came = bufs
+    d, c, t = place_of()
+    own = kept.shape[1]
+    half = own // 2
+    to_x, to_y, to_t = (d, beside(c, 1), t), (d, beside(c, 2), t), (d, c, 1 - t)
+
+    def link(k):
+        return remote(over.at[k], came.at[k], send, receive, 4 + k, to_x if k % 2 == 0 else to_y)
+
+    def core(i):
+        return remote(to_core.at[i], from_core.at[i], send, receive, i, to_t)
+
+    def ready(k, i, h, extra=None):
+        rows = pl.ds(h * half, half)
+        total = kept[i, rows, :]
+        if extra is not None:
+            total = total + came[extra].astype(F32)
+        over[k] = total.astype(BF16)
+        link(k).start()
+
+    def step(p, carry):
+        i = lax.div(p, 2)
+        across = 3 - i
+        x, y = lax.rem(c, 2), lax.div(c, 2)
+        block = lax.rem(x + lax.rem(across, 2), 2) + 2 * lax.rem(y + lax.div(across, 2), 2)
+        mine = lax.rem(p, 2)
+        who = mine * t + (1 - mine) * (1 - t)
+        piece(pl.multiple_of((2 * block + who) * own, own), kept.at[i])
+
+        @pl.when(mine == 0)
+        def _():
+            to_core[i] = kept[i].astype(BF16)
+            core(i).start()
+
+        @pl.when(mine == 1)
+        def _():
+            core(i).wait_recv()
+            kept[i] = kept[i] + from_core[i].astype(F32)
+
+        @pl.when(p == 1)
+        def _():
+            ready(0, 0, 0)
+            ready(1, 0, 1)
+
+        @pl.when(p == 3)
+        def _():
+            ready(3, 1, 1)
+
+        @pl.when(p == 5)
+        def _():
+            ready(2, 2, 0)
+            link(1).wait_recv()
+            ready(4, 2, 1, 1)
+            link(0).wait_recv()
+            ready(5, 1, 0, 0)
+
+        return carry
+
+    lax.fori_loop(0, 8, step, 0)
+    for h, a, b in ((0, 2, 5), (1, 3, 4)):
+        link(a).wait_recv()
+        link(b).wait_recv()
+        rows = pl.ds(h * half, half)
+        kept[3, rows, :] = kept[3, rows, :] + (came[a].astype(F32) + came[b].astype(F32))
+    for i in range(4):
+        core(i).wait_send()
+    for k in range(6):
+        link(k).wait_send()
+
+
+SCATTER_COPIES = 10
+
+
+def scatter_scratch(own, width):
+    return [
+        pltpu.VMEM((4, own, width), BF16),
+        pltpu.VMEM((4, own, width), BF16),
+        pltpu.VMEM((4, own, width), F32),
+        pltpu.VMEM((6, own // 2, width), BF16),
+        pltpu.VMEM((6, own // 2, width), BF16),
+    ]
+
+
+def by_tiles(a, weights, out_ref, tile=512):
+    width = out_ref.shape[1]
+
+    @pl.loop(0, width // tile)
+    def _(n):
+        columns = pl.ds(pl.multiple_of(n * tile, tile), tile)
+        total = None
+        for x, w in zip(a, weights):
+            term = dot(x, w[columns, :], 1, 1)
+            total = term if total is None else total + term
+        out_ref[:, columns] = total
+
+
+def norm_parts(rows):
+    scale = lax.rsqrt(jnp.mean(rows * rows, axis=1, keepdims=True) + EPSILON)
+    return scale, rows * scale
+
+
+def norm_back(e, hat, scale):
+    return scale * (e - hat * jnp.mean(e * hat, axis=1, keepdims=True))
+
+
+def call(kernel, name, collective, arrays, out_shape, scratch, spaces=None, out_spaces=None, flops=0):
+    vmem = pl.BlockSpec(memory_space=pltpu.VMEM)
+    moved = sum(a.size * a.dtype.itemsize for a in arrays)
+    return pl.pallas_call(
+        kernel,
+        in_specs=spaces or [vmem] * len(arrays),
+        out_specs=out_spaces or [vmem] * len(out_shape),
+        out_shape=out_shape,
+        scratch_shapes=scratch,
+        compiler_params=pltpu.CompilerParams(
+            collective_id=collective, has_side_effects=True, vmem_limit_bytes=VMEM_MOST
+        ),
+        cost_estimate=pl.CostEstimate(flops=flops, bytes_accessed=moved, transcendentals=0),
+        name=name,
+    )(*arrays)
+
+
+def sems(count):
+    return [pltpu.SemaphoreType.DMA((count,)), pltpu.SemaphoreType.DMA((count,))]
+
+
+def depth(d, k):
+    return lax.rem(d + k, lax.axis_size("dp"))
+
+
+def front(x, seg, w_attn, w_mlp, tokens):
+    width = x.shape[1]
+    own = tokens // 8
+    deep = lax.axis_size("dp")
+
+    def kernel(
+        x_ref, seg_ref, wa_ref, wm_ref, rows_ref, segs_ref, wa_out, wm_out,
+        send, receive, small_send, small_receive, deep_send, deep_receive, here,
+    ):
+        d, c, t = place_of()
+        greet(
+            [(d, beside(c, k), t) for k in (1, 2, 3)]
+            + [(d, c, 1 - t)]
+            + [(depth(d, k), c, t) for k in range(1, deep)]
+        )
+        jobs = (
+            (lambda block: wa_ref.at[block], lambda block: wa_out.at[d, block]),
+            (lambda block: seg_ref.at[0], lambda block: segs_ref.at[block]),
+            (lambda block: wm_ref.at[block], lambda block: wm_out.at[block]),
+        )
+
+        def local(n):
+            return pltpu.make_async_copy(jobs[n][0](c), jobs[n][1](c), here.at[n])
+
+        def out(n, k):
+            return remote(
+                jobs[n][0](beside(c, k)), jobs[n][1](c), small_send, small_receive,
+                3 * n + k - 1, (d, beside(c, k), t),
+            )
+
+        def arrival(n, k):
+            block = beside(c, k)
+            return remote(
+                jobs[n][0](block), jobs[n][1](block), small_send, small_receive,
+                3 * n + k - 1, (d, block, t),
+            )
+
+        def along(k):
+            return remote(
+                wa_out.at[d], wa_out.at[d], deep_send, deep_receive, k - 1, (depth(d, k), c, t)
+            )
+
+        def from_depth(k):
+            there = wa_out.at[depth(d, deep - k)]
+            return remote(there, there, deep_send, deep_receive, k - 1, (depth(d, k), c, t))
+
+        local(0).start()
+        for k in (3, 1, 2):
+            out(0, k).start()
+        mine = pl.multiple_of((2 * c + t) * own, own)
+        _, hat = norm_parts(x_ref[pl.ds(pl.multiple_of(t * own, own), own), :].astype(F32))
+        rows_ref[pl.ds(mine, own), :] = hat.astype(BF16)
+
+        def early():
+            for n in (1, 2):
+                local(n).start()
+                for k in (3, 1, 2):
+                    out(n, k).start()
+            local(0).wait()
+            for k in (1, 2, 3):
+                arrival(0, k).wait_recv()
+            for k in range(1, deep):
+                along(k).start()
+
+        gather_rows(rows_ref, send, receive, early=early)
+        for n in (1, 2):
+            local(n).wait()
+            for k in (1, 2, 3):
+                arrival(n, k).wait_recv()
+        for k in range(1, deep):
+            from_depth(k).wait_recv()
+        for n in range(3):
+            for k in (1, 2, 3):
+                out(n, k).wait_send()
+        for k in range(1, deep):
+            along(k).wait_send()
+
+    vmem, hbm = pl.BlockSpec(memory_space=pltpu.VMEM), pl.BlockSpec(memory_space=pl.ANY)
+    return call(
+        kernel,
+        "front",
+        1,
+        (x, seg[None], w_attn, w_mlp),
+        [
+            jax.ShapeDtypeStruct((tokens, width), BF16),
+            jax.ShapeDtypeStruct((4,) + seg.shape, seg.dtype),
+            jax.ShapeDtypeStruct((deep,) + w_attn.shape, BF16),
+            jax.ShapeDtypeStruct(w_mlp.shape, BF16),
+        ],
+        sems(GATHER_COPIES) + sems(9) + sems(deep - 1) + [pltpu.SemaphoreType.DMA((3,))],
+        [vmem, hbm, hbm, hbm],
+        [vmem, hbm, hbm, hbm],
+    )
+
+
+def cotangent_rows(cot, tokens):
+    width = cot.shape[1]
+    own = tokens // 8
+
+    def kernel(x_ref, rows_ref, send, receive):
+        d, c, t = place_of()
+        greet([(d, beside(c, 1), t), (d, beside(c, 2), t), (d, c, 1 - t)])
+        mine = pl.multiple_of((2 * c + t) * own, own)
+        rows_ref[pl.ds(mine, own), :] = x_ref[pl.ds(pl.multiple_of(t * own, own), own), :]
+        gather_rows(rows_ref, send, receive)
+
+    return call(
+        kernel, "cotangent_rows", 2, (cot,), [jax.ShapeDtypeStruct((tokens, width), BF16)],
+        sems(GATHER_COPIES),
+    )[0]
+
+
+def to_middle(heads_out, w_out, x):
+    tokens, width = heads_out.shape[0], x.shape[1]
+    own = tokens // 8
+
+    def kernel(h_ref, w_ref, x_ref, mid_ref, rows_ref, *rest):
+        bufs, (s_send, s_receive, g_send, g_receive) = rest[:5], rest[5:]
+        d, c, t = place_of()
+        greet([(d, beside(c, 1), t), (d, beside(c, 2), t), (d, c, 1 - t)])
+
+        def piece(start, out_ref):
+            by_tiles([h_ref[pl.ds(start, own), :]], [w_ref], out_ref)
+
+        scatter_rows(piece, bufs, s_send, s_receive)
+        middle = bufs[2][3] + x_ref[pl.ds(pl.multiple_of(t * own, own), own), :].astype(F32)
+        mid_ref[...] = middle
+        _, hat = norm_parts(middle)
+        rows_ref[pl.ds(pl.multiple_of((2 * c + t) * own, own), own), :] = hat.astype(BF16)
+        gather_rows(rows_ref, g_send, g_receive)
+
+    return call(
+        kernel, "to_middle", 3, (heads_out, w_out, x),
+        [jax.ShapeDtypeStruct((own, width), F32), jax.ShapeDtypeStruct((tokens, width), BF16)],
+        scatter_scratch(own, width) + sems(SCATTER_COPIES) + sems(GATHER_COPIES),
+        flops=2 * tokens * width * heads_out.shape[1],
+    )
+
+
+def feed_forward(rows_two, cot, middle, w_gate, w_up, w_down):
+    tokens, width = rows_two.shape
+    own = tokens // 8
+    units = w_gate.shape[1]
+
+    def kernel(
+        rows_ref, cot_ref, mid_ref, g_ref, u_ref, d_ref, hid_ref, gg_ref, gu_ref, out_ref,
+        row_buf, cot_buf, here, *rest,
+    ):
+        bufs, (s_send, s_receive, t_send, t_receive) = rest[:5], rest[5:]
+        d, c, t = place_of()
+        greet([(d, beside(c, 1), t), (d, beside(c, 2), t), (d, c, 1 - t)])
+
+        def piece(start, out_ref):
+            first = pltpu.make_async_copy(rows_ref.at[pl.ds(start, own)], row_buf, here.at[0])
+            other = pltpu.make_async_copy(cot_ref.at[pl.ds(start, own)], cot_buf, here.at[1])
+            first.start()
+            other.start()
+            first.wait()
+            rows = row_buf[...]
+            gate = dot(rows, g_ref[...], 1, 0)
+            up = dot(rows, u_ref[...], 1, 0)
+            other.wait()
+            g_hidden = dot(cot_buf[...], d_ref[...], 1, 0)
+            sig = jax.nn.sigmoid(gate)
+            silu = gate * sig
+            hidden = (silu * up).astype(BF16)
+            hid_ref[pl.ds(start, own), :] = hidden
+            gu_ref[pl.ds(start, own), :] = (g_hidden * silu).astype(BF16)
+            gg_ref[pl.ds(start, own), :] = (
+                g_hidden * up * sig * (1.0 + gate * (1.0 - sig))
+            ).astype(BF16)
+            by_tiles([hidden], [d_ref], out_ref)
+
+        scatter_rows(piece, bufs, s_send, s_receive)
+        place = out_ref.at[pl.ds(pl.multiple_of(t * own, own), own)]
+        place[...] = (mid_ref[...] + bufs[2][3]).astype(BF16)
+        copy = remote(place, place, t_send, t_receive, 0, (d, c, 1 - t))
+        copy.start()
+        copy.wait_send()
+        there = out_ref.at[pl.ds(pl.multiple_of((1 - t) * own, own), own)]
+        remote(there, there, t_send, t_receive, 0, (d, c, 1 - t)).wait_recv()
+
+    vmem, hbm = pl.BlockSpec(memory_space=pltpu.VMEM), pl.BlockSpec(memory_space=pl.ANY)
+    return call(
+        kernel, "feed_forward", 4, (rows_two, cot, middle, w_gate, w_up, w_down),
+        [jax.ShapeDtypeStruct((tokens, units), BF16)] * 3
+        + [jax.ShapeDtypeStruct((2 * own, width), BF16)],
+        [pltpu.VMEM((own, width), BF16), pltpu.VMEM((own, width), BF16), pltpu.SemaphoreType.DMA((2,))]
+        + scatter_scratch(own, width) + sems(SCATTER_COPIES) + sems(1),
+        [hbm, hbm, vmem, vmem, vmem, vmem],
+        flops=8 * tokens * width * units,
+    )
+
+
+def to_branch(g_gate, g_up, w_gate, w_up, middle, cot, w_out):
+    tokens, width = g_gate.shape[0], middle.shape[1]
+    own = tokens // 8
+    wide = w_out.shape[1]
+
+    def kernel(gg_ref, gu_ref, g_ref, u_ref, mid_ref, cot_ref, w_ref, gm_ref, rows_ref, mix_ref, *rest):
+        bufs, (s_send, s_receive, g_send, g_receive) = rest[:5], rest[5:]
+        d, c, t = place_of()
+        greet([(d, beside(c, 1), t), (d, beside(c, 2), t), (d, c, 1 - t)])
+
+        def piece(start, out_ref):
+            by_tiles(
+                [gg_ref[pl.ds(start, own), :], gu_ref[pl.ds(start, own), :]], [g_ref, u_ref], out_ref
+            )
+
+        scatter_rows(piece, bufs, s_send, s_receive)
+        scale, hat = norm_parts(mid_ref[...])
+        g_middle = cot_ref[pl.ds(pl.multiple_of(t * own, own), own), :].astype(F32) + norm_back(
+            bufs[2][3], hat, scale
+        )
+        gm_ref[...] = g_middle
+        rows_ref[pl.ds(pl.multiple_of((2 * c + t) * own, own), own), :] = g_middle.astype(BF16)
+
+        def mix(start):
+            mix_ref[pl.ds(start, own), :] = dot(
+                rows_ref[pl.ds(start, own), :], w_ref[...], 1, 0
+            ).astype(BF16)
+
+        gather_rows(rows_ref, g_send, g_receive, mix)
+
+    return call(
+        kernel, "to_branch", 5, (g_gate, g_up, w_gate, w_up, middle, cot, w_out),
+        [
+            jax.ShapeDtypeStruct((own, width), F32),
+            jax.ShapeDtypeStruct((tokens, width), BF16),
+            jax.ShapeDtypeStruct((tokens, wide), BF16),
+        ],
+        scatter_scratch(own, width) + sems(SCATTER_COPIES) + sems(GATHER_COPIES),
+        flops=4 * tokens * width * (g_gate.shape[1] + wide),
+    )
+
+
+def to_input(g_qkv, w_qkv, x, g_middle, back, weights, gain, heads):
+    tokens, width = g_qkv.shape[0], x.shape[1]
+    own = tokens // 8
+    deep = lax.axis_size("dp")
+    across = back.shape[1]
+    group = back.shape[0] // deep
+    held = group // 4
+    wide, narrow = heads * DV, heads * F
+
+    def kernel(
+        g_ref, w_ref, x_ref, gm_ref, back_ref, wq_ref, wk_ref, wv_ref, gain_ref,
+        out_ref, gq_ref, gk_ref, gv_ref, go_ref, gg_ref, *rest,
+    ):
+        bufs, (s_send, s_receive, t_send, t_receive) = rest[:5], rest[5:9]
+        terms, sums, parts, scalar, d_send, d_receive, p_send, p_receive = rest[9:]
+        d, c, t = place_of()
+        greet(
+            [(d, beside(c, k), t) for k in (1, 2, 3)]
+            + [(d, c, 1 - t)]
+            + [(depth(d, k), c, t) for k in range(1, deep)]
+        )
+
+        def deeper(k):
+            rows = pl.ds(pl.multiple_of(depth(d, k) * group, group), group)
+            return remote(
+                back_ref.at[rows], terms.at[k - 1], d_send, d_receive, k - 1, (depth(d, k), c, t)
+            )
+
+        def to_block(k):
+            rows = pl.ds(pl.multiple_of(beside(c, k) * held, held), held)
+            return remote(
+                sums.at[rows], parts.at[c], p_send, p_receive, k - 1, (d, beside(c, k), t)
+            )
+
+        def from_block(k):
+            there = parts.at[beside(c, k)]
+            return remote(there, there, p_send, p_receive, k - 1, (d, beside(c, k), t))
+
+        for k in (2, 1, 3)[: deep - 1] if deep == 4 else range(1, deep):
+            deeper(k).start()
+
+        def piece(start, ref):
+            by_tiles([g_ref[pl.ds(start, own), :]], [w_ref], ref)
+
+        scatter_rows(piece, bufs, s_send, s_receive)
+        scale, hat = norm_parts(x_ref[pl.ds(pl.multiple_of(t * own, own), own), :].astype(F32))
+        place = out_ref.at[pl.ds(pl.multiple_of(t * own, own), own)]
+        place[...] = gm_ref[...] + norm_back(bufs[2][3], hat, scale)
+        copy = remote(place, place, t_send, t_receive, 0, (d, c, 1 - t))
+        copy.start()
+
+        for k in range(1, deep):
+            deeper(k).wait_recv()
+        rows = pl.ds(pl.multiple_of(d * group, group), group)
+        total = back_ref[rows, :].astype(F32)
+        for k in range(1, deep):
+            total = total + terms[k - 1].astype(F32)
+        sums[...] = total.astype(BF16)
+        for k in (3, 1, 2):
+            to_block(k).start()
+        parts[c] = sums[pl.ds(pl.multiple_of(c * held, held), held), :]
+        for k in (1, 2, 3):
+            from_block(k).wait_recv()
+        gain_column = gain_ref[...]
+
+        def owned(start, count):
+            return jnp.concatenate(
+                [parts[b][:, start : start + count].astype(F32) for b in range(4)], axis=1
+            )
+
+        own_term = jnp.zeros((held, 1), F32)
+        for ref, weight, start, count in (
+            (gv_ref, wv_ref, 0, wide),
+            (gq_ref, wq_ref, wide, narrow),
+            (gk_ref, wk_ref, wide + narrow, narrow),
+        ):
+            s = owned(start, count)
+            own_term = own_term + jnp.sum(s * weight[...].astype(F32), axis=1, keepdims=True)
+            ref[...] = s * gain_column
+        go_ref[...] = owned(wide + 2 * narrow, wide)
+        scalar[0] = jnp.broadcast_to(own_term, (held, 128))
+        swap = remote(scalar.at[0], scalar.at[1], t_send, t_receive, 1, (d, c, 1 - t))
+        swap.start()
+        swap.wait()
+        gg_ref[...] = own_term + scalar[1][:, :1]
+
+        copy.wait_send()
+        there = out_ref.at[pl.ds(pl.multiple_of((1 - t) * own, own), own)]
+        remote(there, there, t_send, t_receive, 0, (d, c, 1 - t)).wait_recv()
+        for k in range(1, deep):
+            deeper(k).wait_send()
+        for k in (1, 2, 3):
+            to_block(k).wait_send()
+
+    w_q, w_k, w_v = weights
+    return call(
+        kernel, "to_input", 6, (g_qkv, w_qkv, x, g_middle, back, w_q, w_k, w_v, gain),
+        [
+            jax.ShapeDtypeStruct((2 * own, width), F32),
+            jax.ShapeDtypeStruct(w_q.shape, F32),
+            jax.ShapeDtypeStruct(w_k.shape, F32),
+            jax.ShapeDtypeStruct(w_v.shape, F32),
+            jax.ShapeDtypeStruct(w_v.shape, F32),
+            jax.ShapeDtypeStruct((held, 1), F32),
+        ],
+        scatter_scratch(own, width) + sems(SCATTER_COPIES) + sems(2)
+        + [
+            pltpu.VMEM((deep - 1, group, across), BF16),
+            pltpu.VMEM((group, across), BF16),
+            pltpu.VMEM((4, held, across), BF16),
+            pltpu.VMEM((2, held, 128), F32),
+        ]
+        + sems(deep - 1) + sems(3),
+        flops=2 * tokens * width * g_qkv.shape[1],
+    )
+
+
 def by_columns(weight, parts):
     rows, columns = weight.shape
     return weight.reshape(rows, parts, columns // parts).transpose(1, 0, 2)
@@ -551,135 +1142,79 @@
     mlp_gain,
 ):
     parts = lax.axis_size("ctx")
-    plane = ("ctx", "tp")
     heads = q_weight.shape[1] // F // parts
     wide = heads * DV
     narrow = heads * F
     units = gate_weight.shape[1] // parts
-    rows = activations.shape[1] // lax.axis_size("tp")
-    mine = lax.axis_index("tp") * rows
-    f32, bf16 = jnp.float32, jnp.bfloat16
-
-    def dot(a, b, ca, cb):
-        return lax.dot_general(a, b, (((ca,), (cb,)), ((), ())), preferred_element_type=f32)
-
-    def gather(own):
-        return lax.all_gather(own, plane, axis=0, tiled=True)
-
-    def scatter(partial):
-        return lax.psum_scatter(
-            partial.astype(bf16), plane, scatter_dimension=0, tiled=True
-        ).astype(f32)
-
-    def fetch(packed):
-        mixed = lax.all_to_all(packed, "ctx", 0, 0, tiled=True)
-        return lax.all_gather(mixed, "dp", axis=0, tiled=True).reshape(-1, packed.shape[2])
-
-    gain_one = attn_gain.astype(f32)[:, None]
-    gain_two = mlp_gain.astype(f32)[:, None]
-    scaled = lambda w, g: (w.astype(f32) * g).astype(bf16)
-    w_attn = fetch(
-        jnp.concatenate(
-            [
-                by_columns(scaled(v_weight, gain_one), parts),
-                by_columns(scaled(q_weight, gain_one), parts),
-                by_columns(scaled(k_weight, gain_one), parts),
-                by_columns(o_weight, parts),
-            ],
-            axis=2,
-        )
-    )
-    w_mlp = fetch(
-        jnp.concatenate(
-            [
-                by_columns(scaled(gate_weight, gain_two), parts),
-                by_columns(scaled(up_weight, gain_two), parts),
-                by_columns(down_weight, parts),
-            ],
-            axis=2,
-        )
-    )
+    tokens = activations.shape[1] * parts
+    x, cot_block = activations[0], cotangent[0]
+
+    gain_one = attn_gain.astype(F32)[:, None]
+    gain_two = mlp_gain.astype(F32)[:, None]
+    scaled = lambda w, g: (w.astype(F32) * g).astype(BF16)
+    cut_attn = jnp.concatenate(
+        [
+            by_columns(scaled(v_weight, gain_one), parts),
+            by_columns(scaled(q_weight, gain_one), parts),
+            by_columns(scaled(k_weight, gain_one), parts),
+            by_columns(o_weight, parts),
+        ],
+        axis=2,
+    )
+    cut_mlp = jnp.concatenate(
+        [
+            by_columns(scaled(gate_weight, gain_two), parts),
+            by_columns(scaled(up_weight, gain_two), parts),
+            by_columns(down_weight, parts),
+        ],
+        axis=2,
+    )
+    rows_one, segments, w_attn, cut_mlp = front(x, seg_ids, cut_attn, cut_mlp, tokens)
+    w_attn = w_attn.reshape(-1, w_attn.shape[3])
+    w_mlp = lax.all_gather(cut_mlp, "dp", axis=0, tiled=True).reshape(-1, cut_mlp.shape[2])
     w_qkv, w_out = w_attn[:, : wide + 2 * narrow], w_attn[:, wide + 2 * narrow :]
     w_gate, w_up, w_down = w_mlp[:, :units], w_mlp[:, units : 2 * units], w_mlp[:, 2 * units :]
-
-    x_own = lax.dynamic_slice_in_dim(activations[0], mine, rows, 0).astype(f32)
-    r_one = lax.rsqrt(jnp.mean(x_own * x_own, axis=1, keepdims=True) + EPSILON)
-    hat_one = x_own * r_one
-    rows_one = gather(hat_one.astype(bf16))
-    cot_own = lax.dynamic_slice_in_dim(cotangent[0], mine, rows, 0)
-    cot = gather(cot_own)
-    segments = lax.all_gather(seg_ids[0], "ctx", axis=0, tiled=True)
-    seg_rows, seg_cols = segments[:, None], segments[None, :]
-
-    qkv = dot(rows_one, w_qkv, 1, 0).astype(bf16)
+    cot = cotangent_rows(cot_block, tokens)
+    seg_rows, seg_cols = segments.reshape(tokens, 1), segments.reshape(1, tokens)
+
+    qkv = dot(rows_one, w_qkv, 1, 0).astype(BF16)
     mixed, denom, heads_out = attention_forward(qkv, seg_rows, seg_cols, heads)
-    middle = x_own + scatter(dot(heads_out, w_out, 1, 1))
-    r_two = lax.rsqrt(jnp.mean(middle * middle, axis=1, keepdims=True) + EPSILON)
-    hat_two = middle * r_two
-    rows_two = gather(hat_two.astype(bf16))
-    gate = dot(rows_two, w_gate, 1, 0)
-    up = dot(rows_two, w_up, 1, 0)
-    sig = jax.nn.sigmoid(gate)
-    hidden = (gate * sig * up).astype(bf16)
-    out_own = (middle + scatter(dot(hidden, w_down, 1, 1))).astype(bf16)
-    out = lax.all_gather(out_own, "tp", axis=0, tiled=True)
-
-    g_hidden = dot(cot, w_down, 1, 0)
-    g_gate = (g_hidden * up * sig * (1.0 + gate * (1.0 - sig))).astype(bf16)
-    g_up = (g_hidden * gate * sig).astype(bf16)
-    e_two = scatter(dot(g_gate, w_gate, 1, 1) + dot(g_up, w_up, 1, 1))
-    g_middle = cot_own.astype(f32) + r_two * (
-        e_two - hat_two * jnp.mean(e_two * hat_two, axis=1, keepdims=True)
-    )
-    back_mlp = to_owner(
-        jnp.concatenate(
-            [dot(rows_two, g_gate, 0, 0), dot(rows_two, g_up, 0, 0), dot(cot, hidden, 0, 0)], axis=1
-        ).astype(bf16)
-    )
-    branch = gather(g_middle.astype(bf16))
-    g_mixed = dot(branch, w_out, 1, 0).astype(bf16)
+    middle, rows_two = to_middle(heads_out, w_out, x)
+    hidden, g_gate, g_up, out = feed_forward(rows_two, cot, middle, w_gate, w_up, w_down)
+    back_mlp = jnp.concatenate(
+        [dot(rows_two, g_gate, 0, 0), dot(rows_two, g_up, 0, 0), dot(cot, hidden, 0, 0)], axis=1
+    ).astype(BF16)
+    g_gate, back_mlp = lax.optimization_barrier((g_gate, back_mlp))
+    back_mlp = to_owner(back_mlp)
+    g_middle, branch, g_mixed = to_branch(g_gate, g_up, w_gate, w_up, middle, cot_block, w_out)
     g_qkv = attention_backward(qkv, g_mixed, mixed, denom, seg_rows, seg_cols, heads)
-    e_one = scatter(dot(g_qkv, w_qkv, 1, 1))
-    g_x = g_middle + r_one * (e_one - hat_one * jnp.mean(e_one * hat_one, axis=1, keepdims=True))
-    g_input = lax.all_gather(g_x, "tp", axis=0, tiled=True)
-    back_attn = to_owner(
-        jnp.concatenate([dot(rows_one, g_qkv, 0, 0), dot(branch, heads_out, 0, 0)], axis=1).astype(
-            bf16
-        )
+    back_attn = jnp.concatenate(
+        [dot(rows_one, g_qkv, 0, 0), dot(branch, heads_out, 0, 0)], axis=1
+    ).astype(BF16)
+    g_input, s_q, s_k, s_v, s_o, attn_row = to_input(
+        g_qkv, w_qkv, x, g_middle, back_attn, (q_weight, k_weight, v_weight), gain_one, heads
     )
 
     def owned(back, start, width):
-        return back[:, :, start : start + width].reshape(back.shape[0], -1).astype(f32)
-
-    s_v = owned(back_attn, 0, wide)
-    s_q = owned(back_attn, wide, narrow)
-    s_k = owned(back_attn, wide + narrow, narrow)
-    s_o = owned(back_attn, wide + 2 * narrow, wide)
+        return back[:, :, start : start + width].reshape(back.shape[0], -1).astype(F32)
+
     s_gate = owned(back_mlp, 0, units)
     s_up = owned(back_mlp, units, units)
     s_down = owned(back_mlp, 2 * units, units)
-    along = lambda s, w: jnp.sum(s * w.astype(f32), axis=1)
-    gains = lax.psum(
-        jnp.stack(
-            [
-                along(s_q, q_weight) + along(s_k, k_weight) + along(s_v, v_weight),
-                along(s_gate, gate_weight) + along(s_up, up_weight),
-            ]
-        ),
-        "tp",
-    )
+    along = lambda s, w: jnp.sum(s * w.astype(F32), axis=1)
+    mlp_row = lax.psum(along(s_gate, gate_weight) + along(s_up, up_weight), "tp")
     return (
         out[None],
         g_input[None],
-        s_q * gain_one,
-        s_k * gain_one,
-        s_v * gain_one,
+        s_q,
+        s_k,
+        s_v,
         s_o,
         s_gate * gain_two,
         s_up * gain_two,
         s_down,
-        gains[0],
-        gains[1],
+        attn_row[:, 0],
+        mlp_row,
     )
 
 

time: 1130 us -> 698 us (0.62)
  the two profiles are of different devices: /device:TPU:0 before, /device:TPU:9 now
where the time goes in v2:
time: 698 us; the launch traced here: 690 us
  Pallas kernels  498 us (71%)
  local copies, waits for them, and re-layouts  71.2 us (10%)
  matrix products  60.4 us (9%)
  waiting for transfers between devices  24.4 us (3%)
  other arithmetic  15.2 us (2%)
  between operations  14.7 us (2%)
    pallas_call x6, Pallas kernels, call(): pl.pallas_call(kernel, in_specs=spaces or [vmem] * len(arrays), out_specs...  455 us
    dot_general x6, matrix products, dot(): lax.dot_general(a, b, (((ca,), (cb,)), ((), ())), preferred_element_type=...  60.4 us
    pallas_call x1, Pallas kernels, attention_backward(): pl.pallas_call(kernel, grid=(blocks,), in_specs=[whole(qkv.shape), whole(...  26.8 us
    reduce_scatter x1, waiting for transfers between devices, to_owner(): summed = lax.psum_scatter(packed, 'dp', scatter_dimension=0, tiled=True)  24.3 us
    unnamed x44, local copies, waits for them, and re-layouts  22.5 us
    pallas_call x1, Pallas kernels, attention_forward(): pl.pallas_call(kernel, grid=(tokens // BLOCK,), in_specs=[pl.BlockSpec(qk...  15.7 us
  transfers between devices with their start and end apart: 3, of which 1 were waited for; matrix products, arithmetic and copies ran while one was open for 5% of the time, Pallas kernels for 50%

profile of v2, /device:TPU:9, one launch (start us, length us, event | category | flops | bytes accessed | tf_op | source)
XLA Modules:
  0.0 690.4 jit_solution(7717202488225754)
XLA Ops:
  8.6 0.9 copy.82
  9.5 0.9 copy.84
  10.6 1.1 copy.86
  11.9 1.1 copy.80
  13.6 1.5 copy.90
  15.1 2.5 copy.92
  17.6 1.4 copy.93
  19.0 1.4 fusion.2
  20.4 2.3 copy.89
  22.6 2.3 copy.91
  24.9 4.8 concatenate.15.wm_ref
  29.7 1.1 pad_maximum_fusion.2.wa_ref
  30.8 77.7 %front.1 = (bf16[2048,2048]{1,0:T(8,128)(2,1)}, s32[4,1,512]{2,1,0:T(1,128)}, bf16[4,4,128,576]{3,2,1,0:T(8,128)(2,1)}, bf16[4,128,2112]{2,1,0:T(8,128)(2,1)}) custom-call(bf16[512,2048]{1,0:T(8,128)(2,1)} %bitcast.57, s32[1,1,512]{2,1,0:T(1,128)} %bitcast.84, bf16[4,128,576]{2,1,0:T(8,128)(2,1)} %pad_maximum_fusion.2.wa_ref, ...), custom_call_target="tpu_custom_call" | custom-call | bytes 4851712 | tf_op jit(solution)/shard_map/front/pallas_call | solution.py:742
  108.5 4.1 copy.96
  112.6 44.2 %cotangent_rows.1.cot_ref = bf16[2048,2048]{1,0:T(8,128)(2,1)} custom-call(bf16[512,2048]{1,0:T(8,128)(2,1)} %bitcast.70), custom_call_target="tpu_custom_call" | custom-call | bytes 2097152 | tf_op jit(solution)/shard_map/cotangent_rows/pallas_call | solution.py:742
  156.8 2.8 slice.33.w_ref
  159.6 1.3 copy.95.row_ref
  161.0 9.5 %convolution_convert_fusion.3.x_ref = bf16[2048,320]{1,0:T(8,128)(2,1)} fusion(bf16[2048,2048]{1,0:T(8,128)(2,1)} %get-tuple-element.35, bf16[2048,576]{1,0:T(8,128)(2,1)} %bitcast.68), kind=kOutput, calls=%fused_computation.5 | convolution fusion | flops 2685009920 | bytes 11272192 | tf_op jit(solution)/shard_map/dot_general | solution.py:531
  170.5 15.7 %attn_forward.1 = (f32[2048,256]{1,0:T(8,128)}, f32[2048,2]{1,0:T(8,128)}, bf16[2048,256]{1,0:T(8,128)(2,1)}) custom-call(bf16[2048,320]{1,0:T(8,128)(2,1)} %convolution_convert_fusion.3.x_ref, s32[2048,1]{1,0:T(8,128)} %copy.95.row_ref, s32[1,2048]{1,0:T(1,128)} %bitcast.81), custom_call_target="tpu_custom_call" | custom-call | flops 3355443200 | bytes 6291456 | tf_op jit(solution)/shard_map/attn_forward/pallas_call | solution.py:383
  186.2 86.2 %to_middle.1 = (f32[256,2048]{1,0:T(8,128)}, bf16[2048,2048]{1,0:T(8,128)(2,1)}) custom-call(bf16[2048,256]{1,0:T(8,128)(2,1)} %get-tuple-element.38.h_ref, bf16[2048,256]{1,0:T(8,128)(2,1)} %slice.33.w_ref, bf16[512,2048]{1,0:T(8,128)(2,1)} %bitcast.58), custom_call_target="tpu_custom_call" | custom-call | flops 2147483648 | bytes 4194304 | tf_op jit(solution)/shard_map/to_middle/pallas_call | solution.py:742
  272.4 11.7 %copy.97 = bf16[16,128,2112]{2,1,0:T(8,128)(2,1)} copy(bf16[16,128,2112]{1,2,0:T(8,128)(2,1)} %all-gather.2.cloned.1.call-done) | data formatting | bytes 17301504 | tf_op jit(solution)/shard_map/all_gather | solution.py:1174
  284.1 6.9 %fusion.6 = (bf16[2048,704]{1,0:T(8,128)(2,1)}, bf16[2048,704]{1,0:T(8,128)(2,1)}, bf16[2048,704]{1,0:T(8,128)(2,1)}) fusion(bf16[2048,2112]{1,0:T(8,128)(2,1)} %bitcast.55), kind=kLoop, calls=%fused_computation.27 | loop fusion | bytes 17301504 | tf_op jit(solution)/shard_map/slice | solution.py:1176
  291.0 75.2 %feed_forward.1 = (bf16[2048,704]{1,0:T(8,128)(2,1)}, bf16[2048,704]{1,0:T(8,128)(2,1)}, bf16[2048,704]{1,0:T(8,128)(2,1)}, bf16[512,2048]{1,0:T(8,128)(2,1)}) custom-call(bf16[2048,2048]{1,0:T(8,128)(2,1)} %get-tuple-element.39.rows_ref, bf16[2048,2048]{1,0:T(8,128)(2,1)} %cotangent_rows.1.cot_ref, f32[256,2048]{1,0:T(8,128)} %get-tuple-element.40.mid_ref, ...), custom_call_target="tpu_custom_call" | custom-call | flops 23622320128 | bytes 27525120 | tf_op jit(solution)/shard_map/feed_forward/pallas_call | solution.py:742
  366.3 9.7 %fusion = bf16[2048,704]{0,1:T(8,128)(2,1)S(1)} fusion(bf16[2048,704]{1,0:T(8,128)(2,1)} %get-tuple-element.45, bf16[2048,2048]{1,0:T(8,128)(2,1)} %cotangent_rows.1.cot_ref), kind=kOutput, calls=%fused_computation.4 | convolution fusion | flops 5907021824 | bytes 14155776 | tf_op jit(solution)/shard_map/dot_general | solution.py:531
  376.0 20.4 %convolution_convert_fusion.2 = bf16[2048,704]{0,1:T(8,128)(2,1)S(1)} fusion(bf16[2048,2048]{1,0:T(8,128)(2,1)} %get-tuple-element.39.rows_ref, bf16[2048,704]{1,0:T(8,128)(2,1)S(1)} %copy-done.10), kind=kOutput, calls=%fused_computation.3 | convolution fusion | flops 5907021824 | bytes 14155776 | tf_op jit(solution)/shard_map/dot_general | solution.py:531
  396.5 6.7 convolution_convert_fusion.1
  403.2 4.4 pad_maximum_fusion
  407.6 2.7 slice.32.w_ref
  411.1 92.8 %to_branch.1 = (f32[256,2048]{1,0:T(8,128)}, bf16[2048,2048]{1,0:T(8,128)(2,1)}, bf16[2048,256]{1,0:T(8,128)(2,1)}) custom-call(bf16[2048,704]{1,0:T(8,128)(2,1)} %get-tuple-element.46.gg_ref, bf16[2048,704]{1,0:T(8,128)(2,1)} %get-tuple-element.44.gu_ref, bf16[2048,704]{1,0:T(8,128)(2,1)} %get-tuple-element.94.g_ref, ...), custom_call_target="tpu_custom_call" | custom-call | flops 16106127360 | bytes 16777216 | tf_op jit(solution)/shard_map/to_branch/pallas_call | solution.py:742
  503.9 26.8 %attn_backward.1.g_ref = bf16[2048,320]{1,0:T(8,128)(2,1)} custom-call(bf16[2048,320]{1,0:T(8,128)(2,1)} %convolution_convert_fusion.3.x_ref, bf16[2048,256]{1,0:T(8,128)(2,1)} %get-tuple-element.47.gm_ref, f32[2048,256]{1,0:T(8,128)} %get-tuple-element.48.m_ref, f32[2048,2]{1,0:T(8,128)} %get-tuple-element.49.d_ref, s32[2048,1]{1,0:T(8,128)} %copy.95.row_ref, ...), custom_call_target="tpu_custom_call" | custom-call | flops 6710886400 | bytes 6291456 | tf_op jit(solution)/shard_map/attn_backward/pallas_call | solution.py:499
  530.7 24.3 %reduce-scatter.2.cloned.1.call-done = bf16[512,2112]{0,1:T(8,128)(2,1)} async-done(((bf16[2048,2112]{0,1:T(8,128)(2,1)}), bf16[512,2112]{0,1:T(8,128)(2,1)}) %reduce-scatter.2.cloned.1.call-update) | async-done | bytes 2162704 | tf_op jit(solution)/shard_map/reduce_scatter | solution.py:1123
  555.0 3.3 copy_bitcast_fusion
  558.3 3.8 all-to-all-start
  562.1 7.8 %convolution_convert_fusion.4 = bf16[2048,320]{0,1:T(8,128)(2,1)} fusion(bf16[2048,2048]{1,0:T(8,128)(2,1)} %get-tuple-element.35, bf16[2048,320]{1,0:T(8,128)(2,1)} %attn_backward.1.g_ref), kind=kOutput, calls=%fused_computation.6 | convolution fusion | flops 2685009920 | bytes 11010048 | tf_op jit(solution)/shard_map/dot_general | solution.py:531
  569.9 2.5 copy.100
  572.5 6.2 convolution_convert_fusion.5
  578.7 2.3 pad_maximum_fusion.1.back_ref
  581.0 79.2 %to_input.1 = (f32[512,2048]{1,0:T(8,128)}, f32[128,128]{1,0:T(8,128)}, f32[128,128]{1,0:T(8,128)}, f32[128,1024]{1,0:T(8,128)}, f32[128,1024]{1,0:T(8,128)}, /*index=5*/f32[128,1]{1,0:T(8,128)}) custom-call(bf16[2048,320]{1,0:T(8,128)(2,1)} %attn_backward.1.g_ref, bf16[2048,320]{1,0:T(8,128)(2,1)} %slice.32.w_ref, bf16[512,2048]{1,0:T(8,128)(2,1)} %bitcast.59, ...), custom_call_target="tpu_custom_call" | custom-call | flops 2684354560 | bytes 9503232 | tf_op jit(solution)/shard_map/to_input/pallas_call | solution.py:742
  660.2 1.5 reduce
  661.7 1.2 fusion.7
  663.1 1.5 copy.105
  664.6 2.9 fusion.3
  667.5 3.0 psum.7
  670.5 2.9 copy.103
  673.4 1.5 copy.104
  674.9 3.3 copy.116
  678.3 2.0 copy.117
  681.5 0.8 copy.120
  (50 shorter events, 5.5 us)
Async XLA Ops:
  7.2 6.1 copy-start.4
  7.2 265.2 %all-gather.2.cloned.1.call-start = ((), (), s32[]{:S(2)}) async-start(), calls=%async_computation.2 | async-start | bytes 10813440 | tf_op jit(solution)/shard_map/all_gather | solution.py:1174
  15.1 5.3 copy-start
  112.6 442.4 %reduce-scatter.2.cloned.1.call-start = ((), (), s32[]{:S(2)}) async-start(), calls=%async_computation.3 | async-start | bytes 10813440 | tf_op jit(solution)/shard_map/reduce_scatter | solution.py:1123
  112.6 47.0 %copy-start.9 = (s32[4,1,512]{2,1,0:T(1,128)S(1)}, s32[4,1,512]{2,1,0:T(1,128)}, u32[]{:S(2)}) copy-start(s32[4,1,512]{2,1,0:T(1,128)} %get-tuple-element.37) | copy-start | bytes 24580
  366.2 9.7 %copy-start.10 = (bf16[2048,704]{1,0:T(8,128)(2,1)S(1)}, bf16[2048,704]{1,0:T(8,128)(2,1)}, u32[]{:S(2)}) copy-start(bf16[2048,704]{1,0:T(8,128)(2,1)} %get-tuple-element.46.gg_ref) | copy-start | bytes 8650756
  366.2 30.2 %slice-start = ((s8[8388608]{0:T(1024)(128)(4,1)}), s8[4194304]{0:T(1024)(128)(4,1)S(1)}, s32[]{:S(2)}) async-start(s8[8388608]{0:T(1024)(128)(4,1)} %bitcast.85), calls=%async_computation.4 | async-start | bytes 8388608
  376.0 20.5 %slice-start.1 = ((s8[8388608]{0:T(1024)(128)(4,1)}), s8[4194304]{0:T(1024)(128)(4,1)S(1)}, s32[]{:S(2)}) async-start(s8[8388608]{0:T(1024)(128)(4,1)} %bitcast.85), calls=%async_computation.5 | async-start | bytes 8388608
  376.0 20.5 %copy-start.11 = (bf16[2048,704]{1,0:T(8,128)(2,1)S(1)}, bf16[2048,704]{1,0:T(8,128)(2,1)}, u32[]{:S(2)}) copy-start(bf16[2048,704]{1,0:T(8,128)(2,1)} %get-tuple-element.44.gu_ref) | copy-start | bytes 8650756
  558.3 103.4 %all-to-all-start = ((bf16[4,128,2112]{1,2,0:T(8,128)(2,1)}), bf16[4,128,2112]{1,2,0:T(8,128)(2,1)S(1)}, u32[]{:S(2)}, u32[]{:S(2)}) async-start(bf16[4,128,2112]{1,2,0:T(8,128)(2,1)} %copy_bitcast_fusion), calls=%async_computation.1 | async-start | bytes 4325376 | tf_op jit(solution)/shard_map/all_to_all | solution.py:1125
  572.5 6.2 copy-start.2
  662.9 1.7 copy-start.1
  674.9 3.3 copy-start.3
  678.2 2.0 copy-start.8
  678.2 2.7 copy-start.7
  678.2 3.3 copy-start.6
  678.2 4.1 copy-start.5
Sparse Core Ops, SparseCore 0:
  112.7 149.6 all-gather.1
  407.8 147.1 reduce-scatter.1

commit v3 on v0

--- a/solution.py
+++ b/solution.py
@@ -1,6 +1,8 @@
 import jax
 import jax.numpy as jnp
 from jax import lax
+from jax.experimental import pallas as pl
+from jax.experimental.pallas import tpu as pltpu
 from jax.sharding import PartitionSpec as P
 
 F = 16
@@ -9,6 +11,7 @@
 
 EPSILON = 1e-05
 PRECISE = lax.Precision.HIGHEST
+VMEM_MOST = 60 * 2**20
 
 
 def prefix(x, axis, join, neutral, backward):
@@ -316,6 +319,1305 @@
     )
 
 
+BLOCK = 512
+
+
+MESH = pl.DeviceIdType.MESH
+BF16, F32 = jnp.bfloat16, jnp.float32
+
+
+def dot(a, b, ca, cb):
+    return lax.dot_general(a, b, (((ca,), (cb,)), ((), ())), preferred_element_type=F32)
+
+
+def place_of():
+    return lax.axis_index("dp"), lax.axis_index("ctx"), lax.axis_index("tp")
+
+
+def beside(c, across):
+    x, y = lax.rem(c, 2), lax.div(c, 2)
+    return lax.rem(x + across % 2, 2) + 2 * lax.rem(y + across // 2, 2)
+
+
+def greet(devices):
+    barrier = pltpu.get_barrier_semaphore()
+    for device in devices:
+        pl.semaphore_signal(barrier, inc=1, device_id=device, device_id_type=MESH)
+    pl.semaphore_wait(barrier, len(devices))
+
+
+def remote(source, target, send, receive, k, device):
+    return pltpu.make_async_remote_copy(
+        src_ref=source,
+        dst_ref=target,
+        send_sem=send.at[k],
+        recv_sem=receive.at[k],
+        device_id=device,
+        device_id_type=MESH,
+    )
+
+
+def gather_rows(buf, send, receive, piece=None, early=None, middle=None, late=None):
+    d, c, t = place_of()
+    own = buf.shape[0] // 8
+    half = own // 2
+    to_x, to_y, to_t = (d, beside(c, 1), t), (d, beside(c, 2), t), (d, c, 1 - t)
+    started = []
+
+    def part(across, core, h):
+        block = c if across == 0 else beside(c, across)
+        start = (2 * block + core) * own + h * half
+        return buf.at[pl.ds(pl.multiple_of(start, half), half)]
+
+    def put(k, across, h, device):
+        ref = part(across, t, h)
+        copy = remote(ref, ref, send, receive, k, device)
+        copy.start()
+        started.append(copy)
+
+    def got(k, across, core, h):
+        ref = part(across, core, h)
+        remote(ref, ref, send, receive, k, to_t).wait_recv()
+
+    def work(across, core):
+        if piece is not None:
+            block = c if across == 0 else beside(c, across)
+            piece(pl.multiple_of((2 * block + core) * own, own))
+
+    put(0, 0, 0, to_x)
+    put(1, 0, 1, to_y)
+    put(2, 0, 1, to_x)
+    put(3, 0, 0, to_y)
+    put(6, 0, 0, to_t)
+    put(7, 0, 1, to_t)
+    if early is not None:
+        early()
+    work(0, t)
+    got(6, 0, 1 - t, 0)
+    got(7, 0, 1 - t, 1)
+    work(0, 1 - t)
+    got(0, 1, t, 0)
+    put(4, 1, 0, to_y)
+    put(8, 1, 0, to_t)
+    got(1, 2, t, 1)
+    put(5, 2, 1, to_x)
+    put(9, 2, 1, to_t)
+    if middle is not None:
+        middle()
+    got(2, 1, t, 1)
+    put(10, 1, 1, to_t)
+    got(3, 2, t, 0)
+    put(11, 2, 0, to_t)
+    if late is not None:
+        late()
+    work(1, t)
+    work(2, t)
+    got(8, 1, 1 - t, 0)
+    got(10, 1, 1 - t, 1)
+    work(1, 1 - t)
+    got(9, 2, 1 - t, 1)
+    got(11, 2, 1 - t, 0)
+    work(2, 1 - t)
+    got(4, 3, t, 0)
+    put(12, 3, 0, to_t)
+    got(5, 3, t, 1)
+    put(13, 3, 1, to_t)
+    work(3, t)
+    got(12, 3, 1 - t, 0)
+    got(13, 3, 1 - t, 1)
+    work(3, 1 - t)
+    for copy in started:
+        copy.wait_send()
+
+
+GATHER_COPIES = 14
+
+
+def scatter_rows(terms, bufs, send, receive, fill=None):
+    to_core, from_core, kept, over, came, stage = bufs
+    d, c, t = place_of()
+    own, width = kept.shape[1:]
+    half = own // 2
+    tile = stage.shape[1]
+    to_x, to_y, to_t = (d, beside(c, 1), t), (d, beside(c, 2), t), (d, c, 1 - t)
+
+    def link(k):
+        return remote(over.at[k], came.at[k], send, receive, 4 + k, to_x if k % 2 == 0 else to_y)
+
+    def core(i):
+        return remote(to_core.at[lax.rem(i, 2)], from_core.at[i], send, receive, i, to_t)
+
+    def total(i, h, *extra):
+        rows = pl.ds(h * half, half)
+        out = kept[i % 3, rows, :]
+        for k in extra:
+            out = out + came[k].astype(F32)
+        return out
+
+    def ready(k, i, h, *extra):
+        over[k] = total(i, h, *extra).astype(BF16)
+
+    def joined(i):
+        core(i).wait_recv()
+        slot = lax.rem(i, 3)
+        kept[slot] = kept[slot] + from_core[i].astype(F32)
+
+    def step(i, carry):
+        across = 3 - i
+        x, y = lax.rem(c, 2), lax.div(c, 2)
+        block = lax.rem(x + lax.rem(across, 2), 2) + 2 * lax.rem(y + lax.div(across, 2), 2)
+        pairs = terms(i, pl.multiple_of(2 * block * own, 2 * own))
+
+        @pl.when(i >= 2)
+        def _():
+            core(i - 2).wait_send()
+
+        @pl.loop(0, width // tile)
+        def _(n):
+            columns = pl.ds(pl.multiple_of(n * tile, tile), tile)
+            out = None
+            for rows, matrix, part in pairs:
+                term = dot(rows, matrix[columns, part], 1, 1)
+                out = term if out is None else out + term
+            stage[...] = out
+            to_core[lax.rem(i, 2), :, columns] = stage[
+                pl.ds(pl.multiple_of((1 - t) * own, own), own), :
+            ].astype(BF16)
+            kept[lax.rem(i, 3), :, columns] = stage[pl.ds(pl.multiple_of(t * own, own), own), :]
+
+        core(i).start()
+
+        @pl.when(i == 0)
+        def _():
+            joined(0)
+            ready(0, 0, 0)
+            link(0).start()
+            ready(1, 0, 1)
+            link(1).start()
+
+        @pl.when(i == 2)
+        def _():
+            joined(1)
+            ready(3, 1, 1)
+            link(3).start()
+
+        return carry
+
+    lax.fori_loop(0, 4, step, 0)
+    joined(2)
+    ready(2, 2, 0)
+    link(2).start()
+    if fill is not None:
+        fill(0)
+    link(0).wait_recv()
+    link(1).wait_recv()
+    ready(4, 2, 1, 1)
+    ready(5, 1, 0, 0)
+    link(4).start()
+    link(5).start()
+    joined(3)
+    if fill is not None:
+        fill(1)
+    for k in (2, 3, 4, 5):
+        link(k).wait_recv()
+    core(2).wait_send()
+    core(3).wait_send()
+    for k in range(6):
+        link(k).wait_send()
+    return jnp.concatenate([total(3, 0, 2, 5), total(3, 1, 3, 4)], axis=0)
+
+
+SCATTER_COPIES = 10
+
+
+def scatter_scratch(own, width):
+    return [
+        pltpu.VMEM((2, own, width), BF16),
+        pltpu.VMEM((4, own, width), BF16),
+        pltpu.VMEM((3, own, width), F32),
+        pltpu.VMEM((6, own // 2, width), BF16),
+        pltpu.VMEM((6, own // 2, width), BF16),
+        pltpu.VMEM((2 * own, width // 2), F32),
+    ]
+
+
+def norm_parts(rows):
+    scale = lax.rsqrt(jnp.mean(rows * rows, axis=1, keepdims=True) + EPSILON)
+    return scale, rows * scale
+
+
+def norm_back(e, hat, scale):
+    return scale * (e - hat * jnp.mean(e * hat, axis=1, keepdims=True))
+
+
+def call(kernel, name, collective, arrays, out_shape, scratch, spaces=None, out_spaces=None, flops=0):
+    vmem = pl.BlockSpec(memory_space=pltpu.VMEM)
+    moved = sum(a.size * a.dtype.itemsize for a in arrays)
+    return pl.pallas_call(
+        kernel,
+        in_specs=spaces or [vmem] * len(arrays),
+        out_specs=out_spaces or [vmem] * len(out_shape),
+        out_shape=out_shape,
+        scratch_shapes=scratch,
+        compiler_params=pltpu.CompilerParams(
+            collective_id=collective, has_side_effects=True, vmem_limit_bytes=VMEM_MOST
+        ),
+        cost_estimate=pl.CostEstimate(flops=flops, bytes_accessed=moved, transcendentals=0),
+        name=name,
+    )(*arrays)
+
+
+def sems(count):
+    return [pltpu.SemaphoreType.DMA((count,)), pltpu.SemaphoreType.DMA((count,))]
+
+
+def depth(d, k):
+    return lax.rem(d + k, lax.axis_size("dp"))
+
+
+def columns(ref, gain, start, count):
+    low = start // 128 * 128
+    high = -(-(start + count) // 128) * 128
+    value = ref[:, low:high].astype(F32)
+    if gain is not None:
+        value = value * gain
+    return value[:, start - low : start - low + count]
+
+
+def whole_tiles(count):
+    return -(-count // 128) * 128
+
+
+def front(x, seg, weights, gains, tokens, heads):
+    width = x.shape[1]
+    own = tokens // 8
+    deep = lax.axis_size("dp")
+    held, units = weights[4].shape[0], weights[4].shape[1] // 4
+    wide, narrow = heads * DV, heads * F
+    main = units // 128 * 128
+    packed = 2 * wide + 2 * narrow
+
+    def kernel(
+        x_ref, seg_ref, q_ref, k_ref, v_ref, o_ref, g_ref, u_ref, one_ref, two_ref,
+        rows_ref, segs_ref, wa_out, wg_out,
+        cut_a, cut_g,
+        send, receive, small_send, small_receive, deep_send, deep_receive, here,
+    ):
+        d, c, t = place_of()
+        jobs = (
+            (lambda block: cut_a.at[block], lambda block: wa_out.at[d, block]),
+            (lambda block: seg_ref.at[0], lambda block: segs_ref.at[block]),
+            (lambda block: cut_g.at[block], lambda block: wg_out.at[block]),
+        )
+
+        def local(n):
+            return pltpu.make_async_copy(jobs[n][0](c), jobs[n][1](c), here.at[n])
+
+        def out(n, k):
+            return remote(
+                jobs[n][0](beside(c, k)), jobs[n][1](c), small_send, small_receive,
+                3 * n + k - 1, (d, beside(c, k), t),
+            )
+
+        def arrival(n, k):
+            block = beside(c, k)
+            return remote(
+                jobs[n][0](block), jobs[n][1](block), small_send, small_receive,
+                3 * n + k - 1, (d, block, t),
+            )
+
+        def along(k):
+            return remote(
+                wa_out.at[d], wa_out.at[d], deep_send, deep_receive, k - 1, (depth(d, k), c, t)
+            )
+
+        def from_depth(k):
+            there = wa_out.at[depth(d, deep - k)]
+            return remote(there, there, deep_send, deep_receive, k - 1, (depth(d, k), c, t))
+
+        one, two = one_ref[...], two_ref[...]
+        for b in range(4):
+            cut_a[b, :, :wide] = columns(v_ref, one, b * wide, wide).astype(BF16)
+            cut_a[b, :, wide : 2 * wide] = o_ref[:, b * wide : (b + 1) * wide]
+            cut_a[b, :, 2 * wide :] = jnp.concatenate(
+                [columns(ref, one, b * narrow, narrow) for ref in (q_ref, k_ref)], axis=1
+            ).astype(BF16)
+        greet(
+            [(d, beside(c, k), t) for k in (1, 2, 3)]
+            + [(d, c, 1 - t)]
+            + [(depth(d, k), c, t) for k in range(1, deep)]
+        )
+        local(0).start()
+        for k in (3, 1, 2):
+            out(0, k).start()
+        mine = pl.multiple_of((2 * c + t) * own, own)
+        _, hat = norm_parts(x_ref[pl.ds(pl.multiple_of(t * own, own), own), :].astype(F32))
+        rows_ref[pl.ds(mine, own), :] = hat.astype(BF16)
+
+        def early():
+            for b in range(4):
+                start = b * units
+                cut_g[b, :, :main] = columns(g_ref, two, start, main).astype(BF16)
+                cut_g[b, :, main : 2 * main] = columns(u_ref, two, start, main).astype(BF16)
+                if main < units:
+                    cut_g[b, :, 2 * main :] = jnp.concatenate(
+                        [columns(r, two, start + main, units - main) for r in (g_ref, u_ref)],
+                        axis=1,
+                    ).astype(BF16)
+            local(0).wait()
+            for k in (1, 2, 3):
+                arrival(0, k).wait_recv()
+            for k in range(1, deep):
+                along(k).start()
+            for n in (1, 2):
+                local(n).start()
+                for k in (3, 1, 2):
+                    out(n, k).start()
+
+        gather_rows(rows_ref, send, receive, early=early)
+        for n in (1, 2):
+            local(n).wait()
+            for k in (1, 2, 3):
+                arrival(n, k).wait_recv()
+        for k in range(1, deep):
+            from_depth(k).wait_recv()
+        for n in range(3):
+            for k in (1, 2, 3):
+                out(n, k).wait_send()
+        for k in range(1, deep):
+            along(k).wait_send()
+
+    vmem, hbm = pl.BlockSpec(memory_space=pltpu.VMEM), pl.BlockSpec(memory_space=pl.ANY)
+    return call(
+        kernel,
+        "front",
+        1,
+        (x, seg[None]) + tuple(weights) + tuple(gains),
+        [
+            jax.ShapeDtypeStruct((tokens, width), BF16),
+            jax.ShapeDtypeStruct((4,) + seg.shape, seg.dtype),
+            jax.ShapeDtypeStruct((deep, 4, held, packed), BF16),
+            jax.ShapeDtypeStruct((4, held, 2 * units), BF16),
+        ],
+        [
+            pltpu.VMEM((4, held, packed), BF16),
+            pltpu.VMEM((4, held, 2 * units), BF16),
+        ]
+        + sems(GATHER_COPIES) + sems(9) + sems(deep - 1) + [pltpu.SemaphoreType.DMA((3,))],
+        [vmem, hbm] + [vmem] * 8,
+        [vmem, hbm, hbm, hbm],
+    )
+
+
+def apart(tokens):
+    return (tokens // 2 - 2) // BLOCK + 2
+
+
+def first_seen(i, tokens):
+    return jnp.maximum(i - apart(tokens) + 1, 0)
+
+
+def attend_back(qkv, g_mixed, mixed, denom, seg_rows, seg_cols, branch, heads_out, heads):
+    tokens, width = branch.shape
+    wide, narrow = heads * DV, heads * F
+    blocks = tokens // BLOCK
+    deep = lax.axis_size("dp")
+    group = width // deep
+
+    def kernel(
+        x_ref, gm_ref, m_ref, d_ref, row_ref, col_ref, br_ref, h_ref, g_ref, sum_ref,
+        gq_ref, numer_ref, gden_ref, key_ref, back_ref, came, br_buf, load, send, receive,
+    ):
+        d, c, t = place_of()
+
+        def fetch(n):
+            part = pl.ds(pl.multiple_of(depth(d, n + 1) * group, group), group)
+            slot = lax.rem(n, 2)
+            return pltpu.make_async_copy(br_ref.at[:, part], br_buf.at[slot], load.at[slot])
+
+        def deeper(n):
+            return remote(
+                back_ref.at[n], came.at[n], send, receive, n, (depth(d, n + 1), c, t)
+            )
+
+        fetch(0).start()
+        greet([(depth(d, k), c, t) for k in range(1, deep)])
+
+        def plane(n, carry):
+            @pl.when(n < deep - 1)
+            def _():
+                fetch(n + 1).start()
+
+            fetch(n).wait()
+            back_ref[n] = dot(br_buf[lax.rem(n, 2)], h_ref[...], 0, 0).astype(BF16)
+
+            @pl.when(n < deep - 1)
+            def _():
+                deeper(n).start()
+
+            return carry
+
+        lax.fori_loop(0, deep, plane, 0)
+
+        gq_ref[...] = jnp.zeros_like(gq_ref)
+        for h in range(heads):
+            part = pl.ds(h * DV, DV)
+            gm = gm_ref[:, part].astype(F32)
+            inverse = 1.0 / d_ref[:, h : h + 1]
+            numer_ref[:, part] = (gm * inverse).astype(BF16)
+            down = -jnp.sum(gm * m_ref[:, part], axis=1, keepdims=True) * inverse
+            gden_ref[h : h + 1, :] = jnp.transpose(jnp.broadcast_to(down, (tokens, 128)), (1, 0))[:1]
+        key_ref[...] = jnp.transpose(x_ref[:, wide : wide + 2 * narrow].astype(F32), (1, 0)).astype(
+            BF16
+        )
+        place = lax.broadcasted_iota(jnp.int32, (BLOCK, BLOCK), 1) - lax.broadcasted_iota(
+            jnp.int32, (BLOCK, BLOCK), 0
+        )
+        tempered = BF16(F**-0.5)
+
+        @pl.loop(0, blocks)
+        def _(j):
+            start = pl.multiple_of(j * BLOCK, BLOCK)
+            own = row_ref[pl.ds(start, BLOCK), :]
+            values = [x_ref[pl.ds(start, BLOCK), h * DV : (h + 1) * DV] for h in range(heads)]
+            keys = [
+                x_ref[pl.ds(start, BLOCK), wide + (heads + h) * F : wide + (heads + h + 1) * F]
+                * tempered
+                for h in range(heads)
+            ]
+            across = [
+                key_ref[(heads + h) * F : (heads + h + 1) * F, pl.ds(start, BLOCK)] * tempered
+                for h in range(heads)
+            ]
+
+            def step(i, sums):
+                base = pl.multiple_of(i * BLOCK, BLOCK)
+                visible = (place >= start - base) & (own == col_ref[:, pl.ds(base, BLOCK)])
+                out = []
+                for h in range(heads):
+                    queries = x_ref[pl.ds(base, BLOCK), wide + h * F : wide + (h + 1) * F]
+                    numer = numer_ref[pl.ds(base, BLOCK), h * DV : (h + 1) * DV]
+                    s = dot(keys[h], queries, 1, 1)
+                    a = jnp.where(visible, (0.5 * s + 1.0) * s + 1.0, 0.0).astype(BF16)
+                    ga = dot(values[h], numer, 1, 1) + gden_ref[h : h + 1, pl.ds(base, BLOCK)]
+                    gs = jnp.where(visible, ga * (1.0 + s), 0.0).astype(BF16)
+                    gq_ref[h * F : (h + 1) * F, pl.ds(base, BLOCK)] += dot(across[h], gs, 1, 0)
+                    out += [sums[2 * h] + dot(a, numer, 1, 0), sums[2 * h + 1] + dot(gs, queries, 1, 0)]
+                return tuple(out)
+
+            zeros = []
+            for h in range(heads):
+                zeros += [jnp.zeros((BLOCK, DV), F32), jnp.zeros((BLOCK, F), F32)]
+            sums = lax.fori_loop(
+                j, jnp.minimum(j + apart(tokens), blocks), step, tuple(zeros)
+            )
+            for h in range(heads):
+                g_ref[pl.ds(start, BLOCK), h * DV : (h + 1) * DV] = sums[2 * h].astype(BF16)
+                g_ref[
+                    pl.ds(start, BLOCK), wide + (heads + h) * F : wide + (heads + h + 1) * F
+                ] = (sums[2 * h + 1] * F**-0.5).astype(BF16)
+
+        g_ref[:, wide : wide + narrow] = jnp.transpose(gq_ref[...], (1, 0)).astype(BF16)
+        total = back_ref[deep - 1].astype(F32)
+        for n in range(deep - 1):
+            deeper(n).wait_recv()
+            total = total + came[n].astype(F32)
+        sum_ref[...] = total.astype(BF16)
+        for n in range(deep - 1):
+            deeper(n).wait_send()
+
+    vmem, hbm = pl.BlockSpec(memory_space=pltpu.VMEM), pl.BlockSpec(memory_space=pl.ANY)
+    return call(
+        kernel, "attend_back", 7,
+        (qkv, g_mixed, mixed, denom, seg_rows, seg_cols, branch, heads_out),
+        [jax.ShapeDtypeStruct(qkv.shape, BF16), jax.ShapeDtypeStruct((group, wide), BF16)],
+        [
+            pltpu.VMEM((narrow, tokens), F32),
+            pltpu.VMEM((tokens, wide), BF16),
+            pltpu.VMEM((8, tokens), F32),
+            pltpu.VMEM((2 * narrow, tokens), BF16),
+            pltpu.VMEM((deep, group, wide), BF16),
+            pltpu.VMEM((deep - 1, group, wide), BF16),
+            pltpu.VMEM((2, tokens, group), BF16),
+            pltpu.SemaphoreType.DMA((2,)),
+        ]
+        + sems(deep - 1),
+        [vmem] * 6 + [hbm, vmem],
+    )
+
+
+def attend_block(i, x_ref, ext_ref, row_ref, col_ref, mixed_ref, denom_ref, low_ref, heads):
+    wide = heads * DV
+    base = pl.multiple_of(i * BLOCK, BLOCK)
+    own = row_ref[pl.ds(base, BLOCK), :]
+    place = lax.broadcasted_iota(jnp.int32, (BLOCK, BLOCK), 0) - lax.broadcasted_iota(
+        jnp.int32, (BLOCK, BLOCK), 1
+    )
+    queries = [
+        x_ref[pl.ds(base, BLOCK), wide + h * F : wide + (h + 1) * F] * jnp.bfloat16(F**-0.5)
+        for h in range(heads)
+    ]
+
+    def step(j, sums):
+        start = pl.multiple_of(j * BLOCK, BLOCK)
+        visible = (place >= start - base) & (own == col_ref[:, pl.ds(start, BLOCK)])
+        out = []
+        for h in range(heads):
+            keys = x_ref[
+                pl.ds(start, BLOCK), wide + (heads + h) * F : wide + (heads + h + 1) * F
+            ]
+            s = dot(queries[h], keys, 1, 1)
+            a = jnp.where(visible, (0.5 * s + 1.0) * s + 1.0, 0.0).astype(BF16)
+            out.append(
+                sums[h] + dot(a, ext_ref[pl.ds(start, BLOCK), 2 * h * DV : (2 * h + 2) * DV], 1, 0)
+            )
+        return tuple(out)
+
+    sums = lax.fori_loop(
+        first_seen(i, x_ref.shape[0]),
+        i + 1,
+        step,
+        tuple(jnp.zeros((BLOCK, 2 * DV), F32) for _ in range(heads)),
+    )
+    for h in range(heads):
+        denom = sums[h][:, DV:]
+        mixed = sums[h][:, :DV] / denom
+        mixed_ref[pl.ds(base, BLOCK), h * DV : (h + 1) * DV] = mixed
+        low_ref[pl.ds(base, BLOCK), h * DV : (h + 1) * DV] = mixed.astype(BF16)
+        denom_ref[pl.ds(base, BLOCK), h : h + 1] = denom[:, :1]
+
+
+def attend(rows_one, w_attn, seg_rows, seg_cols, cot, w_down, heads):
+    tokens, width = rows_one.shape
+    own = tokens // 8
+    wide, narrow = heads * DV, heads * F
+    held, units = w_down.shape[0], w_down.shape[1] // 4
+    filled = whole_tiles(units)
+
+    def kernel(
+        x_ref, w_ref, row_ref, col_ref, cot_ref, d_ref,
+        qkv_ref, mixed_ref, denom_ref, low_ref, rows_ref, wd_out,
+        ext_ref, cut, send, receive, d_send, d_receive, here,
+    ):
+        d, c, t = place_of()
+
+        def out(k):
+            return remote(
+                cut.at[beside(c, k)], wd_out.at[c], d_send, d_receive, k - 1, (d, beside(c, k), t)
+            )
+
+        def arrival(k):
+            there = wd_out.at[beside(c, k)]
+            return remote(there, there, d_send, d_receive, k - 1, (d, beside(c, k), t))
+
+        local = pltpu.make_async_copy(cut.at[c], wd_out.at[c], here.at[0])
+        for b in range(4):
+            part = columns(d_ref, None, b * units, units)
+            if units < filled:
+                part = jnp.concatenate([part, jnp.zeros((held, filled - units), F32)], axis=1)
+            cut[b] = part.astype(BF16)
+        greet([(d, beside(c, k), t) for k in (1, 2, 3)] + [(d, c, 1 - t)])
+        mine = pl.multiple_of((2 * c + t) * own, own)
+        rows_ref[pl.ds(mine, own), :] = cot_ref[
+            pl.ds(pl.multiple_of(t * own, own), own), : width // 2
+        ]
+
+        def blocks(first, last):
+            @pl.loop(first, last)
+            def _(i):
+                attend_block(
+                    i, qkv_ref, ext_ref, row_ref, col_ref, mixed_ref, denom_ref, low_ref, heads
+                )
+
+        def early():
+            local.start()
+            for k in (3, 1, 2):
+                out(k).start()
+
+            @pl.loop(0, tokens // BLOCK)
+            def _(n):
+                rows = pl.ds(pl.multiple_of(n * BLOCK, BLOCK), BLOCK)
+                values = dot(x_ref[rows, :], w_ref[:, :wide], 1, 0).astype(BF16)
+                qkv_ref[rows, :wide] = values
+                qkv_ref[rows, wide:] = dot(x_ref[rows, :], w_ref[:, 2 * wide :], 1, 0).astype(BF16)
+                for h in range(heads):
+                    ext_ref[rows, 2 * h * DV : (2 * h + 1) * DV] = values[:, h * DV : (h + 1) * DV]
+                    ext_ref[rows, (2 * h + 1) * DV : (2 * h + 2) * DV] = jnp.ones((BLOCK, DV), BF16)
+
+        gather_rows(
+            rows_ref, send, receive, early=early,
+            middle=lambda: blocks(0, tokens // BLOCK // 2),
+            late=lambda: blocks(tokens // BLOCK // 2, tokens // BLOCK),
+        )
+        local.wait()
+        for k in (1, 2, 3):
+            arrival(k).wait_recv()
+            out(k).wait_send()
+
+    vmem, hbm = pl.BlockSpec(memory_space=pltpu.VMEM), pl.BlockSpec(memory_space=pl.ANY)
+    return call(
+        kernel, "attend", 2, (rows_one, w_attn, seg_rows, seg_cols, cot, w_down),
+        [
+            jax.ShapeDtypeStruct((tokens, wide + 2 * narrow), BF16),
+            jax.ShapeDtypeStruct((tokens, wide), F32),
+            jax.ShapeDtypeStruct((tokens, heads), F32),
+            jax.ShapeDtypeStruct((tokens, wide), BF16),
+            jax.ShapeDtypeStruct((tokens, width // 2), BF16),
+            jax.ShapeDtypeStruct((4, held, filled), BF16),
+        ],
+        [pltpu.VMEM((tokens, 2 * wide), BF16), pltpu.VMEM((4, held, filled), BF16)]
+        + sems(GATHER_COPIES) + sems(3) + [pltpu.SemaphoreType.DMA((1,))],
+        None,
+        [vmem] * 5 + [hbm],
+    )
+
+
+def to_middle(heads_out, w_attn, x):
+    tokens, width = heads_out.shape[0], x.shape[1]
+    own = tokens // 8
+    wide = heads_out.shape[1]
+
+    def kernel(h_ref, w_ref, x_ref, mid_ref, rows_ref, *rest):
+        bufs, (s_send, s_receive, g_send, g_receive) = rest[:6], rest[6:]
+        d, c, t = place_of()
+        greet([(d, beside(c, 1), t), (d, beside(c, 2), t), (d, c, 1 - t)])
+
+        def terms(i, start):
+            return [(h_ref[pl.ds(start, 2 * own), :], w_ref, slice(wide, 2 * wide))]
+
+        total = scatter_rows(terms, bufs, s_send, s_receive)
+        middle = total + x_ref[pl.ds(pl.multiple_of(t * own, own), own), :].astype(F32)
+        mid_ref[...] = middle
+        _, hat = norm_parts(middle)
+        rows_ref[pl.ds(pl.multiple_of((2 * c + t) * own, own), own), :] = hat.astype(BF16)
+        gather_rows(rows_ref, g_send, g_receive)
+
+    return call(
+        kernel, "to_middle", 3, (heads_out, w_attn, x),
+        [jax.ShapeDtypeStruct((own, width), F32), jax.ShapeDtypeStruct((tokens, width), BF16)],
+        scatter_scratch(own, width) + sems(SCATTER_COPIES) + sems(GATHER_COPIES),
+        flops=2 * tokens * width * heads_out.shape[1],
+    )
+
+
+def gate_up(rows_two, w_both, cot):
+    tokens, width = rows_two.shape
+    own = tokens // 8
+    units = w_both.shape[1] // 2
+    main = units // 128 * 128
+    count = tokens // BLOCK
+
+    def kernel(
+        x_ref, w_ref, cot_ref, hid_out, slope_out, silu_out, rows_ref,
+        x_buf, w_buf, hid_ref, slope_ref, silu_ref, load, store, send, receive,
+    ):
+        d, c, t = place_of()
+
+        def fetch(i):
+            rows = pl.ds(pl.multiple_of(i * BLOCK, BLOCK), BLOCK)
+            slot = lax.rem(i, 2)
+            return pltpu.make_async_copy(x_ref.at[rows], x_buf.at[slot], load.at[slot])
+
+        def given(i):
+            rows = pl.ds(pl.multiple_of(i * BLOCK, BLOCK), BLOCK)
+            slot = lax.rem(i, 2)
+            return [
+                pltpu.make_async_copy(source.at[slot], target.at[rows], store.at[n, slot])
+                for n, (source, target) in enumerate(
+                    ((hid_ref, hid_out), (slope_ref, slope_out), (silu_ref, silu_out))
+                )
+            ]
+
+        weights = pltpu.make_async_copy(w_ref, w_buf, load.at[2])
+        weights.start()
+        fetch(0).start()
+        greet([(d, beside(c, 1), t), (d, beside(c, 2), t), (d, c, 1 - t)])
+        mine = pl.multiple_of((2 * c + t) * own, own)
+        rows_ref[pl.ds(mine, own), :] = cot_ref[
+            pl.ds(pl.multiple_of(t * own, own), own), width // 2 :
+        ]
+
+        def blocks(first, last):
+            @pl.loop(first, last)
+            def _(i):
+                slot = lax.rem(i, 2)
+
+                @pl.when(i + 1 < count)
+                def _():
+                    fetch(i + 1).start()
+
+                fetch(i).wait()
+                both = dot(x_buf[slot], w_buf[...], 1, 0)
+
+                @pl.when(i >= 2)
+                def _():
+                    for copy in given(i - 2):
+                        copy.wait()
+
+                def act(gate, up, part):
+                    sig = jax.nn.sigmoid(gate)
+                    silu = gate * sig
+                    hid_ref[slot, :, part] = (silu * up).astype(BF16)
+                    slope_ref[slot, :, part] = (up * sig * (1.0 + gate * (1.0 - sig))).astype(BF16)
+                    silu_ref[slot, :, part] = silu.astype(BF16)
+
+                act(both[:, :main], both[:, main : 2 * main], slice(0, main))
+                if main < units:
+                    act(
+                        both[:, 2 * main : main + units],
+                        both[:, main + units :],
+                        slice(main, units),
+                    )
+                for copy in given(i):
+                    copy.start()
+
+        def early():
+            weights.wait()
+            blocks(0, 1)
+
+        gather_rows(
+            rows_ref, send, receive, early=early,
+            middle=lambda: blocks(1, count // 2), late=lambda: blocks(count // 2, count),
+        )
+        for i in (count - 2, count - 1):
+            for copy in given(i):
+                copy.wait()
+
+    vmem, hbm = pl.BlockSpec(memory_space=pltpu.VMEM), pl.BlockSpec(memory_space=pl.ANY)
+    return call(
+        kernel, "gate_up", 8, (rows_two, w_both, cot),
+        [jax.ShapeDtypeStruct((tokens, units), BF16)] * 3
+        + [jax.ShapeDtypeStruct((tokens, width // 2), BF16)],
+        [
+            pltpu.VMEM((2, BLOCK, width), BF16),
+            pltpu.VMEM(w_both.shape, BF16),
+            pltpu.VMEM((2, BLOCK, units), BF16),
+            pltpu.VMEM((2, BLOCK, units), BF16),
+            pltpu.VMEM((2, BLOCK, units), BF16),
+            pltpu.SemaphoreType.DMA((3,)),
+            pltpu.SemaphoreType.DMA((3, 2)),
+        ]
+        + sems(GATHER_COPIES),
+        [hbm, hbm, vmem],
+        [hbm, hbm, hbm, vmem],
+        flops=4 * tokens * width * units,
+    )
+
+
+def feed_forward(hidden, slope, silu, cot_low, cot_high, middle, w_down, rows_two):
+    tokens, width = rows_two.shape
+    own = tokens // 8
+    units = hidden.shape[1]
+    main = units // 128 * 128
+    tile = 256
+    part_width = width // 2
+
+    def kernel(
+        hid_ref, slope_ref, silu_ref, low_ref, high_ref, mid_ref, d_ref, two_ref,
+        g_out, out_ref, grad_ref,
+        hid_buf, slope_buf, silu_buf, low_buf, high_buf, d_buf, g_ref, here, g_store,
+        cols, out, load, store, *rest,
+    ):
+        bufs, (s_send, s_receive, t_send, t_receive) = rest[:6], rest[6:]
+        d, c, t = place_of()
+
+        def block_rows(i):
+            across = 3 - i
+            x, y = lax.rem(c, 2), lax.div(c, 2)
+            block = lax.rem(x + lax.rem(across, 2), 2) + 2 * lax.rem(y + lax.div(across, 2), 2)
+            return pl.ds(pl.multiple_of(2 * block * own, 2 * own), 2 * own)
+
+        def fetch(i):
+            part = block_rows(i)
+            return [
+                pltpu.make_async_copy(source.at[part], target, here.at[n])
+                for n, (source, target) in enumerate(
+                    (
+                        (low_ref, low_buf),
+                        (high_ref, high_buf),
+                        (slope_ref, slope_buf),
+                        (silu_ref, silu_buf),
+                    )
+                )
+            ]
+
+        def fetch_hidden(i):
+            return pltpu.make_async_copy(hid_ref.at[block_rows(i)], hid_buf, here.at[4])
+
+        def g_given(i):
+            part = block_rows(i)
+            return pltpu.make_async_copy(g_ref.at[part], g_out.at[part], g_store.at[i])
+
+        weights = pltpu.make_async_copy(d_ref, d_buf, here.at[5])
+        weights.start()
+        for copy in fetch(0):
+            copy.start()
+
+        def wanted(n):
+            part = pl.ds(pl.multiple_of(n * tile, tile), tile)
+            slot = lax.rem(n, 2)
+            return pltpu.make_async_copy(two_ref.at[:, part], cols.at[slot], load.at[slot])
+
+        def given(n):
+            part = pl.ds(pl.multiple_of(n * tile, tile), tile)
+            slot = lax.rem(n, 2)
+            return pltpu.make_async_copy(out.at[slot], grad_ref.at[part], store.at[slot])
+
+        last = width // tile
+
+        def tiles(first, end):
+            @pl.loop(first, end)
+            def _(n):
+                wanted(n).wait()
+
+                @pl.when(n + 1 < last)
+                def _():
+                    wanted(n + 1).start()
+
+                @pl.when(n >= 2)
+                def _():
+                    given(n - 2).wait()
+
+                slot = lax.rem(n, 2)
+                out[slot] = dot(cols[slot], g_ref[...], 0, 0).astype(BF16)
+                given(n).start()
+
+        wanted(0).start()
+        greet([(d, beside(c, 1), t), (d, beside(c, 2), t), (d, c, 1 - t)])
+        weights.wait()
+
+        def terms(i, start):
+            part = pl.ds(start, 2 * own)
+            fetch_hidden(i).start()
+            for copy in fetch(i):
+                copy.wait()
+            g_hidden = dot(low_buf[...], d_buf[:part_width, :units], 1, 0) + dot(
+                high_buf[...], d_buf[part_width:, :units], 1, 0
+            )
+            gg = g_hidden * slope_buf[...].astype(F32)
+            gu = g_hidden * silu_buf[...].astype(F32)
+            g_ref[part, :main] = gg[:, :main].astype(BF16)
+            g_ref[part, main : 2 * main] = gu[:, :main].astype(BF16)
+            if main < units:
+                g_ref[part, 2 * main :] = jnp.concatenate(
+                    [gg[:, main:], gu[:, main:]], axis=1
+                ).astype(BF16)
+            g_given(i).start()
+
+            @pl.when(i < 3)
+            def _():
+                for copy in fetch(i + 1):
+                    copy.start()
+
+            fetch_hidden(i).wait()
+            return [(hid_buf[...], d_buf, slice(0, units))]
+
+        def fill(n):
+            if n == 0:
+                tiles(0, 2)
+            else:
+                tiles(2, last)
+
+        total = scatter_rows(terms, bufs, s_send, s_receive, fill)
+        place = out_ref.at[pl.ds(pl.multiple_of(t * own, own), own)]
+        place[...] = (mid_ref[...] + total).astype(BF16)
+        copy = remote(place, place, t_send, t_receive, 0, (d, c, 1 - t))
+        copy.start()
+        copy.wait_send()
+        there = out_ref.at[pl.ds(pl.multiple_of((1 - t) * own, own), own)]
+        remote(there, there, t_send, t_receive, 0, (d, c, 1 - t)).wait_recv()
+        given(last - 2).wait()
+        given(last - 1).wait()
+        for i in range(4):
+            g_given(i).wait()
+
+    vmem, hbm = pl.BlockSpec(memory_space=pltpu.VMEM), pl.BlockSpec(memory_space=pl.ANY)
+    return call(
+        kernel, "feed_forward", 4,
+        (hidden, slope, silu, cot_low, cot_high, middle, w_down, rows_two),
+        [
+            jax.ShapeDtypeStruct((tokens, 2 * units), BF16),
+            jax.ShapeDtypeStruct((2 * own, width), BF16),
+            jax.ShapeDtypeStruct((width, 2 * units), BF16),
+        ],
+        [
+            pltpu.VMEM((2 * own, units), BF16),
+            pltpu.VMEM((2 * own, units), BF16),
+            pltpu.VMEM((2 * own, units), BF16),
+            pltpu.VMEM((2 * own, part_width), BF16),
+            pltpu.VMEM((2 * own, part_width), BF16),
+            pltpu.VMEM(w_down.shape, BF16),
+            pltpu.VMEM((tokens, 2 * units), BF16),
+            pltpu.SemaphoreType.DMA((6,)),
+            pltpu.SemaphoreType.DMA((4,)),
+            pltpu.VMEM((2, tokens, tile), BF16),
+            pltpu.VMEM((2, tile, 2 * units), BF16),
+            pltpu.SemaphoreType.DMA((2,)),
+            pltpu.SemaphoreType.DMA((2,)),
+        ]
+        + scatter_scratch(own, width) + sems(SCATTER_COPIES) + sems(1),
+        [hbm] * 5 + [vmem, hbm, hbm],
+        [hbm, vmem, hbm],
+        flops=8 * tokens * width * units,
+    )
+
+
+def to_branch(g_both, w_both, middle, cot, w_attn, wide):
+    tokens, width = g_both.shape[0], middle.shape[1]
+    own = tokens // 8
+
+    def kernel(
+        g_ref, w_ref, mid_ref, cot_ref, o_ref, gm_ref, rows_ref, mix_ref, g_buf, w_buf, load, *rest
+    ):
+        bufs, (s_send, s_receive, g_send, g_receive) = rest[:6], rest[6:]
+        d, c, t = place_of()
+
+        def fetch(i):
+            across = 3 - i
+            x, y = lax.rem(c, 2), lax.div(c, 2)
+            block = lax.rem(x + lax.rem(across, 2), 2) + 2 * lax.rem(y + lax.div(across, 2), 2)
+            part = pl.ds(pl.multiple_of(2 * block * own, 2 * own), 2 * own)
+            slot = lax.rem(i, 2)
+            return pltpu.make_async_copy(g_ref.at[part], g_buf.at[slot], load.at[slot])
+
+        weights = pltpu.make_async_copy(w_ref, w_buf, load.at[2])
+        weights.start()
+        fetch(0).start()
+        greet([(d, beside(c, 1), t), (d, beside(c, 2), t), (d, c, 1 - t)])
+        weights.wait()
+
+        def terms(i, start):
+            fetch(i).wait()
+
+            @pl.when(i < 3)
+            def _():
+                fetch(i + 1).start()
+
+            return [(g_buf[lax.rem(i, 2)], w_buf, slice(None))]
+
+        total = scatter_rows(terms, bufs, s_send, s_receive)
+        scale, hat = norm_parts(mid_ref[...])
+        g_middle = cot_ref[pl.ds(pl.multiple_of(t * own, own), own), :].astype(F32) + norm_back(
+            total, hat, scale
+        )
+        gm_ref[...] = g_middle
+        rows_ref[pl.ds(pl.multiple_of((2 * c + t) * own, own), own), :] = g_middle.astype(BF16)
+
+        def mix(start):
+            mix_ref[pl.ds(start, own), :] = dot(
+                rows_ref[pl.ds(start, own), :], o_ref[:, wide : 2 * wide], 1, 0
+            ).astype(BF16)
+
+        gather_rows(rows_ref, g_send, g_receive, mix)
+
+    return call(
+        kernel, "to_branch", 5, (g_both, w_both, middle, cot, w_attn),
+        [
+            jax.ShapeDtypeStruct((own, width), F32),
+            jax.ShapeDtypeStruct((tokens, width), BF16),
+            jax.ShapeDtypeStruct((tokens, wide), BF16),
+        ],
+        [
+            pltpu.VMEM((2, 2 * own, g_both.shape[1]), BF16),
+            pltpu.VMEM(w_both.shape, BF16),
+            pltpu.SemaphoreType.DMA((3,)),
+        ]
+        + scatter_scratch(own, width) + sems(SCATTER_COPIES) + sems(GATHER_COPIES),
+        [pl.BlockSpec(memory_space=pl.ANY)] * 2 + [pl.BlockSpec(memory_space=pltpu.VMEM)] * 3,
+        flops=4 * tokens * width * (g_both.shape[1] // 2 + wide),
+    )
+
+
+def as_row(column):
+    return jnp.transpose(jnp.broadcast_to(column, (column.shape[0], 128)), (1, 0))[:8]
+
+
+def to_input(
+    g_qkv, w_attn, x, g_middle, rows_one, sum_out, sum_both, sum_down, weights, gains, heads
+):
+    tokens, width = g_qkv.shape[0], x.shape[1]
+    own = tokens // 8
+    deep = lax.axis_size("dp")
+    across = g_qkv.shape[1]
+    group = width // deep
+    held = group // 4
+    wide, narrow = heads * DV, heads * F
+    both, units = sum_both.shape[1], sum_down.shape[1]
+    main = units // 128 * 128
+
+    def kernel(
+        g_ref, w_ref, x_ref, gm_ref, one_ref, so_ref, both_ref, down_ref,
+        wq_ref, wk_ref, wv_ref, wg_ref, wu_ref, gain_ref, gain_two_ref,
+        out_ref, gq_ref, gk_ref, gv_ref, go_ref, gg_ref, gu_ref, gd_ref, row_ref, row_two_ref,
+        *rest,
+    ):
+        bufs, (s_send, s_receive, t_send, t_receive) = rest[:6], rest[6:10]
+        (
+            came_deep, sums, parts_a, parts_b, parts_d, parts_o, scalar, back_ref, one_buf, load,
+            d_send, d_receive, p_send, p_receive,
+        ) = rest[10:]
+        d, c, t = place_of()
+
+        def fetch(n):
+            part = pl.ds(pl.multiple_of(depth(d, n + 1) * group, group), group)
+            slot = lax.rem(n, 2)
+            return pltpu.make_async_copy(one_ref.at[:, part], one_buf.at[slot], load.at[slot])
+
+        fetch(0).start()
+        greet(
+            [(d, beside(c, k), t) for k in (1, 2, 3)]
+            + [(d, c, 1 - t)]
+            + [(depth(d, k), c, t) for k in range(1, deep)]
+        )
+
+        def deeper(k):
+            rows = pl.ds(pl.multiple_of(depth(d, k) * group, group), group)
+            return remote(
+                back_ref.at[rows], came_deep.at[k - 1], d_send, d_receive, k - 1,
+                (depth(d, k), c, t),
+            )
+
+        jobs = ((sums, parts_a), (both_ref, parts_b), (down_ref, parts_d), (so_ref, parts_o))
+
+        def rows_of(block):
+            return pl.ds(pl.multiple_of(block * held, held), held)
+
+        def to_block(n, k):
+            source, target = jobs[n]
+            return remote(
+                source.at[rows_of(beside(c, k))], target.at[c], p_send, p_receive, 3 * n + k - 1,
+                (d, beside(c, k), t),
+            )
+
+        def from_block(n, k):
+            there = jobs[n][1].at[beside(c, k)]
+            return remote(there, there, p_send, p_receive, 3 * n + k - 1, (d, beside(c, k), t))
+
+        def at_home(n):
+            source, target = jobs[n]
+            return pltpu.make_async_copy(source.at[rows_of(c)], target.at[c], load.at[n + 1])
+
+        def plane(n, carry):
+            rows = pl.ds(pl.multiple_of(depth(d, n + 1) * group, group), group)
+
+            @pl.when(n < deep - 1)
+            def _():
+                fetch(n + 1).start()
+
+            fetch(n).wait()
+            back_ref[rows, :] = dot(one_buf[lax.rem(n, 2)], g_ref[...], 0, 0).astype(BF16)
+
+            @pl.when(n < deep - 1)
+            def _():
+                remote(
+                    back_ref.at[rows], came_deep.at[n], d_send, d_receive, n,
+                    (depth(d, n + 1), c, t),
+                ).start()
+
+            return carry
+
+        lax.fori_loop(0, deep, plane, 0)
+
+        def terms(i, start):
+            part = pl.ds(start, 2 * own)
+            return [
+                (g_ref[part, :wide], w_ref, slice(0, wide)),
+                (g_ref[part, wide:], w_ref, slice(2 * wide, None)),
+            ]
+
+        def fill(n):
+            if n == 0:
+                for job in (1, 2, 3):
+                    for k in (3, 1, 2):
+                        to_block(job, k).start()
+                    at_home(job).start()
+
+        e_one = scatter_rows(terms, bufs, s_send, s_receive, fill)
+        scale, hat = norm_parts(x_ref[pl.ds(pl.multiple_of(t * own, own), own), :].astype(F32))
+        place = out_ref.at[pl.ds(pl.multiple_of(t * own, own), own)]
+        place[...] = gm_ref[...] + norm_back(e_one, hat, scale)
+        copy = remote(place, place, t_send, t_receive, 0, (d, c, 1 - t))
+        copy.start()
+
+        for n in (1, 2, 3):
+            at_home(n).wait()
+            for k in (1, 2, 3):
+                from_block(n, k).wait_recv()
+        gain_two = gain_two_ref[...]
+        for b in range(4):
+            whole = parts_b[b].astype(F32)
+            for ref, first, rest_of in (
+                (gg_ref, 0, 2 * main),
+                (gu_ref, main, main + units),
+            ):
+                s = whole[:, first : first + main]
+                if main < units:
+                    s = jnp.concatenate([s, whole[:, rest_of : rest_of + units - main]], axis=1)
+                ref[:, b * units : (b + 1) * units] = s * gain_two
+            gd_ref[:, b * units : (b + 1) * units] = parts_d[b].astype(F32)
+            go_ref[:, b * wide : (b + 1) * wide] = parts_o[b].astype(F32)
+        term_two = (
+            jnp.sum(gg_ref[...] * wg_ref[...].astype(F32), axis=1, keepdims=True)
+            + jnp.sum(gu_ref[...] * wu_ref[...].astype(F32), axis=1, keepdims=True)
+        ) / gain_two
+
+        for k in range(1, deep):
+            deeper(k).wait_recv()
+        mine = pl.ds(pl.multiple_of(d * group, group), group)
+        total = back_ref[mine, :].astype(F32)
+        for k in range(1, deep):
+            total = total + came_deep[k - 1].astype(F32)
+        sums[...] = total.astype(BF16)
+        for k in (3, 1, 2):
+            to_block(0, k).start()
+        parts_a[c] = sums[rows_of(c), :]
+        for k in (1, 2, 3):
+            from_block(0, k).wait_recv()
+        gain_one = gain_ref[...]
+
+        def owned(start, count):
+            return jnp.concatenate(
+                [parts_a[b][:, start : start + count].astype(F32) for b in range(4)], axis=1
+            )
+
+        term_one = jnp.zeros((held, 1), F32)
+        for ref, weight, start, count in (
+            (gv_ref, wv_ref, 0, wide),
+            (gq_ref, wq_ref, wide, narrow),
+            (gk_ref, wk_ref, wide + narrow, narrow),
+        ):
+            s = owned(start, count)
+            term_one = term_one + jnp.sum(s * weight[...].astype(F32), axis=1, keepdims=True)
+            ref[...] = s * gain_one
+        scalar[0, 0] = as_row(term_one)
+        scalar[0, 1] = as_row(term_two)
+        swap = remote(scalar.at[0], scalar.at[1], t_send, t_receive, 1, (d, c, 1 - t))
+        swap.start()
+        swap.wait()
+        row_ref[...] = (scalar[0, 0] + scalar[1, 0])[:1]
+        row_two_ref[...] = (scalar[0, 1] + scalar[1, 1])[:1]
+
+        copy.wait_send()
+        there = out_ref.at[pl.ds(pl.multiple_of((1 - t) * own, own), own)]
+        remote(there, there, t_send, t_receive, 0, (d, c, 1 - t)).wait_recv()
+        for k in range(1, deep):
+            deeper(k).wait_send()
+        for n in range(4):
+            for k in (1, 2, 3):
+                to_block(n, k).wait_send()
+
+    w_q, w_k, w_v, w_gate, w_up = weights
+    vmem, hbm = pl.BlockSpec(memory_space=pltpu.VMEM), pl.BlockSpec(memory_space=pl.ANY)
+    return call(
+        kernel, "to_input", 6,
+        (g_qkv, w_attn, x, g_middle, rows_one, sum_out, sum_both, sum_down)
+        + tuple(weights) + tuple(gains),
+        [jax.ShapeDtypeStruct((2 * own, width), F32)]
+        + [jax.ShapeDtypeStruct(w.shape, F32) for w in (w_q, w_k, w_v, w_v, w_gate, w_up, w_up)]
+        + [jax.ShapeDtypeStruct((1, held), F32)] * 2,
+        scatter_scratch(own, width) + sems(SCATTER_COPIES) + sems(2)
+        + [
+            pltpu.VMEM((deep - 1, group, across), BF16),
+            pltpu.VMEM((group, across), BF16),
+            pltpu.VMEM((4, held, across), BF16),
+            pltpu.VMEM((4, held, both), BF16),
+            pltpu.VMEM((4, held, units), BF16),
+            pltpu.VMEM((4, held, wide), BF16),
+            pltpu.VMEM((2, 2, 8, held), F32),
+            pltpu.VMEM((width, across), BF16),
+            pltpu.VMEM((2, tokens, group), BF16),
+            pltpu.SemaphoreType.DMA((5,)),
+        ]
+        + sems(deep - 1) + sems(12),
+        [vmem] * 4 + [hbm] * 4 + [vmem] * 7,
+        flops=2 * tokens * width * g_qkv.shape[1],
+    )
+
+
+def plane_shards(
+    activations,
+    seg_ids,
+    cotangent,
+    q_weight,
+    k_weight,
+    v_weight,
+    o_weight,
+    gate_weight,
+    up_weight,
+    down_weight,
+    attn_gain,
+    mlp_gain,
+):
+    parts = lax.axis_size("ctx")
+    heads = q_weight.shape[1] // F // parts
+    tokens = activations.shape[1] * parts
+    x, cot_block = activations[0], cotangent[0]
+    gain_one = attn_gain.astype(F32)[:, None]
+    gain_two = mlp_gain.astype(F32)[:, None]
+    rows_one, segments, w_attn, cut_both = front(
+        x,
+        seg_ids,
+        (q_weight, k_weight, v_weight, o_weight, gate_weight, up_weight),
+        (gain_one, gain_two),
+        tokens,
+        heads,
+    )
+    w_attn = w_attn.reshape(-1, w_attn.shape[3])
+    w_both = lax.all_gather(cut_both, "dp", axis=0, tiled=True).reshape(-1, cut_both.shape[2])
+    seg_rows, seg_cols = segments.reshape(tokens, 1), segments.reshape(1, tokens)
+    qkv, mixed, denom, heads_out, cot_low, cut_down = attend(
+        rows_one, w_attn, seg_rows, seg_cols, cot_block, down_weight, heads
+    )
+    w_down = lax.all_gather(cut_down, "dp", axis=0, tiled=True).reshape(-1, cut_down.shape[2])
+    middle, rows_two = to_middle(heads_out, w_attn, x)
+    hidden, slope, silu, cot_high = gate_up(rows_two, w_both, cot_block)
+    back_down = jnp.concatenate([dot(cot_low, hidden, 0, 0), dot(cot_high, hidden, 0, 0)]).astype(
+        BF16
+    )
+    w_down, back_down = lax.optimization_barrier((w_down, back_down))
+    sum_down = lax.psum_scatter(back_down, "dp", scatter_dimension=0, tiled=True)
+    g_both, out, back_both = feed_forward(
+        hidden, slope, silu, cot_low, cot_high, middle, w_down, rows_two
+    )
+    sum_both = lax.psum_scatter(back_both, "dp", scatter_dimension=0, tiled=True)
+    g_middle, branch, g_mixed = to_branch(g_both, w_both, middle, cot_block, w_attn, heads * DV)
+    g_qkv, sum_out = attend_back(
+        qkv, g_mixed, mixed, denom, seg_rows, seg_cols, branch, heads_out, heads
+    )
+    g_input, s_q, s_k, s_v, s_o, s_gate, s_up, s_down, attn_row, mlp_row = to_input(
+        g_qkv,
+        w_attn,
+        x,
+        g_middle,
+        rows_one,
+        sum_out,
+        sum_both,
+        sum_down,
+        (q_weight, k_weight, v_weight, gate_weight, up_weight),
+        (gain_one, gain_two),
+        heads,
+    )
+    return (
+        out[None],
+        g_input[None],
+        s_q,
+        s_k,
+        s_v,
+        s_o,
+        s_gate,
+        s_up,
+        s_down,
+        attn_row[0],
+        mlp_row[0],
+    )
+
+
+def layer(*arrays):
+    heads = arrays[3].shape[1] // F
+    plan = shards if heads % lax.axis_size("ctx") else plane_shards
+    return plan(*arrays)
+
+
 def solution(mesh):
     placed = (
         P("dp", "ctx", None),
@@ -332,7 +1634,7 @@
         P(("dp", "ctx")),
     )
     return jax.shard_map(
-        shards,
+        layer,
         mesh=mesh,
         in_specs=placed,
         out_specs=(

time: 2850 us -> 570 us (0.20)
  waiting for transfers between devices: 2270 us -> 0.13 us
  Pallas kernels: 0 us -> 515 us
  blocking collectives: 271 us -> 0 us
  matrix products: 199 us -> 13.8 us
  other arithmetic: 44.8 us -> 3.29 us
    reduce_scatter x7 -> x2, waiting for transfers between devices: 1830 us -> 0.04 us  [the longest x1 0.02 us: plane_shards(): lax.psum_scatter(back_down, 'dp', scatter_dimension=0, tiled=True)]
    pallas_call x0 -> x8, Pallas kernels: none -> 515 us  [call(): pl.pallas_call(kernel, in_specs=spaces or [vmem] * len(arrays), out_specs...]
    all_gather x7 -> x2, waiting for transfers between devices: 423 us -> 0.02 us  [the longest x1 0.02 us: plane_shards(): lax.all_gather(cut_both, 'dp', axis=0, tiled=True)]
    dot_general x34 -> x2, matrix products: 199 us -> 13.8 us  [dot(): lax.dot_general(a, b, (((ca,), (cb,)), ((), ())), preferred_element_type=...]
    all_gather x6 -> x0, blocking collectives: 180 us -> none  [the longest x1 42.4 us: shards(): lax.all_gather(attn_gain, ('dp', 'ctx'), axis=0, tiled=True)]
    unnamed x2 -> x0, blocking collectives: 90.2 us -> none
  transfers between devices with their start and end apart: 17 -> 4, of which waited for: 13 -> 0; matrix products, arithmetic and copies ran while one was open for 6% -> 4% of each run, Pallas kernels for 0% -> 61%
where the time goes in v3:
time: 570 us; the launch traced here: 565 us
  Pallas kernels  515 us (90%)
  local copies, waits for them, and re-layouts  18.2 us (3%)
  between operations  14.2 us (2%)
  matrix products  13.8 us (2%)
    pallas_call x8, Pallas kernels, call(): pl.pallas_call(kernel, in_specs=spaces or [vmem] * len(arrays), out_specs...  515 us
    dot_general x2, matrix products, dot(): lax.dot_general(a, b, (((ca,), (cb,)), ((), ())), preferred_element_type=...  13.8 us
    unnamed x33, local copies, waits for them, and re-layouts  12.3 us
  transfers between devices with their start and end apart: 4, of which 0 were waited for; matrix products, arithmetic and copies ran while one was open for 4% of the time, Pallas kernels for 61%

profile of v3, /device:TPU:0, one launch (start us, length us, event | category | flops | bytes accessed | tf_op | source)
XLA Modules:
  0.0 564.9 jit_solution(7783656328633490997)
XLA Ops:
  7.2 0.0 all-gather.3.cloned.1.call-start
  7.2 0.7 bitcast_convert_fusion.1
  7.9 0.7 bitcast_convert_fusion
  8.5 0.7 copy.46.two_ref.gain_two_ref
  9.3 0.7 copy.45.one_ref.gain_ref
  10.0 71.8 %front.1 = (bf16[2048,2048]{1,0:T(8,128)(2,1)}, s32[4,1,512]{2,1,0:T(1,128)}, bf16[4,4,128,576]{3,2,1,0:T(8,128)(2,1)}, bf16[4,128,1408]{2,1,0:T(8,128)(2,1)}) custom-call(bf16[512,2048]{1,0:T(8,128)(2,1)} %bitcast.26, s32[1,1,512]{2,1,0:T(1,128)} %bitcast.37, bf16[128,128]{1,0:T(8,128)(2,1)} %wq_ref.1, bf16[128,128]{1,0:T(8,128)(2,1)} %wk_ref.1, ...), custom_call_target="tpu_custom_call" | custom-call | bytes 4131840 | tf_op jit(solution)/shard_map/front/pallas_call | solution.py:556
  81.8 0.0 all-gather.3.cloned.1.call-update
  81.8 0.0 all-gather.5.cloned.1.call-start
  81.9 2.0 copy.47.row_ref
  83.9 40.3 %attend.1 = (bf16[2048,320]{1,0:T(8,128)(2,1)}, f32[2048,256]{1,0:T(8,128)}, f32[2048,2]{1,0:T(8,128)}, bf16[2048,256]{1,0:T(8,128)(2,1)}, bf16[2048,1024]{1,0:T(8,128)(2,1)}, /*index=5*/bf16[4,128,768]{2,1,0:T(8,128)(2,1)}) custom-call(bf16[2048,2048]{1,0:T(8,128)(2,1)} %get-tuple-element.47.x_ref.one_ref, bf16[2048,576]{1,0:T(8,128)(2,1)} %bitcast.22, ...), custom_call_target="tpu_custom_call" | custom-call | bytes 13582336 | tf_op jit(solution)/shard_map/attend/pallas_call | solution.py:556
  124.2 0.0 all-gather.5.cloned.1.call-update
  124.3 0.3 reduce-scatter.5.cloned.1.call-start
  124.5 86.3 %to_middle.1 = (f32[256,2048]{1,0:T(8,128)}, bf16[2048,2048]{1,0:T(8,128)(2,1)}) custom-call(bf16[2048,256]{1,0:T(8,128)(2,1)} %get-tuple-element.50.h_ref, bf16[2048,576]{1,0:T(8,128)(2,1)} %bitcast.23, bf16[512,2048]{1,0:T(8,128)(2,1)} %bitcast.27), custom_call_target="tpu_custom_call" | custom-call | flops 2147483648 | bytes 5505024 | tf_op jit(solution)/shard_map/to_middle/pallas_call | solution.py:556
  210.8 0.0 all-gather.3.cloned.1.call-done
  210.8 30.1 %gate_up.1 = (bf16[2048,704]{1,0:T(8,128)(2,1)}, bf16[2048,704]{1,0:T(8,128)(2,1)}, bf16[2048,704]{1,0:T(8,128)(2,1)}, bf16[2048,1024]{1,0:T(8,128)(2,1)}) custom-call(bf16[2048,2048]{1,0:T(8,128)(2,1)} %get-tuple-element.51.x_ref.two_ref, bf16[2048,1408]{1,0:T(8,128)(2,1)} %bitcast.38, bf16[512,2048]{1,0:T(8,128)(2,1)} %bitcast.31), custom_call_target="tpu_custom_call" | custom-call | flops 11811160064 | bytes 16252928 | tf_op jit(solution)/shard_map/gate_up/pallas_call | solution.py:556
  241.0 6.4 %convolution_convert_fusion = bf16[1024,704]{0,1:T(8,128)(2,1)S(1)} fusion(bf16[2048,1024]{1,0:T(8,128)(2,1)} %get-tuple-element.57.high_ref, bf16[2048,704]{1,0:T(8,128)(2,1)} %get-tuple-element.53.hid_ref), kind=kOutput, calls=%fused_computation.1 | convolution fusion | flops 2953510912 | bytes 8519680 | tf_op jit(solution)/shard_map/dot_general | solution.py:330
  247.4 0.7 copy.49
  248.1 7.5 %convolution_convert_fusion.1 = bf16[1024,704]{0,1:T(8,128)(2,1)} fusion(bf16[2048,1024]{1,0:T(8,128)(2,1)} %get-tuple-element.56.low_ref, bf16[2048,704]{1,0:T(8,128)(2,1)} %get-tuple-element.53.hid_ref), kind=kOutput, calls=%fused_computation.2 | convolution fusion | flops 2953510912 | bytes 8519680 | tf_op jit(solution)/shard_map/dot_general | solution.py:330
  255.5 1.7 copy.48
  257.2 2.0 pad_maximum_fusion
  259.2 0.0 reduce-scatter.5.cloned.1.call-update
  259.2 0.0 reduce-scatter.3.cloned.1.call-start
  259.3 55.3 %feed_forward.1 = (bf16[2048,1408]{1,0:T(8,128)(2,1)}, bf16[512,2048]{1,0:T(8,128)(2,1)}, bf16[2048,1408]{1,0:T(8,128)(2,1)}) custom-call(bf16[2048,704]{1,0:T(8,128)(2,1)} %get-tuple-element.53.hid_ref, bf16[2048,704]{1,0:T(8,128)(2,1)} %get-tuple-element.54.slope_ref, bf16[2048,704]{1,0:T(8,128)(2,1)} %get-tuple-element.55.silu_ref, ...), custom_call_target="tpu_custom_call" | custom-call | flops 23622320128 | bytes 30670848 | tf_op jit(solution)/shard_map/feed_forward/pallas_call | solution.py:556
  314.5 0.0 reduce-scatter.3.cloned.1.call-update
  314.6 94.7 %to_branch.1 = (f32[256,2048]{1,0:T(8,128)}, bf16[2048,2048]{1,0:T(8,128)(2,1)}, bf16[2048,256]{1,0:T(8,128)(2,1)}) custom-call(bf16[2048,1408]{1,0:T(8,128)(2,1)} %get-tuple-element.63.g_ref, bf16[2048,1408]{1,0:T(8,128)(2,1)} %bitcast.39, f32[256,2048]{1,0:T(8,128)} %get-tuple-element.58.mid_ref, bf16[512,2048]{1,0:T(8,128)(2,1)} %bitcast.32, ...), custom_call_target="tpu_custom_call" | custom-call | flops 16106127360 | bytes 18087936 | tf_op jit(solution)/shard_map/to_branch/pallas_call | solution.py:556
  409.3 40.3 %attend_back.1 = (bf16[2048,320]{1,0:T(8,128)(2,1)}, bf16[512,256]{1,0:T(8,128)(2,1)}) custom-call(bf16[2048,320]{1,0:T(8,128)(2,1)} %get-tuple-element.62.x_ref, bf16[2048,256]{1,0:T(8,128)(2,1)} %get-tuple-element.64.gm_ref, f32[2048,256]{1,0:T(8,128)} %get-tuple-element.65.m_ref, f32[2048,2]{1,0:T(8,128)} %get-tuple-element.66.d_ref, ...), custom_call_target="tpu_custom_call" | custom-call | bytes 13926400 | tf_op jit(solution)/shard_map/attend_back/pallas_call | solution.py:556
  449.6 0.0 reduce-scatter.5.cloned.1.call-done.down_ref
  449.7 0.0 reduce-scatter.3.cloned.1.call-done.both_ref
  449.7 0.0 copy-start.1
  449.7 96.2 %to_input.1 = (f32[512,2048]{1,0:T(8,128)}, f32[128,128]{1,0:T(8,128)}, f32[128,128]{1,0:T(8,128)}, f32[128,1024]{1,0:T(8,128)}, f32[128,1024]{1,0:T(8,128)}, /*...) custom-call(bf16[2048,320]{1,0:T(8,128)(2,1)} %get-tuple-element.68.g, ...), custom_call_target="tpu_custom_call" | custom-call | flops 2684354560 | bytes 20448256 | tf_op jit(solution)/shard_map/to_input/pallas_call | solution.py:556
  545.9 0.0 copy-start
  545.9 0.0 copy-done.1
  545.9 1.3 copy.64
  547.2 1.6 copy-done
  548.8 2.1 copy.65
  551.0 0.0 copy-done.8
  551.0 0.6 copy.66
  551.6 0.0 copy-done.7
  551.6 0.6 copy.67
  552.2 0.8 copy.68
  553.0 0.8 copy.69
  553.8 1.1 copy.70
  554.9 0.0 copy-done.3
  554.9 1.1 copy.71
  556.0 0.0 copy-done.2
  556.0 1.1 copy.72
  557.1 0.5 copy.73
  557.7 0.5 copy.74
  (15 shorter events, 0.0 us)
Async XLA Ops:
  7.2 203.6 %all-gather.3.cloned.1.call-start = ((), (), s32[]{:S(2)}) async-start(), calls=%async_computation.2 | async-start | bytes 7208960 | tf_op jit(solution)/shard_map/all_gather | solution.py:1566
  81.8 177.4 %all-gather.5.cloned.1.call-start = ((), (), s32[]{:S(2)}) async-start(), calls=%async_computation.3 | async-start | bytes 3932160 | tf_op jit(solution)/shard_map/all_gather | solution.py:1571
  124.3 325.4 %reduce-scatter.5.cloned.1.call-start = ((), (), s32[]{:S(2)}) async-start(), calls=%async_computation.5 | async-start | bytes 3932160 | tf_op jit(solution)/shard_map/reduce_scatter | solution.py:1578
  259.2 190.5 %reduce-scatter.3.cloned.1.call-start = ((), (), s32[]{:S(2)}) async-start(), calls=%async_computation.4 | async-start | bytes 7208960 | tf_op jit(solution)/shard_map/reduce_scatter | solution.py:1582
  449.7 96.2 %copy-start.1 = (bf16[512,2048]{1,0:T(8,128)(2,1)S(1)}, bf16[512,2048]{1,0:T(8,128)(2,1)}, u32[]{:S(2)}) copy-start(bf16[512,2048]{1,0:T(8,128)(2,1)} %get-tuple-element.61) | copy-start | bytes 6291460
  545.9 2.9 copy-start
  548.8 2.2 copy-start.8
  548.8 2.8 copy-start.7
  548.8 3.4 copy-start.6
  548.8 4.2 copy-start.5
  548.8 5.0 copy-start.4
  551.0 4.0 copy-start.3
  553.0 3.0 copy-start.2
  554.9 2.2 copy-start.10
  554.9 2.7 copy-start.9
Sparse Core Ops, SparseCore 0:
  81.9 112.2 all-gather.2
  195.8 61.7 all-gather.4
  260.5 63.7 reduce-scatter.4
  326.4 111.1 reduce-scatter.2

commit v4 on v3

--- a/solution.py
+++ b/solution.py
@@ -339,11 +339,24 @@
     return lax.rem(x + across % 2, 2) + 2 * lax.rem(y + across // 2, 2)
 
 
-def greet(devices):
+def say(devices):
     barrier = pltpu.get_barrier_semaphore()
     for device in devices:
         pl.semaphore_signal(barrier, inc=1, device_id=device, device_id_type=MESH)
-    pl.semaphore_wait(barrier, len(devices))
+
+
+def hear(count):
+    pl.semaphore_wait(pltpu.get_barrier_semaphore(), count)
+
+
+def greet(devices):
+    say(devices)
+    hear(len(devices))
+
+
+def around():
+    d, c, t = place_of()
+    return [(d, beside(c, 1), t), (d, beside(c, 2), t), (d, c, 1 - t)]
 
 
 def remote(source, target, send, receive, k, device):
@@ -357,7 +370,9 @@
     )
 
 
-def gather_rows(buf, send, receive, piece=None, early=None, middle=None, late=None):
+def gather_rows(
+    buf, out, send, receive, store, piece=None, early=None, middle=None, late=None
+):
     d, c, t = place_of()
     own = buf.shape[0] // 8
     half = own // 2
@@ -379,10 +394,17 @@
         ref = part(across, core, h)
         remote(ref, ref, send, receive, k, to_t).wait_recv()
 
+    stored = []
+
     def work(across, core):
+        block = c if across == 0 else beside(c, across)
+        start = pl.multiple_of((2 * block + core) * own, own)
+        rows = pl.ds(start, own)
+        copy = pltpu.make_async_copy(buf.at[rows], out.at[rows], store.at[len(stored)])
+        copy.start()
+        stored.append(copy)
         if piece is not None:
-            block = c if across == 0 else beside(c, across)
-            piece(pl.multiple_of((2 * block + core) * own, own))
+            piece(start)
 
     put(0, 0, 0, to_x)
     put(1, 0, 1, to_y)
@@ -428,116 +450,185 @@
     work(3, 1 - t)
     for copy in started:
         copy.wait_send()
+    for copy in stored:
+        copy.wait()
 
 
 GATHER_COPIES = 14
 
 
-def scatter_rows(terms, bufs, send, receive, fill=None):
+def gather_scratch(tokens, width):
+    return (
+        [pltpu.VMEM((tokens, width), BF16)]
+        + sems(GATHER_COPIES)
+        + [pltpu.SemaphoreType.DMA((8,))]
+    )
+
+
+def exchange(jobs, held, send, receive, local):
+    d, c, t = place_of()
+
+    def rows_of(block):
+        return pl.ds(pl.multiple_of(block * held, held), held)
+
+    def to_block(n, k):
+        source, target = jobs[n]
+        return remote(
+            source.at[rows_of(beside(c, k))], target.at[c], send, receive, 3 * n + k - 1,
+            (d, beside(c, k), t),
+        )
+
+    def from_block(n, k):
+        there = jobs[n][1].at[beside(c, k)]
+        return remote(there, there, send, receive, 3 * n + k - 1, (d, beside(c, k), t))
+
+    def at_home(n):
+        source, target = jobs[n]
+        return pltpu.make_async_copy(source.at[rows_of(c)], target.at[c], local.at[n])
+
+    def hand_on(n):
+        for k in (3, 1, 2):
+            to_block(n, k).start()
+        at_home(n).start()
+
+    def landed(n):
+        at_home(n).wait()
+        for k in (1, 2, 3):
+            from_block(n, k).wait_recv()
+            to_block(n, k).wait_send()
+
+    return hand_on, landed
+
+
+def scatter_order(i):
+    c = lax.axis_index("ctx")
+    across = 3 - i
+    x, y = lax.rem(c, 2), lax.div(c, 2)
+    return lax.rem(x + lax.rem(across, 2), 2) + 2 * lax.rem(y + lax.div(across, 2), 2)
+
+
+def scatter_rows(terms, bufs, send, receive, enter, fill=None):
     to_core, from_core, kept, over, came, stage = bufs
     d, c, t = place_of()
-    own, width = kept.shape[1:]
+    own, tile = kept.shape[2:]
     half = own // 2
-    tile = stage.shape[1]
     to_x, to_y, to_t = (d, beside(c, 1), t), (d, beside(c, 2), t), (d, c, 1 - t)
 
-    def link(k):
-        return remote(over.at[k], came.at[k], send, receive, 4 + k, to_x if k % 2 == 0 else to_y)
-
-    def core(i):
-        return remote(to_core.at[lax.rem(i, 2)], from_core.at[i], send, receive, i, to_t)
-
-    def total(i, h, *extra):
-        rows = pl.ds(h * half, half)
-        out = kept[i % 3, rows, :]
+    def link(k, n):
+        return remote(
+            over.at[k, n], came.at[k, n], send, receive, 8 + 2 * k + n, to_x if k % 2 == 0 else to_y
+        )
+
+    def core(i, n):
+        return remote(to_core.at[lax.rem(i, 2), n], from_core.at[i, n], send, receive, 2 * i + n, to_t)
+
+    def total(i, h, n, *extra):
+        out = kept[i % 3, n, pl.ds(h * half, half), :]
         for k in extra:
-            out = out + came[k].astype(F32)
+            out = out + came[k, n].astype(F32)
         return out
 
-    def ready(k, i, h, *extra):
-        over[k] = total(i, h, *extra).astype(BF16)
-
-    def joined(i):
-        core(i).wait_recv()
-        slot = lax.rem(i, 3)
-        kept[slot] = kept[slot] + from_core[i].astype(F32)
+    def go(k, i, h, n, *extra):
+        over[k, n] = total(i, h, n, *extra).astype(BF16)
+        link(k, n).start()
+
+    def joined(i, n):
+        core(i, n).wait_recv()
+        kept[lax.rem(i, 3), n] = kept[lax.rem(i, 3), n] + from_core[i, n].astype(F32)
+
+    def product(pairs, i, n):
+        columns = pl.ds(n * tile, tile)
+        theirs = pl.ds(pl.multiple_of((1 - t) * own, own), own)
+        mine = pl.ds(pl.multiple_of(t * own, own), own)
+        if not isinstance(pairs, list):
+            to_core[lax.rem(i, 2), n] = pairs[theirs, columns]
+            kept[lax.rem(i, 3), n] = pairs[mine, columns].astype(F32)
+            return
+        out = None
+        for rows, matrix, part in pairs:
+            term = dot(rows, matrix[columns, part], 1, 1)
+            out = term if out is None else out + term
+        stage[...] = out
+        to_core[lax.rem(i, 2), n] = stage[theirs, :].astype(BF16)
+        kept[lax.rem(i, 3), n] = stage[mine, :]
+
+    def begin(i):
+        return pl.multiple_of(2 * scatter_order(i) * own, 2 * own)
+
+    pairs = terms(0, begin(0))
+    product(pairs, 0, 0)
+    enter()
+    core(0, 0).start()
+    product(pairs, 0, 1)
+    core(0, 1).start()
+    for n in (0, 1):
+        joined(0, n)
+        go(0, 0, 0, n)
+        go(1, 0, 1, n)
 
     def step(i, carry):
-        across = 3 - i
-        x, y = lax.rem(c, 2), lax.div(c, 2)
-        block = lax.rem(x + lax.rem(across, 2), 2) + 2 * lax.rem(y + lax.div(across, 2), 2)
-        pairs = terms(i, pl.multiple_of(2 * block * own, 2 * own))
+        pairs = terms(i, begin(i))
 
         @pl.when(i >= 2)
         def _():
-            core(i - 2).wait_send()
-
-        @pl.loop(0, width // tile)
-        def _(n):
-            columns = pl.ds(pl.multiple_of(n * tile, tile), tile)
-            out = None
-            for rows, matrix, part in pairs:
-                term = dot(rows, matrix[columns, part], 1, 1)
-                out = term if out is None else out + term
-            stage[...] = out
-            to_core[lax.rem(i, 2), :, columns] = stage[
-                pl.ds(pl.multiple_of((1 - t) * own, own), own), :
-            ].astype(BF16)
-            kept[lax.rem(i, 3), :, columns] = stage[pl.ds(pl.multiple_of(t * own, own), own), :]
-
-        core(i).start()
-
-        @pl.when(i == 0)
-        def _():
-            joined(0)
-            ready(0, 0, 0)
-            link(0).start()
-            ready(1, 0, 1)
-            link(1).start()
+            for n in (0, 1):
+                core(i - 2, n).wait_send()
+
+        for n in (0, 1):
+            product(pairs, i, n)
+            core(i, n).start()
 
         @pl.when(i == 2)
         def _():
-            joined(1)
-            ready(3, 1, 1)
-            link(3).start()
+            for n in (0, 1):
+                joined(1, n)
+                go(3, 1, 1, n)
 
         return carry
 
-    lax.fori_loop(0, 4, step, 0)
-    joined(2)
-    ready(2, 2, 0)
-    link(2).start()
+    lax.fori_loop(1, 4, step, 0)
+    for n in (0, 1):
+        joined(2, n)
+        go(2, 2, 0, n)
     if fill is not None:
         fill(0)
-    link(0).wait_recv()
-    link(1).wait_recv()
-    ready(4, 2, 1, 1)
-    ready(5, 1, 0, 0)
-    link(4).start()
-    link(5).start()
-    joined(3)
+    for n in (0, 1):
+        link(0, n).wait_recv()
+        link(1, n).wait_recv()
+        go(4, 2, 1, n, 1)
+        go(5, 1, 0, n, 0)
+    for n in (0, 1):
+        joined(3, n)
     if fill is not None:
         fill(1)
-    for k in (2, 3, 4, 5):
-        link(k).wait_recv()
-    core(2).wait_send()
-    core(3).wait_send()
-    for k in range(6):
-        link(k).wait_send()
-    return jnp.concatenate([total(3, 0, 2, 5), total(3, 1, 3, 4)], axis=0)
-
-
-SCATTER_COPIES = 10
+    for n in (0, 1):
+        for k in (2, 3, 4, 5):
+            link(k, n).wait_recv()
+        core(2, n).wait_send()
+        core(3, n).wait_send()
+        for k in range(6):
+            link(k, n).wait_send()
+    return jnp.concatenate(
+        [
+            jnp.concatenate([total(3, 0, n, 2, 5), total(3, 1, n, 3, 4)], axis=0)
+            for n in (0, 1)
+        ],
+        axis=1,
+    )
+
+
+SCATTER_COPIES = 20
 
 
 def scatter_scratch(own, width):
+    tile = width // 2
     return [
-        pltpu.VMEM((2, own, width), BF16),
-        pltpu.VMEM((4, own, width), BF16),
-        pltpu.VMEM((3, own, width), F32),
-        pltpu.VMEM((6, own // 2, width), BF16),
-        pltpu.VMEM((6, own // 2, width), BF16),
-        pltpu.VMEM((2 * own, width // 2), F32),
+        pltpu.VMEM((2, 2, own, tile), BF16),
+        pltpu.VMEM((4, 2, own, tile), BF16),
+        pltpu.VMEM((3, 2, own, tile), F32),
+        pltpu.VMEM((6, 2, own // 2, tile), BF16),
+        pltpu.VMEM((6, 2, own // 2, tile), BF16),
+        pltpu.VMEM((2 * own, tile), F32),
     ]
 
 
@@ -599,9 +690,8 @@
 
     def kernel(
         x_ref, seg_ref, q_ref, k_ref, v_ref, o_ref, g_ref, u_ref, one_ref, two_ref,
-        rows_ref, segs_ref, wa_out, wg_out,
-        cut_a, cut_g,
-        send, receive, small_send, small_receive, deep_send, deep_receive, here,
+        rows_out, segs_ref, wa_out, wg_out,
+        cut_a, cut_g, rows_ref, send, receive, store, small_send, small_receive, deep_send, deep_receive, here,
     ):
         d, c, t = place_of()
         jobs = (
@@ -636,17 +726,19 @@
             return remote(there, there, deep_send, deep_receive, k - 1, (depth(d, k), c, t))
 
         one, two = one_ref[...], two_ref[...]
+        met = (
+            [(d, beside(c, k), t) for k in (1, 2, 3)]
+            + [(d, c, 1 - t)]
+            + [(depth(d, k), c, t) for k in range(1, deep)]
+        )
+        say(met)
         for b in range(4):
             cut_a[b, :, :wide] = columns(v_ref, one, b * wide, wide).astype(BF16)
             cut_a[b, :, wide : 2 * wide] = o_ref[:, b * wide : (b + 1) * wide]
             cut_a[b, :, 2 * wide :] = jnp.concatenate(
                 [columns(ref, one, b * narrow, narrow) for ref in (q_ref, k_ref)], axis=1
             ).astype(BF16)
-        greet(
-            [(d, beside(c, k), t) for k in (1, 2, 3)]
-            + [(d, c, 1 - t)]
-            + [(depth(d, k), c, t) for k in range(1, deep)]
-        )
+        hear(len(met))
         local(0).start()
         for k in (3, 1, 2):
             out(0, k).start()
@@ -674,7 +766,7 @@
                 for k in (3, 1, 2):
                     out(n, k).start()
 
-        gather_rows(rows_ref, send, receive, early=early)
+        gather_rows(rows_ref, rows_out, send, receive, store, early=early)
         for n in (1, 2):
             local(n).wait()
             for k in (1, 2, 3):
@@ -703,9 +795,9 @@
             pltpu.VMEM((4, held, packed), BF16),
             pltpu.VMEM((4, held, 2 * units), BF16),
         ]
-        + sems(GATHER_COPIES) + sems(9) + sems(deep - 1) + [pltpu.SemaphoreType.DMA((3,))],
+        + gather_scratch(tokens, width) + sems(9) + sems(deep - 1) + [pltpu.SemaphoreType.DMA((3,))],
         [vmem, hbm] + [vmem] * 8,
-        [vmem, hbm, hbm, hbm],
+        [hbm, hbm, hbm, hbm],
     )
 
 
@@ -717,18 +809,35 @@
     return jnp.maximum(i - apart(tokens) + 1, 0)
 
 
-def attend_back(qkv, g_mixed, mixed, denom, seg_rows, seg_cols, branch, heads_out, heads):
+def attend_back(
+    qkv, g_mixed, mixed, denom, seg_rows, seg_cols, branch, heads_out, out_terms, middle, sum_down, heads
+):
     tokens, width = branch.shape
     wide, narrow = heads * DV, heads * F
     blocks = tokens // BLOCK
     deep = lax.axis_size("dp")
     group = width // deep
+    own = tokens // 8
+    held, units = sum_down.shape[0] // 4, sum_down.shape[1]
 
     def kernel(
-        x_ref, gm_ref, m_ref, d_ref, row_ref, col_ref, br_ref, h_ref, g_ref, sum_ref,
+        x_ref, gm_ref, m_ref, d_ref, row_ref, col_ref, br_ref, h_ref, term_ref, mid_ref, down_ref,
+        g_ref, out_ref, go_ref, gd_ref,
         gq_ref, numer_ref, gden_ref, key_ref, back_ref, came, br_buf, load, send, receive,
+        term_buf, term_load, sums, parts_o, parts_d, p_send, p_receive, local, *rest,
     ):
+        bufs, (s_send, s_receive, t_send, t_receive) = rest[:6], rest[6:]
         d, c, t = place_of()
+        hand_on, landed = exchange(
+            ((sums, parts_o), (down_ref, parts_d)), held, p_send, p_receive, local
+        )
+
+        def fetch_terms(i):
+            part = pl.ds(pl.multiple_of(2 * scatter_order(i) * own, 2 * own), 2 * own)
+            slot = lax.rem(i, 2)
+            return pltpu.make_async_copy(term_ref.at[part], term_buf.at[slot], term_load.at[slot])
+
+        fetch_terms(0).start()
 
         def fetch(n):
             part = pl.ds(pl.multiple_of(depth(d, n + 1) * group, group), group)
@@ -741,7 +850,12 @@
             )
 
         fetch(0).start()
-        greet([(depth(d, k), c, t) for k in range(1, deep)])
+        met = (
+            around()
+            + [(d, beside(c, 3), t)]
+            + [(depth(d, k), c, t) for k in range(1, deep)]
+        )
+        say(met)
 
         def plane(n, carry):
             @pl.when(n < deep - 1)
@@ -757,28 +871,29 @@
 
             return carry
 
-        lax.fori_loop(0, deep, plane, 0)
-
-        gq_ref[...] = jnp.zeros_like(gq_ref)
-        for h in range(heads):
-            part = pl.ds(h * DV, DV)
-            gm = gm_ref[:, part].astype(F32)
-            inverse = 1.0 / d_ref[:, h : h + 1]
-            numer_ref[:, part] = (gm * inverse).astype(BF16)
-            down = -jnp.sum(gm * m_ref[:, part], axis=1, keepdims=True) * inverse
-            gden_ref[h : h + 1, :] = jnp.transpose(jnp.broadcast_to(down, (tokens, 128)), (1, 0))[:1]
-        key_ref[...] = jnp.transpose(x_ref[:, wide : wide + 2 * narrow].astype(F32), (1, 0)).astype(
-            BF16
-        )
+        def prepare():
+            gq_ref[...] = jnp.zeros_like(gq_ref)
+            for h in range(heads):
+                part = pl.ds(h * DV, DV)
+                gm = gm_ref[:, part].astype(F32)
+                inverse = 1.0 / d_ref[:, h : h + 1]
+                numer_ref[:, part] = (gm * inverse).astype(BF16)
+                down = -jnp.sum(gm * m_ref[:, part], axis=1, keepdims=True) * inverse
+                gden_ref[h : h + 1, :] = jnp.transpose(
+                    jnp.broadcast_to(down, (tokens, 128)), (1, 0)
+                )[:1]
+            key_ref[...] = jnp.transpose(
+                x_ref[:, wide : wide + 2 * narrow].astype(F32), (1, 0)
+            ).astype(BF16)
+
         place = lax.broadcasted_iota(jnp.int32, (BLOCK, BLOCK), 1) - lax.broadcasted_iota(
             jnp.int32, (BLOCK, BLOCK), 0
         )
         tempered = BF16(F**-0.5)
 
-        @pl.loop(0, blocks)
-        def _(j):
+        def one_block(j):
             start = pl.multiple_of(j * BLOCK, BLOCK)
-            own = row_ref[pl.ds(start, BLOCK), :]
+            ids = row_ref[pl.ds(start, BLOCK), :]
             values = [x_ref[pl.ds(start, BLOCK), h * DV : (h + 1) * DV] for h in range(heads)]
             keys = [
                 x_ref[pl.ds(start, BLOCK), wide + (heads + h) * F : wide + (heads + h + 1) * F]
@@ -792,7 +907,7 @@
 
             def step(i, sums):
                 base = pl.multiple_of(i * BLOCK, BLOCK)
-                visible = (place >= start - base) & (own == col_ref[:, pl.ds(base, BLOCK)])
+                visible = (place >= start - base) & (ids == col_ref[:, pl.ds(base, BLOCK)])
                 out = []
                 for h in range(heads):
                     queries = x_ref[pl.ds(base, BLOCK), wide + h * F : wide + (h + 1) * F]
@@ -817,20 +932,61 @@
                     pl.ds(start, BLOCK), wide + (heads + h) * F : wide + (heads + h + 1) * F
                 ] = (sums[2 * h + 1] * F**-0.5).astype(BF16)
 
+        def terms(i, start):
+            fetch_terms(i).wait()
+
+            @pl.when(i < 3)
+            def _():
+                fetch_terms(i + 1).start()
+
+            return term_buf.at[lax.rem(i, 2)]
+
+        def fill(n):
+            if n == 0:
+                lax.fori_loop(0, deep, plane, 0)
+                hand_on(1)
+                prepare()
+                pl.loop(0, 1)(one_block)
+            else:
+                pl.loop(1, blocks)(one_block)
+
+        moved = scatter_rows(terms, bufs, s_send, s_receive, lambda: hear(len(met)), fill)
+        here = out_ref.at[pl.ds(pl.multiple_of(t * own, own), own)]
+        here[...] = (mid_ref[...] + moved).astype(BF16)
+        copy = remote(here, here, t_send, t_receive, 0, (d, c, 1 - t))
+        copy.start()
         g_ref[:, wide : wide + narrow] = jnp.transpose(gq_ref[...], (1, 0)).astype(BF16)
         total = back_ref[deep - 1].astype(F32)
         for n in range(deep - 1):
             deeper(n).wait_recv()
             total = total + came[n].astype(F32)
-        sum_ref[...] = total.astype(BF16)
+        sums[...] = total.astype(BF16)
+        hand_on(0)
+        landed(1)
+        for b in range(4):
+            gd_ref[:, b * units : (b + 1) * units] = parts_d[b].astype(F32)
+        landed(0)
+        for b in range(4):
+            go_ref[:, b * wide : (b + 1) * wide] = parts_o[b].astype(F32)
         for n in range(deep - 1):
             deeper(n).wait_send()
+        copy.wait_send()
+        there = out_ref.at[pl.ds(pl.multiple_of((1 - t) * own, own), own)]
+        remote(there, there, t_send, t_receive, 0, (d, c, 1 - t)).wait_recv()
 
     vmem, hbm = pl.BlockSpec(memory_space=pltpu.VMEM), pl.BlockSpec(memory_space=pl.ANY)
     return call(
         kernel, "attend_back", 7,
-        (qkv, g_mixed, mixed, denom, seg_rows, seg_cols, branch, heads_out),
-        [jax.ShapeDtypeStruct(qkv.shape, BF16), jax.ShapeDtypeStruct((group, wide), BF16)],
+        (
+            qkv, g_mixed, mixed, denom, seg_rows, seg_cols, branch, heads_out, out_terms, middle,
+            sum_down,
+        ),
+        [
+            jax.ShapeDtypeStruct(qkv.shape, BF16),
+            jax.ShapeDtypeStruct((2 * own, width), BF16),
+            jax.ShapeDtypeStruct((held, 4 * wide), F32),
+            jax.ShapeDtypeStruct((held, 4 * units), F32),
+        ],
         [
             pltpu.VMEM((narrow, tokens), F32),
             pltpu.VMEM((tokens, wide), BF16),
@@ -841,8 +997,16 @@
             pltpu.VMEM((2, tokens, group), BF16),
             pltpu.SemaphoreType.DMA((2,)),
         ]
-        + sems(deep - 1),
-        [vmem] * 6 + [hbm, vmem],
+        + sems(deep - 1)
+        + [pltpu.VMEM((2, 2 * own, width), BF16), pltpu.SemaphoreType.DMA((2,))]
+        + [
+            pltpu.VMEM((group, wide), BF16),
+            pltpu.VMEM((4, held, wide), BF16),
+            pltpu.VMEM((4, held, units), BF16),
+        ]
+        + sems(6) + [pltpu.SemaphoreType.DMA((2,))]
+        + scatter_scratch(own, width) + sems(SCATTER_COPIES) + sems(1),
+        [vmem] * 6 + [hbm, vmem, hbm, vmem, hbm],
     )
 
 
@@ -896,8 +1060,8 @@
 
     def kernel(
         x_ref, w_ref, row_ref, col_ref, cot_ref, d_ref,
-        qkv_ref, mixed_ref, denom_ref, low_ref, rows_ref, wd_out,
-        ext_ref, cut, send, receive, d_send, d_receive, here,
+        qkv_ref, mixed_ref, denom_ref, low_ref, rows_out, wd_out,
+        ext_ref, cut, rows_ref, send, receive, store, d_send, d_receive, here,
     ):
         d, c, t = place_of()
 
@@ -911,13 +1075,15 @@
             return remote(there, there, d_send, d_receive, k - 1, (d, beside(c, k), t))
 
         local = pltpu.make_async_copy(cut.at[c], wd_out.at[c], here.at[0])
+        met = [(d, beside(c, k), t) for k in (1, 2, 3)] + [(d, c, 1 - t)]
+        say(met)
         for b in range(4):
             part = columns(d_ref, None, b * units, units)
             if units < filled:
                 part = jnp.concatenate([part, jnp.zeros((held, filled - units), F32)], axis=1)
             cut[b] = part.astype(BF16)
-        greet([(d, beside(c, k), t) for k in (1, 2, 3)] + [(d, c, 1 - t)])
         mine = pl.multiple_of((2 * c + t) * own, own)
+        hear(len(met))
         rows_ref[pl.ds(mine, own), :] = cot_ref[
             pl.ds(pl.multiple_of(t * own, own), own), : width // 2
         ]
@@ -945,7 +1111,7 @@
                     ext_ref[rows, (2 * h + 1) * DV : (2 * h + 2) * DV] = jnp.ones((BLOCK, DV), BF16)
 
         gather_rows(
-            rows_ref, send, receive, early=early,
+            rows_ref, rows_out, send, receive, store, early=early,
             middle=lambda: blocks(0, tokens // BLOCK // 2),
             late=lambda: blocks(tokens // BLOCK // 2, tokens // BLOCK),
         )
@@ -966,9 +1132,9 @@
             jax.ShapeDtypeStruct((4, held, filled), BF16),
         ],
         [pltpu.VMEM((tokens, 2 * wide), BF16), pltpu.VMEM((4, held, filled), BF16)]
-        + sems(GATHER_COPIES) + sems(3) + [pltpu.SemaphoreType.DMA((1,))],
+        + gather_scratch(tokens, width // 2) + sems(3) + [pltpu.SemaphoreType.DMA((1,))],
         None,
-        [vmem] * 5 + [hbm],
+        [vmem] * 4 + [hbm, hbm],
     )
 
 
@@ -977,39 +1143,43 @@
     own = tokens // 8
     wide = heads_out.shape[1]
 
-    def kernel(h_ref, w_ref, x_ref, mid_ref, rows_ref, *rest):
-        bufs, (s_send, s_receive, g_send, g_receive) = rest[:6], rest[6:]
+    def kernel(h_ref, w_ref, x_ref, mid_ref, rows_out, *rest):
+        bufs, (s_send, s_receive, rows_ref, g_send, g_receive, store) = rest[:6], rest[6:]
         d, c, t = place_of()
-        greet([(d, beside(c, 1), t), (d, beside(c, 2), t), (d, c, 1 - t)])
+        say(around())
 
         def terms(i, start):
             return [(h_ref[pl.ds(start, 2 * own), :], w_ref, slice(wide, 2 * wide))]
 
-        total = scatter_rows(terms, bufs, s_send, s_receive)
+        total = scatter_rows(terms, bufs, s_send, s_receive, lambda: hear(3))
         middle = total + x_ref[pl.ds(pl.multiple_of(t * own, own), own), :].astype(F32)
         mid_ref[...] = middle
         _, hat = norm_parts(middle)
         rows_ref[pl.ds(pl.multiple_of((2 * c + t) * own, own), own), :] = hat.astype(BF16)
-        gather_rows(rows_ref, g_send, g_receive)
+        gather_rows(rows_ref, rows_out, g_send, g_receive, store)
 
     return call(
         kernel, "to_middle", 3, (heads_out, w_attn, x),
         [jax.ShapeDtypeStruct((own, width), F32), jax.ShapeDtypeStruct((tokens, width), BF16)],
-        scatter_scratch(own, width) + sems(SCATTER_COPIES) + sems(GATHER_COPIES),
+        scatter_scratch(own, width) + sems(SCATTER_COPIES) + gather_scratch(tokens, width),
+        None,
+        [pl.BlockSpec(memory_space=pltpu.VMEM), pl.BlockSpec(memory_space=pl.ANY)],
         flops=2 * tokens * width * heads_out.shape[1],
     )
 
 
-def gate_up(rows_two, w_both, cot):
+def gate_up(rows_two, w_both, cot, cot_low):
     tokens, width = rows_two.shape
     own = tokens // 8
     units = w_both.shape[1] // 2
     main = units // 128 * 128
     count = tokens // BLOCK
+    tile = 256
 
     def kernel(
-        x_ref, w_ref, cot_ref, hid_out, slope_out, silu_out, rows_ref,
-        x_buf, w_buf, hid_ref, slope_ref, silu_ref, load, store, send, receive,
+        x_ref, w_ref, cot_ref, low_ref, hid_out, slope_out, silu_out, rows_out, down_out,
+        x_buf, w_buf, low_buf, hid_ref, slope_ref, silu_ref, down_buf, load, store, down_store,
+        rows_ref, send, receive, row_store,
     ):
         d, c, t = place_of()
 
@@ -1022,16 +1192,22 @@
             rows = pl.ds(pl.multiple_of(i * BLOCK, BLOCK), BLOCK)
             slot = lax.rem(i, 2)
             return [
-                pltpu.make_async_copy(source.at[slot], target.at[rows], store.at[n, slot])
+                pltpu.make_async_copy(source, target.at[rows], store.at[n, slot])
                 for n, (source, target) in enumerate(
-                    ((hid_ref, hid_out), (slope_ref, slope_out), (silu_ref, silu_out))
+                    (
+                        (hid_ref.at[rows], hid_out),
+                        (slope_ref.at[slot], slope_out),
+                        (silu_ref.at[slot], silu_out),
+                    )
                 )
             ]
 
         weights = pltpu.make_async_copy(w_ref, w_buf, load.at[2])
         weights.start()
         fetch(0).start()
-        greet([(d, beside(c, 1), t), (d, beside(c, 2), t), (d, c, 1 - t)])
+        low_copy = pltpu.make_async_copy(low_ref, low_buf, load.at[3])
+        low_copy.start()
+        greet(around())
         mine = pl.multiple_of((2 * c + t) * own, own)
         rows_ref[pl.ds(mine, own), :] = cot_ref[
             pl.ds(pl.multiple_of(t * own, own), own), width // 2 :
@@ -1057,7 +1233,9 @@
                 def act(gate, up, part):
                     sig = jax.nn.sigmoid(gate)
                     silu = gate * sig
-                    hid_ref[slot, :, part] = (silu * up).astype(BF16)
+                    hid_ref[pl.ds(pl.multiple_of(i * BLOCK, BLOCK), BLOCK), part] = (
+                        silu * up
+                    ).astype(BF16)
                     slope_ref[slot, :, part] = (up * sig * (1.0 + gate * (1.0 - sig))).astype(BF16)
                     silu_ref[slot, :, part] = silu.astype(BF16)
 
@@ -1071,66 +1249,92 @@
                 for copy in given(i):
                     copy.start()
 
+        per = width // 2 // tile
+
+        def down_given(base, n):
+            slot = lax.rem(n, 2)
+            rows = pl.ds(pl.multiple_of(base + n * tile, tile), tile)
+            return pltpu.make_async_copy(down_buf.at[slot], down_out.at[rows], down_store.at[slot])
+
+        def down_tiles(source, base, end):
+            @pl.loop(0, end)
+            def _(n):
+                @pl.when(n >= 2)
+                def _():
+                    down_given(base, n - 2).wait()
+
+                part = pl.ds(pl.multiple_of(n * tile, tile), tile)
+                down_buf[lax.rem(n, 2)] = dot(source[:, part], hid_ref[...], 0, 0).astype(BF16)
+                down_given(base, n).start()
+
         def early():
             weights.wait()
             blocks(0, 1)
 
+        def later():
+            blocks(count // 2, count)
+            low_copy.wait()
+            down_tiles(low_buf, 0, per)
+            for n in (per - 2, per - 1):
+                down_given(0, n).wait()
+
         gather_rows(
-            rows_ref, send, receive, early=early,
-            middle=lambda: blocks(1, count // 2), late=lambda: blocks(count // 2, count),
+            rows_ref, rows_out, send, receive, row_store, early=early,
+            middle=lambda: blocks(1, count // 2), late=later,
         )
+        down_tiles(rows_ref, width // 2, per)
+        for n in (per - 2, per - 1):
+            down_given(width // 2, n).wait()
         for i in (count - 2, count - 1):
             for copy in given(i):
                 copy.wait()
 
     vmem, hbm = pl.BlockSpec(memory_space=pltpu.VMEM), pl.BlockSpec(memory_space=pl.ANY)
     return call(
-        kernel, "gate_up", 8, (rows_two, w_both, cot),
+        kernel, "gate_up", 8, (rows_two, w_both, cot, cot_low),
         [jax.ShapeDtypeStruct((tokens, units), BF16)] * 3
-        + [jax.ShapeDtypeStruct((tokens, width // 2), BF16)],
+        + [
+            jax.ShapeDtypeStruct((tokens, width // 2), BF16),
+            jax.ShapeDtypeStruct((width, units), BF16),
+        ],
         [
             pltpu.VMEM((2, BLOCK, width), BF16),
             pltpu.VMEM(w_both.shape, BF16),
+            pltpu.VMEM(cot_low.shape, BF16),
+            pltpu.VMEM((tokens, units), BF16),
             pltpu.VMEM((2, BLOCK, units), BF16),
             pltpu.VMEM((2, BLOCK, units), BF16),
-            pltpu.VMEM((2, BLOCK, units), BF16),
-            pltpu.SemaphoreType.DMA((3,)),
+            pltpu.VMEM((2, tile, units), BF16),
+            pltpu.SemaphoreType.DMA((4,)),
             pltpu.SemaphoreType.DMA((3, 2)),
+            pltpu.SemaphoreType.DMA((2,)),
         ]
-        + sems(GATHER_COPIES),
-        [hbm, hbm, vmem],
-        [hbm, hbm, hbm, vmem],
+        + gather_scratch(tokens, width // 2),
+        [hbm, hbm, vmem, hbm],
+        [hbm] * 5,
         flops=4 * tokens * width * units,
     )
 
 
-def feed_forward(hidden, slope, silu, cot_low, cot_high, middle, w_down, rows_two):
+def feed_forward(slope, silu, cot_low, cot_high, w_down, rows_two):
     tokens, width = rows_two.shape
-    own = tokens // 8
-    units = hidden.shape[1]
+    units = slope.shape[1]
     main = units // 128 * 128
     tile = 256
     part_width = width // 2
+    count = tokens // BLOCK
 
     def kernel(
-        hid_ref, slope_ref, silu_ref, low_ref, high_ref, mid_ref, d_ref, two_ref,
-        g_out, out_ref, grad_ref,
-        hid_buf, slope_buf, silu_buf, low_buf, high_buf, d_buf, g_ref, here, g_store,
-        cols, out, load, store, *rest,
+        slope_ref, silu_ref, low_ref, high_ref, d_ref, two_ref, g_out, grad_ref,
+        slope_buf, silu_buf, low_buf, high_buf, d_buf, g_ref, here, g_store, cols, out, load, store,
     ):
-        bufs, (s_send, s_receive, t_send, t_receive) = rest[:6], rest[6:]
-        d, c, t = place_of()
-
-        def block_rows(i):
-            across = 3 - i
-            x, y = lax.rem(c, 2), lax.div(c, 2)
-            block = lax.rem(x + lax.rem(across, 2), 2) + 2 * lax.rem(y + lax.div(across, 2), 2)
-            return pl.ds(pl.multiple_of(2 * block * own, 2 * own), 2 * own)
+        def rows(i):
+            return pl.ds(pl.multiple_of(i * BLOCK, BLOCK), BLOCK)
 
         def fetch(i):
-            part = block_rows(i)
+            slot = lax.rem(i, 2)
             return [
-                pltpu.make_async_copy(source.at[part], target, here.at[n])
+                pltpu.make_async_copy(source.at[rows(i)], target.at[slot], here.at[n, slot])
                 for n, (source, target) in enumerate(
                     (
                         (low_ref, low_buf),
@@ -1141,17 +1345,8 @@
                 )
             ]
 
-        def fetch_hidden(i):
-            return pltpu.make_async_copy(hid_ref.at[block_rows(i)], hid_buf, here.at[4])
-
         def g_given(i):
-            part = block_rows(i)
-            return pltpu.make_async_copy(g_ref.at[part], g_out.at[part], g_store.at[i])
-
-        weights = pltpu.make_async_copy(d_ref, d_buf, here.at[5])
-        weights.start()
-        for copy in fetch(0):
-            copy.start()
+            return pltpu.make_async_copy(g_ref.at[rows(i)], g_out.at[rows(i)], g_store.at[i])
 
         def wanted(n):
             part = pl.ds(pl.multiple_of(n * tile, tile), tile)
@@ -1163,39 +1358,30 @@
             slot = lax.rem(n, 2)
             return pltpu.make_async_copy(out.at[slot], grad_ref.at[part], store.at[slot])
 
-        last = width // tile
-
-        def tiles(first, end):
-            @pl.loop(first, end)
-            def _(n):
-                wanted(n).wait()
-
-                @pl.when(n + 1 < last)
-                def _():
-                    wanted(n + 1).start()
-
-                @pl.when(n >= 2)
-                def _():
-                    given(n - 2).wait()
-
-                slot = lax.rem(n, 2)
-                out[slot] = dot(cols[slot], g_ref[...], 0, 0).astype(BF16)
-                given(n).start()
-
+        weights = pltpu.make_async_copy(d_ref, d_buf, load.at[2])
+        weights.start()
+        for copy in fetch(0):
+            copy.start()
         wanted(0).start()
-        greet([(d, beside(c, 1), t), (d, beside(c, 2), t), (d, c, 1 - t)])
         weights.wait()
 
-        def terms(i, start):
-            part = pl.ds(start, 2 * own)
-            fetch_hidden(i).start()
+        @pl.loop(0, count)
+        def _(i):
+            slot = lax.rem(i, 2)
+
+            @pl.when(i + 1 < count)
+            def _():
+                for copy in fetch(i + 1):
+                    copy.start()
+
             for copy in fetch(i):
                 copy.wait()
-            g_hidden = dot(low_buf[...], d_buf[:part_width, :units], 1, 0) + dot(
-                high_buf[...], d_buf[part_width:, :units], 1, 0
+            g_hidden = dot(low_buf[slot], d_buf[:part_width, :units], 1, 0) + dot(
+                high_buf[slot], d_buf[part_width:, :units], 1, 0
             )
-            gg = g_hidden * slope_buf[...].astype(F32)
-            gu = g_hidden * silu_buf[...].astype(F32)
+            gg = g_hidden * slope_buf[slot].astype(F32)
+            gu = g_hidden * silu_buf[slot].astype(F32)
+            part = rows(i)
             g_ref[part, :main] = gg[:, :main].astype(BF16)
             g_ref[part, main : 2 * main] = gu[:, :main].astype(BF16)
             if main < units:
@@ -1204,87 +1390,89 @@
                 ).astype(BF16)
             g_given(i).start()
 
-            @pl.when(i < 3)
+        last = width // tile
+
+        @pl.loop(0, last)
+        def _(n):
+            @pl.when(n + 1 < last)
             def _():
-                for copy in fetch(i + 1):
-                    copy.start()
-
-            fetch_hidden(i).wait()
-            return [(hid_buf[...], d_buf, slice(0, units))]
-
-        def fill(n):
-            if n == 0:
-                tiles(0, 2)
-            else:
-                tiles(2, last)
-
-        total = scatter_rows(terms, bufs, s_send, s_receive, fill)
-        place = out_ref.at[pl.ds(pl.multiple_of(t * own, own), own)]
-        place[...] = (mid_ref[...] + total).astype(BF16)
-        copy = remote(place, place, t_send, t_receive, 0, (d, c, 1 - t))
-        copy.start()
-        copy.wait_send()
-        there = out_ref.at[pl.ds(pl.multiple_of((1 - t) * own, own), own)]
-        remote(there, there, t_send, t_receive, 0, (d, c, 1 - t)).wait_recv()
+                wanted(n + 1).start()
+
+            wanted(n).wait()
+
+            @pl.when(n >= 2)
+            def _():
+                given(n - 2).wait()
+
+            slot = lax.rem(n, 2)
+            out[slot] = dot(cols[slot], g_ref[...], 0, 0).astype(BF16)
+            given(n).start()
+
         given(last - 2).wait()
         given(last - 1).wait()
-        for i in range(4):
+        for i in range(count):
             g_given(i).wait()
 
-    vmem, hbm = pl.BlockSpec(memory_space=pltpu.VMEM), pl.BlockSpec(memory_space=pl.ANY)
-    return call(
-        kernel, "feed_forward", 4,
-        (hidden, slope, silu, cot_low, cot_high, middle, w_down, rows_two),
-        [
+    hbm = pl.BlockSpec(memory_space=pl.ANY)
+    moved = 2 * tokens * (2 * width + 4 * units) + 6 * width * units
+    return pl.pallas_call(
+        kernel,
+        in_specs=[hbm] * 6,
+        out_specs=[hbm] * 2,
+        out_shape=[
             jax.ShapeDtypeStruct((tokens, 2 * units), BF16),
-            jax.ShapeDtypeStruct((2 * own, width), BF16),
             jax.ShapeDtypeStruct((width, 2 * units), BF16),
         ],
-        [
-            pltpu.VMEM((2 * own, units), BF16),
-            pltpu.VMEM((2 * own, units), BF16),
-            pltpu.VMEM((2 * own, units), BF16),
-            pltpu.VMEM((2 * own, part_width), BF16),
-            pltpu.VMEM((2 * own, part_width), BF16),
+        scratch_shapes=[
+            pltpu.VMEM((2, BLOCK, units), BF16),
+            pltpu.VMEM((2, BLOCK, units), BF16),
+            pltpu.VMEM((2, BLOCK, part_width), BF16),
+            pltpu.VMEM((2, BLOCK, part_width), BF16),
             pltpu.VMEM(w_down.shape, BF16),
             pltpu.VMEM((tokens, 2 * units), BF16),
-            pltpu.SemaphoreType.DMA((6,)),
-            pltpu.SemaphoreType.DMA((4,)),
+            pltpu.SemaphoreType.DMA((4, 2)),
+            pltpu.SemaphoreType.DMA((count,)),
             pltpu.VMEM((2, tokens, tile), BF16),
             pltpu.VMEM((2, tile, 2 * units), BF16),
+            pltpu.SemaphoreType.DMA((3,)),
             pltpu.SemaphoreType.DMA((2,)),
-            pltpu.SemaphoreType.DMA((2,)),
-        ]
-        + scatter_scratch(own, width) + sems(SCATTER_COPIES) + sems(1),
-        [hbm] * 5 + [vmem, hbm, hbm],
-        [hbm, vmem, hbm],
-        flops=8 * tokens * width * units,
-    )
-
-
-def to_branch(g_both, w_both, middle, cot, w_attn, wide):
+        ],
+        compiler_params=pltpu.CompilerParams(vmem_limit_bytes=VMEM_MOST),
+        cost_estimate=pl.CostEstimate(
+            flops=6 * tokens * width * units, bytes_accessed=moved, transcendentals=0
+        ),
+        name="feed_forward",
+    )(slope, silu, cot_low, cot_high, w_down, rows_two)
+
+
+def to_branch(g_both, w_both, middle, cot, w_attn, wide, hidden, w_down):
     tokens, width = g_both.shape[0], middle.shape[1]
     own = tokens // 8
+    units = hidden.shape[1]
+    tile = width // 2
 
     def kernel(
-        g_ref, w_ref, mid_ref, cot_ref, o_ref, gm_ref, rows_ref, mix_ref, g_buf, w_buf, load, *rest
+        g_ref, w_ref, mid_ref, cot_ref, o_ref, hid_ref, d_ref, gm_ref, rows_out, mix_ref, term_ref,
+        g_buf, w_buf, hid_buf, d_buf, term_buf, load, term_store, *rest,
     ):
-        bufs, (s_send, s_receive, g_send, g_receive) = rest[:6], rest[6:]
+        bufs, (s_send, s_receive, rows_ref, g_send, g_receive, store) = rest[:6], rest[6:]
         d, c, t = place_of()
 
         def fetch(i):
-            across = 3 - i
-            x, y = lax.rem(c, 2), lax.div(c, 2)
-            block = lax.rem(x + lax.rem(across, 2), 2) + 2 * lax.rem(y + lax.div(across, 2), 2)
-            part = pl.ds(pl.multiple_of(2 * block * own, 2 * own), 2 * own)
+            part = pl.ds(pl.multiple_of(2 * scatter_order(i) * own, 2 * own), 2 * own)
             slot = lax.rem(i, 2)
             return pltpu.make_async_copy(g_ref.at[part], g_buf.at[slot], load.at[slot])
 
         weights = pltpu.make_async_copy(w_ref, w_buf, load.at[2])
         weights.start()
         fetch(0).start()
-        greet([(d, beside(c, 1), t), (d, beside(c, 2), t), (d, c, 1 - t)])
+        say(around())
         weights.wait()
+        down = pltpu.make_async_copy(d_ref, d_buf, load.at[3])
+        down.start()
+        pltpu.make_async_copy(
+            hid_ref.at[pl.ds(0, BLOCK)], hid_buf, load.at[4]
+        ).start()
 
         def terms(i, start):
             fetch(i).wait()
@@ -1295,7 +1483,7 @@
 
             return [(g_buf[lax.rem(i, 2)], w_buf, slice(None))]
 
-        total = scatter_rows(terms, bufs, s_send, s_receive)
+        total = scatter_rows(terms, bufs, s_send, s_receive, lambda: hear(3))
         scale, hat = norm_parts(mid_ref[...])
         g_middle = cot_ref[pl.ds(pl.multiple_of(t * own, own), own), :].astype(F32) + norm_back(
             total, hat, scale
@@ -1308,22 +1496,66 @@
                 rows_ref[pl.ds(start, own), :], o_ref[:, wide : 2 * wide], 1, 0
             ).astype(BF16)
 
-        gather_rows(rows_ref, g_send, g_receive, mix)
-
+        def block(i):
+            return pl.ds(pl.multiple_of(i * BLOCK, BLOCK), BLOCK)
+
+        def hidden_of(i):
+            return pltpu.make_async_copy(hid_ref.at[block(i)], hid_buf, load.at[4])
+
+        def term_given(i):
+            return pltpu.make_async_copy(term_buf, term_ref.at[block(i)], term_store.at[0])
+
+        def out_terms(first, last):
+            @pl.loop(first, last)
+            def _(i):
+                hidden_of(i).wait()
+
+                @pl.when(i > 0)
+                def _():
+                    term_given(i - 1).wait()
+
+                for n in (0, 1):
+                    columns = slice(n * tile, (n + 1) * tile)
+                    term_buf[:, columns] = dot(
+                        hid_buf[...], d_buf[columns, :units], 1, 1
+                    ).astype(BF16)
+                term_given(i).start()
+
+                @pl.when(i + 1 < tokens // BLOCK)
+                def _():
+                    hidden_of(i + 1).start()
+
+        down.wait()
+        blocks = tokens // BLOCK
+        gather_rows(
+            rows_ref, rows_out, g_send, g_receive, store, mix,
+            lambda: out_terms(0, blocks // 2),
+            lambda: out_terms(blocks // 2, blocks - 1),
+            lambda: out_terms(blocks - 1, blocks),
+        )
+        term_given(blocks - 1).wait()
+
+    vmem, hbm = pl.BlockSpec(memory_space=pltpu.VMEM), pl.BlockSpec(memory_space=pl.ANY)
     return call(
-        kernel, "to_branch", 5, (g_both, w_both, middle, cot, w_attn),
+        kernel, "to_branch", 5, (g_both, w_both, middle, cot, w_attn, hidden, w_down),
         [
             jax.ShapeDtypeStruct((own, width), F32),
             jax.ShapeDtypeStruct((tokens, width), BF16),
             jax.ShapeDtypeStruct((tokens, wide), BF16),
+            jax.ShapeDtypeStruct((tokens, width), BF16),
         ],
         [
             pltpu.VMEM((2, 2 * own, g_both.shape[1]), BF16),
             pltpu.VMEM(w_both.shape, BF16),
-            pltpu.SemaphoreType.DMA((3,)),
+            pltpu.VMEM((BLOCK, units), BF16),
+            pltpu.VMEM(w_down.shape, BF16),
+            pltpu.VMEM((BLOCK, width), BF16),
+            pltpu.SemaphoreType.DMA((5,)),
+            pltpu.SemaphoreType.DMA((1,)),
         ]
-        + scatter_scratch(own, width) + sems(SCATTER_COPIES) + sems(GATHER_COPIES),
-        [pl.BlockSpec(memory_space=pl.ANY)] * 2 + [pl.BlockSpec(memory_space=pltpu.VMEM)] * 3,
+        + scatter_scratch(own, width) + sems(SCATTER_COPIES) + gather_scratch(tokens, width),
+        [hbm, hbm, vmem, vmem, vmem, hbm, hbm],
+        [vmem, hbm, vmem, hbm],
         flops=4 * tokens * width * (g_both.shape[1] // 2 + wide),
     )
 
@@ -1332,9 +1564,7 @@
     return jnp.transpose(jnp.broadcast_to(column, (column.shape[0], 128)), (1, 0))[:8]
 
 
-def to_input(
-    g_qkv, w_attn, x, g_middle, rows_one, sum_out, sum_both, sum_down, weights, gains, heads
-):
+def to_input(g_qkv, w_attn, x, g_middle, rows_one, sum_both, weights, gains, heads):
     tokens, width = g_qkv.shape[0], x.shape[1]
     own = tokens // 8
     deep = lax.axis_size("dp")
@@ -1342,21 +1572,25 @@
     group = width // deep
     held = group // 4
     wide, narrow = heads * DV, heads * F
-    both, units = sum_both.shape[1], sum_down.shape[1]
+    both = sum_both.shape[1]
+    units = both // 2
     main = units // 128 * 128
 
     def kernel(
-        g_ref, w_ref, x_ref, gm_ref, one_ref, so_ref, both_ref, down_ref,
+        g_ref, w_ref, x_ref, gm_ref, one_ref, both_ref,
         wq_ref, wk_ref, wv_ref, wg_ref, wu_ref, gain_ref, gain_two_ref,
-        out_ref, gq_ref, gk_ref, gv_ref, go_ref, gg_ref, gu_ref, gd_ref, row_ref, row_two_ref,
+        out_ref, gq_ref, gk_ref, gv_ref, gg_ref, gu_ref, row_ref, row_two_ref,
         *rest,
     ):
         bufs, (s_send, s_receive, t_send, t_receive) = rest[:6], rest[6:10]
         (
-            came_deep, sums, parts_a, parts_b, parts_d, parts_o, scalar, back_ref, one_buf, load,
-            d_send, d_receive, p_send, p_receive,
+            came_deep, sums, parts_a, parts_b, scalar, back_ref, one_buf, load,
+            d_send, d_receive, p_send, p_receive, local,
         ) = rest[10:]
         d, c, t = place_of()
+        hand_on, landed = exchange(
+            ((sums, parts_a), (both_ref, parts_b)), held, p_send, p_receive, local
+        )
 
         def fetch(n):
             part = pl.ds(pl.multiple_of(depth(d, n + 1) * group, group), group)
@@ -1364,38 +1598,18 @@
             return pltpu.make_async_copy(one_ref.at[:, part], one_buf.at[slot], load.at[slot])
 
         fetch(0).start()
-        greet(
-            [(d, beside(c, k), t) for k in (1, 2, 3)]
-            + [(d, c, 1 - t)]
+        met = (
+            around()
+            + [(d, beside(c, 3), t)]
             + [(depth(d, k), c, t) for k in range(1, deep)]
         )
-
-        def deeper(k):
-            rows = pl.ds(pl.multiple_of(depth(d, k) * group, group), group)
+        say(met)
+
+        def deeper(n):
+            rows = pl.ds(pl.multiple_of(depth(d, n + 1) * group, group), group)
             return remote(
-                back_ref.at[rows], came_deep.at[k - 1], d_send, d_receive, k - 1,
-                (depth(d, k), c, t),
+                back_ref.at[rows], came_deep.at[n], d_send, d_receive, n, (depth(d, n + 1), c, t)
             )
-
-        jobs = ((sums, parts_a), (both_ref, parts_b), (down_ref, parts_d), (so_ref, parts_o))
-
-        def rows_of(block):
-            return pl.ds(pl.multiple_of(block * held, held), held)
-
-        def to_block(n, k):
-            source, target = jobs[n]
-            return remote(
-                source.at[rows_of(beside(c, k))], target.at[c], p_send, p_receive, 3 * n + k - 1,
-                (d, beside(c, k), t),
-            )
-
-        def from_block(n, k):
-            there = jobs[n][1].at[beside(c, k)]
-            return remote(there, there, p_send, p_receive, 3 * n + k - 1, (d, beside(c, k), t))
-
-        def at_home(n):
-            source, target = jobs[n]
-            return pltpu.make_async_copy(source.at[rows_of(c)], target.at[c], load.at[n + 1])
 
         def plane(n, carry):
             rows = pl.ds(pl.multiple_of(depth(d, n + 1) * group, group), group)
@@ -1409,14 +1623,9 @@
 
             @pl.when(n < deep - 1)
             def _():
-                remote(
-                    back_ref.at[rows], came_deep.at[n], d_send, d_receive, n,
-                    (depth(d, n + 1), c, t),
-                ).start()
+                deeper(n).start()
 
             return carry
-
-        lax.fori_loop(0, deep, plane, 0)
 
         def terms(i, start):
             part = pl.ds(start, 2 * own)
@@ -1427,52 +1636,44 @@
 
         def fill(n):
             if n == 0:
-                for job in (1, 2, 3):
-                    for k in (3, 1, 2):
-                        to_block(job, k).start()
-                    at_home(job).start()
-
-        e_one = scatter_rows(terms, bufs, s_send, s_receive, fill)
+                hand_on(1)
+                lax.fori_loop(0, deep, plane, 0)
+                return
+            landed(1)
+            gain_two = gain_two_ref[...]
+            for b in range(4):
+                whole = parts_b[b].astype(F32)
+                for ref, first, rest_of in (
+                    (gg_ref, 0, 2 * main),
+                    (gu_ref, main, main + units),
+                ):
+                    s = whole[:, first : first + main]
+                    if main < units:
+                        s = jnp.concatenate([s, whole[:, rest_of : rest_of + units - main]], axis=1)
+                    ref[:, b * units : (b + 1) * units] = s * gain_two
+            scalar[0, 1] = as_row(
+                (
+                    jnp.sum(gg_ref[...] * wg_ref[...].astype(F32), axis=1, keepdims=True)
+                    + jnp.sum(gu_ref[...] * wu_ref[...].astype(F32), axis=1, keepdims=True)
+                )
+                / gain_two
+            )
+            for m in range(deep - 1):
+                deeper(m).wait_recv()
+            mine = pl.ds(pl.multiple_of(d * group, group), group)
+            total = back_ref[mine, :].astype(F32)
+            for m in range(deep - 1):
+                total = total + came_deep[m].astype(F32)
+            sums[...] = total.astype(BF16)
+            hand_on(0)
+
+        e_one = scatter_rows(terms, bufs, s_send, s_receive, lambda: hear(len(met)), fill)
         scale, hat = norm_parts(x_ref[pl.ds(pl.multiple_of(t * own, own), own), :].astype(F32))
         place = out_ref.at[pl.ds(pl.multiple_of(t * own, own), own)]
         place[...] = gm_ref[...] + norm_back(e_one, hat, scale)
         copy = remote(place, place, t_send, t_receive, 0, (d, c, 1 - t))
         copy.start()
-
-        for n in (1, 2, 3):
-            at_home(n).wait()
-            for k in (1, 2, 3):
-                from_block(n, k).wait_recv()
-        gain_two = gain_two_ref[...]
-        for b in range(4):
-            whole = parts_b[b].astype(F32)
-            for ref, first, rest_of in (
-                (gg_ref, 0, 2 * main),
-                (gu_ref, main, main + units),
-            ):
-                s = whole[:, first : first + main]
-                if main < units:
-                    s = jnp.concatenate([s, whole[:, rest_of : rest_of + units - main]], axis=1)
-                ref[:, b * units : (b + 1) * units] = s * gain_two
-            gd_ref[:, b * units : (b + 1) * units] = parts_d[b].astype(F32)
-            go_ref[:, b * wide : (b + 1) * wide] = parts_o[b].astype(F32)
-        term_two = (
-            jnp.sum(gg_ref[...] * wg_ref[...].astype(F32), axis=1, keepdims=True)
-            + jnp.sum(gu_ref[...] * wu_ref[...].astype(F32), axis=1, keepdims=True)
-        ) / gain_two
-
-        for k in range(1, deep):
-            deeper(k).wait_recv()
-        mine = pl.ds(pl.multiple_of(d * group, group), group)
-        total = back_ref[mine, :].astype(F32)
-        for k in range(1, deep):
-            total = total + came_deep[k - 1].astype(F32)
-        sums[...] = total.astype(BF16)
-        for k in (3, 1, 2):
-            to_block(0, k).start()
-        parts_a[c] = sums[rows_of(c), :]
-        for k in (1, 2, 3):
-            from_block(0, k).wait_recv()
+        landed(0)
         gain_one = gain_ref[...]
 
         def owned(start, count):
@@ -1490,30 +1691,24 @@
             term_one = term_one + jnp.sum(s * weight[...].astype(F32), axis=1, keepdims=True)
             ref[...] = s * gain_one
         scalar[0, 0] = as_row(term_one)
-        scalar[0, 1] = as_row(term_two)
         swap = remote(scalar.at[0], scalar.at[1], t_send, t_receive, 1, (d, c, 1 - t))
         swap.start()
         swap.wait()
         row_ref[...] = (scalar[0, 0] + scalar[1, 0])[:1]
         row_two_ref[...] = (scalar[0, 1] + scalar[1, 1])[:1]
-
         copy.wait_send()
         there = out_ref.at[pl.ds(pl.multiple_of((1 - t) * own, own), own)]
         remote(there, there, t_send, t_receive, 0, (d, c, 1 - t)).wait_recv()
-        for k in range(1, deep):
-            deeper(k).wait_send()
-        for n in range(4):
-            for k in (1, 2, 3):
-                to_block(n, k).wait_send()
+        for m in range(deep - 1):
+            deeper(m).wait_send()
 
     w_q, w_k, w_v, w_gate, w_up = weights
     vmem, hbm = pl.BlockSpec(memory_space=pltpu.VMEM), pl.BlockSpec(memory_space=pl.ANY)
     return call(
         kernel, "to_input", 6,
-        (g_qkv, w_attn, x, g_middle, rows_one, sum_out, sum_both, sum_down)
-        + tuple(weights) + tuple(gains),
+        (g_qkv, w_attn, x, g_middle, rows_one, sum_both) + tuple(weights) + tuple(gains),
         [jax.ShapeDtypeStruct((2 * own, width), F32)]
-        + [jax.ShapeDtypeStruct(w.shape, F32) for w in (w_q, w_k, w_v, w_v, w_gate, w_up, w_up)]
+        + [jax.ShapeDtypeStruct(w.shape, F32) for w in weights]
         + [jax.ShapeDtypeStruct((1, held), F32)] * 2,
         scatter_scratch(own, width) + sems(SCATTER_COPIES) + sems(2)
         + [
@@ -1521,15 +1716,13 @@
             pltpu.VMEM((group, across), BF16),
             pltpu.VMEM((4, held, across), BF16),
             pltpu.VMEM((4, held, both), BF16),
-            pltpu.VMEM((4, held, units), BF16),
-            pltpu.VMEM((4, held, wide), BF16),
             pltpu.VMEM((2, 2, 8, held), F32),
             pltpu.VMEM((width, across), BF16),
             pltpu.VMEM((2, tokens, group), BF16),
-            pltpu.SemaphoreType.DMA((5,)),
+            pltpu.SemaphoreType.DMA((2,)),
         ]
-        + sems(deep - 1) + sems(12),
-        [vmem] * 4 + [hbm] * 4 + [vmem] * 7,
+        + sems(deep - 1) + sems(6) + [pltpu.SemaphoreType.DMA((2,))],
+        [vmem] * 4 + [hbm] * 2 + [vmem] * 7,
         flops=2 * tokens * width * g_qkv.shape[1],
     )
 
@@ -1570,29 +1763,34 @@
     )
     w_down = lax.all_gather(cut_down, "dp", axis=0, tiled=True).reshape(-1, cut_down.shape[2])
     middle, rows_two = to_middle(heads_out, w_attn, x)
-    hidden, slope, silu, cot_high = gate_up(rows_two, w_both, cot_block)
-    back_down = jnp.concatenate([dot(cot_low, hidden, 0, 0), dot(cot_high, hidden, 0, 0)]).astype(
-        BF16
-    )
-    w_down, back_down = lax.optimization_barrier((w_down, back_down))
+    hidden, slope, silu, cot_high, back_down = gate_up(rows_two, w_both, cot_block, cot_low)
     sum_down = lax.psum_scatter(back_down, "dp", scatter_dimension=0, tiled=True)
-    g_both, out, back_both = feed_forward(
-        hidden, slope, silu, cot_low, cot_high, middle, w_down, rows_two
-    )
+    g_both, back_both = feed_forward(slope, silu, cot_low, cot_high, w_down, rows_two)
     sum_both = lax.psum_scatter(back_both, "dp", scatter_dimension=0, tiled=True)
-    g_middle, branch, g_mixed = to_branch(g_both, w_both, middle, cot_block, w_attn, heads * DV)
-    g_qkv, sum_out = attend_back(
-        qkv, g_mixed, mixed, denom, seg_rows, seg_cols, branch, heads_out, heads
-    )
-    g_input, s_q, s_k, s_v, s_o, s_gate, s_up, s_down, attn_row, mlp_row = to_input(
+    g_middle, branch, g_mixed, out_terms = to_branch(
+        g_both, w_both, middle, cot_block, w_attn, heads * DV, hidden, w_down
+    )
+    g_qkv, out, s_o, s_down = attend_back(
+        qkv,
+        g_mixed,
+        mixed,
+        denom,
+        seg_rows,
+        seg_cols,
+        branch,
+        heads_out,
+        out_terms,
+        middle,
+        sum_down,
+        heads,
+    )
+    g_input, s_q, s_k, s_v, s_gate, s_up, attn_row, mlp_row = to_input(
         g_qkv,
         w_attn,
         x,
         g_middle,
         rows_one,
-        sum_out,
         sum_both,
-        sum_down,
         (q_weight, k_weight, v_weight, gate_weight, up_weight),
         (gain_one, gain_two),
         heads,

time: 570 us -> 539 us (0.946)
  Pallas kernels: 515 us -> 488 us
  waiting for transfers between devices: 0.13 us -> 14.4 us
  matrix products: 13.8 us -> 0 us
    pallas_call x8 -> x7, Pallas kernels: 515 us -> 461 us  [call(): pl.pallas_call(kernel, in_specs=spaces or [vmem] * len(arrays), out_specs...]
    pallas_call x0 -> x1, Pallas kernels: none -> 27.4 us  [feed_forward(): pl.pallas_call(kernel, in_specs=[hbm] * 6, out_specs=[hbm] * 2, out_shape...]
    dot_general x2 -> x0, matrix products: 13.8 us -> none  [dot(): lax.dot_general(a, b, (((ca,), (cb,)), ((), ())), preferred_element_type=...]
    all_gather x1, waiting for transfers between devices: 0.01 us -> 11.9 us  [plane_shards(): lax.all_gather(cut_down, 'dp', axis=0, tiled=True)]
  transfers between devices with their start and end apart: 4 -> 4, of which waited for: 0 -> 2; matrix products, arithmetic and copies ran while one was open for 4% -> 0% of each run, Pallas kernels for 61% -> 64%
where the time goes in v4:
time: 539 us; the launch traced here: 534 us
  Pallas kernels  488 us (91%)
  local copies, waits for them, and re-layouts  15.8 us (3%)
  waiting for transfers between devices  14.4 us (3%)
  between operations  14.2 us (3%)
    pallas_call x7, Pallas kernels, call(): pl.pallas_call(kernel, in_specs=spaces or [vmem] * len(arrays), out_specs...  461 us
    pallas_call x1, Pallas kernels, feed_forward(): pl.pallas_call(kernel, in_specs=[hbm] * 6, out_specs=[hbm] * 2, out_shape...  27.4 us
    unnamed x33, local copies, waits for them, and re-layouts  12.3 us
    all_gather x1, waiting for transfers between devices, plane_shards(): lax.all_gather(cut_down, 'dp', axis=0, tiled=True)  11.9 us
  transfers between devices with their start and end apart: 4, of which 2 were waited for; matrix products, arithmetic and copies ran while one was open for 0% of the time, Pallas kernels for 64%

profile of v4, /device:TPU:0, one launch (start us, length us, event | category | flops | bytes accessed | tf_op | source)
XLA Modules:
  0.0 534.3 jit_solution(9942910920901911865)
XLA Ops:
  7.2 0.0 all-gather.3.cloned.1.call-start
  7.2 0.7 bitcast_convert_fusion.1
  7.9 0.7 bitcast_convert_fusion
  8.5 0.7 copy.34.two_ref.gain_two_ref
  9.3 0.7 copy.33.one_ref.gain_ref
  10.0 68.3 %front.1 = (bf16[2048,2048]{1,0:T(8,128)(2,1)}, s32[4,1,512]{2,1,0:T(1,128)}, bf16[4,4,128,576]{3,2,1,0:T(8,128)(2,1)}, bf16[4,128,1408]{2,1,0:T(8,128)(2,1)}) custom-call(bf16[512,2048]{1,0:T(8,128)(2,1)} %bitcast.22, s32[1,1,512]{2,1,0:T(1,128)} %bitcast.33, bf16[128,128]{1,0:T(8,128)(2,1)} %wq_ref.1, bf16[128,128]{1,0:T(8,128)(2,1)} %wk_ref.1, ...), custom_call_target="tpu_custom_call" | custom-call | bytes 4131840 | tf_op jit(solution)/shard_map/front/pallas_call | solution.py:647
  78.4 0.0 all-gather.3.cloned.1.call-update
  78.4 0.0 all-gather.5.cloned.1.call-start
  78.4 2.0 copy.35.row_ref
  80.5 40.3 %attend.1 = (bf16[2048,320]{1,0:T(8,128)(2,1)}, f32[2048,256]{1,0:T(8,128)}, f32[2048,2]{1,0:T(8,128)}, bf16[2048,256]{1,0:T(8,128)(2,1)}, bf16[2048,1024]{1,0:T(8,128)(2,1)}, /*index=5*/bf16[4,128,768]{2,1,0:T(8,128)(2,1)}) custom-call(bf16[2048,2048]{1,0:T(8,128)(2,1)} %get-tuple-element.46.x_ref.one_ref, bf16[2048,576]{1,0:T(8,128)(2,1)} %bitcast.18, ...), custom_call_target="tpu_custom_call" | custom-call | bytes 13582336 | tf_op jit(solution)/shard_map/attend/pallas_call | solution.py:647
  120.7 0.0 all-gather.5.cloned.1.call-update
  120.8 0.2 reduce-scatter.3.cloned.1.call-start
  121.0 81.3 %to_middle.1 = (f32[256,2048]{1,0:T(8,128)}, bf16[2048,2048]{1,0:T(8,128)(2,1)}) custom-call(bf16[2048,256]{1,0:T(8,128)(2,1)} %get-tuple-element.50.h_ref, bf16[2048,576]{1,0:T(8,128)(2,1)} %bitcast.19, bf16[512,2048]{1,0:T(8,128)(2,1)} %bitcast.23), custom_call_target="tpu_custom_call" | custom-call | flops 2147483648 | bytes 5505024 | tf_op jit(solution)/shard_map/to_middle/pallas_call | solution.py:647
  202.3 0.0 all-gather.3.cloned.1.call-done
  202.3 39.8 %gate_up.1 = (bf16[2048,704]{1,0:T(8,128)(2,1)}, bf16[2048,704]{1,0:T(8,128)(2,1)}, bf16[2048,704]{1,0:T(8,128)(2,1)}, bf16[2048,1024]{1,0:T(8,128)(2,1)}, bf16[2048,704]{1,0:T(8,128)(2,1)}) custom-call(bf16[2048,2048]{1,0:T(8,128)(2,1)} %get-tuple-element.51.x_ref.two_ref, bf16[2048,1408]{1,0:T(8,128)(2,1)} %bitcast.34, bf16[512,2048]{1,0:T(8,128)(2,1)} %bitcast.27, ...), custom_call_target="tpu_custom_call" | custom-call | flops 11811160064 | bytes 20447232 | tf_op jit(solution)/shard_map/gate_up/pallas_call | solution.py:647
  242.2 0.0 reduce-scatter.3.cloned.1.call-update
  242.2 0.0 reduce-scatter.5.cloned.1.call-start
  242.3 11.9 %all-gather.5.cloned.1.call-done = bf16[16,128,768]{2,1,0:T(8,128)(2,1)} async-done(((bf16[4,128,768]{2,1,0:T(8,128)(2,1)}), bf16[16,128,768]{2,1,0:T(8,128)(2,1)}) %all-gather.5.cloned.1.call-update) | async-done | bytes 3145744 | tf_op jit(solution)/shard_map/all_gather | solution.py:1764
  254.2 27.4 %feed_forward.1 = (bf16[2048,1408]{1,0:T(8,128)(2,1)}, bf16[2048,1408]{1,0:T(8,128)(2,1)}) custom-call(bf16[2048,704]{1,0:T(8,128)(2,1)} %get-tuple-element.54.slope_ref, bf16[2048,704]{1,0:T(8,128)(2,1)} %get-tuple-element.55.silu_ref, bf16[2048,1024]{1,0:T(8,128)(2,1)} %get-tuple-element.53.low_ref, bf16[2048,1024]{1,0:T(8,128)(2,1)} %get-tuple-element.56.high_ref, ...), custom_call_target="tpu_custom_call" | custom-call | flops 17716740096 | bytes 36962304 | tf_op jit(solution)/shard_map/feed_forward/pallas_call | solution.py:1418
  281.6 0.0 reduce-scatter.5.cloned.1.call-update
  281.6 92.5 %to_branch.1 = (f32[256,2048]{1,0:T(8,128)}, bf16[2048,2048]{1,0:T(8,128)(2,1)}, bf16[2048,256]{1,0:T(8,128)(2,1)}, bf16[2048,2048]{1,0:T(8,128)(2,1)}) custom-call(bf16[2048,1408]{1,0:T(8,128)(2,1)} %get-tuple-element.58.g_ref, bf16[2048,1408]{1,0:T(8,128)(2,1)} %bitcast.35, f32[256,2048]{1,0:T(8,128)} %get-tuple-element.59.mid_ref, ...), custom_call_target="tpu_custom_call" | custom-call | flops 16106127360 | bytes 24117248 | tf_op jit(solution)/shard_map/to_branch/pallas_call | solution.py:647
  374.1 0.0 reduce-scatter.3.cloned.1.call-done.down_ref
  374.1 60.2 %attend_back.1 = (bf16[2048,320]{1,0:T(8,128)(2,1)}, bf16[512,2048]{1,0:T(8,128)(2,1)}, f32[128,1024]{1,0:T(8,128)}, f32[128,2816]{1,0:T(8,128)}) custom-call(bf16[2048,320]{1,0:T(8,128)(2,1)} %get-tuple-element.49.x_ref, bf16[2048,256]{1,0:T(8,128)(2,1)} %get-tuple-element.61.gm_ref, f32[2048,256]{1,0:T(8,128)} %get-tuple-element.62.m_ref, ...), custom_call_target="tpu_custom_call" | custom-call | bytes 25133056 | tf_op jit(solution)/shard_map/attend_back/pallas_call | solution.py:647
  434.3 2.4 reduce-scatter.5.cloned.1.call-done.both_ref
  436.7 78.4 %to_input.1 = (f32[512,2048]{1,0:T(8,128)}, f32[128,128]{1,0:T(8,128)}, f32[128,128]{1,0:T(8,128)}, f32[128,1024]{1,0:T(8,128)}, f32[128,2816]{1,0:T(8,128)}, /*...) custom-call(bf16[2048,320]{1,0:T(8,128)(2,1)} %get-tuple-element.68.g_ref, bf16[2048,576]{1,0:T(8,128)(2,1)} %bitcast.21, ...), custom_call_target="tpu_custom_call" | custom-call | flops 2684354560 | bytes 19465216 | tf_op jit(solution)/shard_map/to_input/pallas_call | solution.py:647
  515.2 0.0 copy-start
  515.2 0.0 copy-done.1
  515.2 1.3 copy.50
  516.5 1.6 copy-done
  518.1 0.0 copy-start.4
  518.1 2.1 copy.51
  520.3 0.0 copy-done.8
  520.3 0.6 copy.52
  520.9 0.0 copy-done.7
  520.9 0.6 copy.53
  521.5 0.0 copy-done.6
  521.5 0.8 copy.54
  522.3 0.0 copy-done.5
  522.3 0.8 copy.55
  523.1 0.0 copy-done.4
  523.1 1.1 copy.56
  524.2 0.0 copy-done.3
  524.2 1.1 copy.57
  525.3 0.0 copy-done.2
  525.3 1.1 copy.58
  526.4 0.0 copy-done.10
  526.4 0.5 copy.59
  527.0 0.5 copy.60
  (10 shorter events, 0.0 us)
Async XLA Ops:
  7.2 195.1 %all-gather.3.cloned.1.call-start = ((), (), s32[]{:S(2)}) async-start(), calls=%async_computation.2 | async-start | bytes 7208960 | tf_op jit(solution)/shard_map/all_gather | solution.py:1759
  78.4 175.8 %all-gather.5.cloned.1.call-start = ((), (), s32[]{:S(2)}) async-start(), calls=%async_computation.3 | async-start | bytes 3932160 | tf_op jit(solution)/shard_map/all_gather | solution.py:1764
  120.8 253.3 %reduce-scatter.3.cloned.1.call-start = ((), (), s32[]{:S(2)}) async-start(), calls=%async_computation.4 | async-start | bytes 3932160 | tf_op jit(solution)/shard_map/reduce_scatter | solution.py:1767
  242.2 194.5 %reduce-scatter.5.cloned.1.call-start = ((), (), s32[]{:S(2)}) async-start(), calls=%async_computation.5 | async-start | bytes 7208960 | tf_op jit(solution)/shard_map/reduce_scatter | solution.py:1769
  436.7 78.5 %copy-start.1 = (bf16[512,2048]{1,0:T(8,128)(2,1)S(1)}, bf16[512,2048]{1,0:T(8,128)(2,1)}, u32[]{:S(2)}) copy-start(bf16[512,2048]{1,0:T(8,128)(2,1)} %get-tuple-element.67) | copy-start | bytes 6291460
  515.2 2.9 copy-start
  518.1 2.2 copy-start.8
  518.1 2.8 copy-start.7
  518.1 3.4 copy-start.6
  518.1 4.2 copy-start.5
  518.1 5.0 copy-start.4
  520.3 4.0 copy-start.3
  523.1 2.2 copy-start.2
  524.2 2.2 copy-start.10
  524.2 2.7 copy-start.9
Sparse Core Ops, SparseCore 0:
  78.5 112.1 all-gather.2
  192.3 61.7 all-gather.4
  256.5 58.8 reduce-scatter.2
  317.6 119.1 reduce-scatter.4

commit v5 on v4

--- a/solution.py
+++ b/solution.py
@@ -1,3 +1,5 @@
+import functools
+
 import jax
 import jax.numpy as jnp
 from jax import lax
@@ -370,14 +372,10 @@
     )
 
 
-def gather_rows(
-    buf, out, send, receive, store, piece=None, early=None, middle=None, late=None
-):
+def gather_steps(buf, send, receive):
     d, c, t = place_of()
     own = buf.shape[0] // 8
     half = own // 2
-    to_x, to_y, to_t = (d, beside(c, 1), t), (d, beside(c, 2), t), (d, c, 1 - t)
-    started = []
 
     def part(across, core, h):
         block = c if across == 0 else beside(c, across)
@@ -388,7 +386,32 @@
         ref = part(across, t, h)
         copy = remote(ref, ref, send, receive, k, device)
         copy.start()
-        started.append(copy)
+        return copy
+
+    return put, part
+
+
+def gather_begin(buf, send, receive):
+    put, _ = gather_steps(buf, send, receive)
+    to_x, to_y, to_t = around()
+    return [
+        put(0, 0, 0, to_x),
+        put(1, 0, 1, to_y),
+        put(2, 0, 1, to_x),
+        put(3, 0, 0, to_y),
+        put(6, 0, 0, to_t),
+        put(7, 0, 1, to_t),
+    ]
+
+
+def gather_rows(
+    buf, out, send, receive, store, piece=None, early=None, middle=None, late=None, begun=None
+):
+    d, c, t = place_of()
+    own = buf.shape[0] // 8
+    to_x, to_y, to_t = around()
+    put, part = gather_steps(buf, send, receive)
+    started = gather_begin(buf, send, receive) if begun is None else begun
 
     def got(k, across, core, h):
         ref = part(across, core, h)
@@ -406,12 +429,6 @@
         if piece is not None:
             piece(start)
 
-    put(0, 0, 0, to_x)
-    put(1, 0, 1, to_y)
-    put(2, 0, 1, to_x)
-    put(3, 0, 0, to_y)
-    put(6, 0, 0, to_t)
-    put(7, 0, 1, to_t)
     if early is not None:
         early()
     work(0, t)
@@ -419,17 +436,17 @@
     got(7, 0, 1 - t, 1)
     work(0, 1 - t)
     got(0, 1, t, 0)
-    put(4, 1, 0, to_y)
-    put(8, 1, 0, to_t)
+    started.append(put(4, 1, 0, to_y))
+    started.append(put(8, 1, 0, to_t))
     got(1, 2, t, 1)
-    put(5, 2, 1, to_x)
-    put(9, 2, 1, to_t)
+    started.append(put(5, 2, 1, to_x))
+    started.append(put(9, 2, 1, to_t))
     if middle is not None:
         middle()
     got(2, 1, t, 1)
-    put(10, 1, 1, to_t)
+    started.append(put(10, 1, 1, to_t))
     got(3, 2, t, 0)
-    put(11, 2, 0, to_t)
+    started.append(put(11, 2, 0, to_t))
     if late is not None:
         late()
     work(1, t)
@@ -441,9 +458,9 @@
     got(11, 2, 1 - t, 0)
     work(2, 1 - t)
     got(4, 3, t, 0)
-    put(12, 3, 0, to_t)
+    started.append(put(12, 3, 0, to_t))
     got(5, 3, t, 1)
-    put(13, 3, 1, to_t)
+    started.append(put(13, 3, 1, to_t))
     work(3, t)
     got(12, 3, 1 - t, 0)
     got(13, 3, 1 - t, 1)
@@ -687,17 +704,30 @@
     wide, narrow = heads * DV, heads * F
     main = units // 128 * 128
     packed = 2 * wide + 2 * narrow
+    part_width = width // 2
+    filled = whole_tiles(units)
+    line = {
+        0: (((0, 2),), ((0, 1),), ()),
+        1: (((1, 0),), ((1, 2), (1, 3)), ((3, 0),)),
+        2: (((2, 3),), ((2, 1), (2, 0)), ((0, 3),)),
+        3: (((3, 1),), ((3, 2),), ()),
+    }
+    if deep != 4:
+        line = {
+            p: (tuple((p, to) for to in range(deep) if to != p), (), ()) for p in range(deep)
+        }
 
     def kernel(
-        x_ref, seg_ref, q_ref, k_ref, v_ref, o_ref, g_ref, u_ref, one_ref, two_ref,
-        rows_out, segs_ref, wa_out, wg_out,
-        cut_a, cut_g, rows_ref, send, receive, store, small_send, small_receive, deep_send, deep_receive, here,
+        x_ref, seg_ref, q_ref, k_ref, v_ref, o_ref, g_ref, u_ref, d_ref, one_ref, two_ref,
+        rows_out, own_ref, segs_ref, wa_out, wg_out, wd_out,
+        cut_a, cut_g, cut_d, rows_ref, send, receive, store, small_send, small_receive, deep_send, deep_receive, here,
     ):
         d, c, t = place_of()
         jobs = (
             (lambda block: cut_a.at[block], lambda block: wa_out.at[d, block]),
             (lambda block: seg_ref.at[0], lambda block: segs_ref.at[block]),
             (lambda block: cut_g.at[block], lambda block: wg_out.at[block]),
+            (lambda block: cut_d.at[block], lambda block: wd_out.at[block]),
         )
 
         def local(n):
@@ -716,14 +746,33 @@
                 3 * n + k - 1, (d, block, t),
             )
 
-        def along(k):
-            return remote(
-                wa_out.at[d], wa_out.at[d], deep_send, deep_receive, k - 1, (depth(d, k), c, t)
+        def shard(slot, s, to):
+            return pltpu.make_async_remote_copy(
+                src_ref=wa_out.at[s], dst_ref=wa_out.at[s], send_sem=deep_send.at[slot],
+                recv_sem=deep_receive.at[s], device_id=(to, c, t), device_id_type=MESH,
             )
 
-        def from_depth(k):
-            there = wa_out.at[depth(d, deep - k)]
-            return remote(there, there, deep_send, deep_receive, k - 1, (depth(d, k), c, t))
+        def in_plane(act):
+            for p in range(deep):
+                pl.when(d == p)(functools.partial(act, p, *line[p]))
+
+        def first_shards(p, first, then, on):
+            for slot, (s, to) in enumerate(first):
+                shard(slot, s, to).start()
+
+        def other_shards(p, first, then, on):
+            for slot, (s, to) in enumerate(then):
+                shard(len(first) + slot, s, to).start()
+            for slot, (s, to) in enumerate(on):
+                shard(len(first) + len(then) + slot, s, to).wait_recv()
+                shard(len(first) + len(then) + slot, s, to).start()
+
+        def end_shards(p, first, then, on):
+            for s in range(deep):
+                if s != p and s not in [handed for handed, _ in on]:
+                    shard(0, s, (p + 1) % deep).wait_recv()
+            for slot, (s, to) in enumerate(first + then + on):
+                shard(slot, s, to).wait_send()
 
         one, two = one_ref[...], two_ref[...]
         met = (
@@ -744,7 +793,12 @@
             out(0, k).start()
         mine = pl.multiple_of((2 * c + t) * own, own)
         _, hat = norm_parts(x_ref[pl.ds(pl.multiple_of(t * own, own), own), :].astype(F32))
-        rows_ref[pl.ds(mine, own), :] = hat.astype(BF16)
+        rows_ref[pl.ds(mine, own), :] = hat[:, :part_width].astype(BF16)
+        own_ref[...] = hat[:, part_width:].astype(BF16)
+        local(0).wait()
+        for k in (1, 2, 3):
+            arrival(0, k).wait_recv()
+        in_plane(first_shards)
 
         def early():
             for b in range(4):
@@ -756,28 +810,32 @@
                         [columns(r, two, start + main, units - main) for r in (g_ref, u_ref)],
                         axis=1,
                     ).astype(BF16)
-            local(0).wait()
-            for k in (1, 2, 3):
-                arrival(0, k).wait_recv()
-            for k in range(1, deep):
-                along(k).start()
+
             for n in (1, 2):
                 local(n).start()
                 for k in (3, 1, 2):
                     out(n, k).start()
-
-        gather_rows(rows_ref, rows_out, send, receive, store, early=early)
-        for n in (1, 2):
+            for b in range(4):
+                part = columns(d_ref, None, b * units, units)
+                if units < filled:
+                    part = jnp.concatenate([part, jnp.zeros((held, filled - units), F32)], axis=1)
+                cut_d[b] = part.astype(BF16)
+            local(3).start()
+            for k in (3, 1, 2):
+                out(3, k).start()
+
+        gather_rows(
+            rows_ref, rows_out, send, receive, store, early=early,
+            middle=lambda: in_plane(other_shards),
+        )
+        for n in (1, 2, 3):
             local(n).wait()
             for k in (1, 2, 3):
                 arrival(n, k).wait_recv()
-        for k in range(1, deep):
-            from_depth(k).wait_recv()
-        for n in range(3):
+        in_plane(end_shards)
+        for n in range(4):
             for k in (1, 2, 3):
                 out(n, k).wait_send()
-        for k in range(1, deep):
-            along(k).wait_send()
 
     vmem, hbm = pl.BlockSpec(memory_space=pltpu.VMEM), pl.BlockSpec(memory_space=pl.ANY)
     return call(
@@ -786,18 +844,21 @@
         1,
         (x, seg[None]) + tuple(weights) + tuple(gains),
         [
-            jax.ShapeDtypeStruct((tokens, width), BF16),
+            jax.ShapeDtypeStruct((tokens, part_width), BF16),
+            jax.ShapeDtypeStruct((own, part_width), BF16),
             jax.ShapeDtypeStruct((4,) + seg.shape, seg.dtype),
             jax.ShapeDtypeStruct((deep, 4, held, packed), BF16),
             jax.ShapeDtypeStruct((4, held, 2 * units), BF16),
+            jax.ShapeDtypeStruct((4, held, filled), BF16),
         ],
         [
             pltpu.VMEM((4, held, packed), BF16),
             pltpu.VMEM((4, held, 2 * units), BF16),
+            pltpu.VMEM((4, held, filled), BF16),
         ]
-        + gather_scratch(tokens, width) + sems(9) + sems(deep - 1) + [pltpu.SemaphoreType.DMA((3,))],
-        [vmem, hbm] + [vmem] * 8,
-        [hbm, hbm, hbm, hbm],
+        + gather_scratch(tokens, part_width) + sems(12) + sems(deep) + [pltpu.SemaphoreType.DMA((4,))],
+        [vmem, hbm] + [vmem] * 9,
+        [hbm, vmem, hbm, hbm, hbm, hbm],
     )
 
 
@@ -1051,42 +1112,62 @@
         denom_ref[pl.ds(base, BLOCK), h : h + 1] = denom[:, :1]
 
 
-def attend(rows_one, w_attn, seg_rows, seg_cols, cot, w_down, heads):
-    tokens, width = rows_one.shape
+def attend(rows_low, own_high, w_attn, seg_rows, seg_cols, cot, heads):
+    tokens, part_width = rows_low.shape
     own = tokens // 8
     wide, narrow = heads * DV, heads * F
-    held, units = w_down.shape[0], w_down.shape[1] // 4
-    filled = whole_tiles(units)
 
     def kernel(
-        x_ref, w_ref, row_ref, col_ref, cot_ref, d_ref,
-        qkv_ref, mixed_ref, denom_ref, low_ref, rows_out, wd_out,
-        ext_ref, cut, rows_ref, send, receive, store, d_send, d_receive, here,
+        x_ref, own_ref, w_ref, row_ref, col_ref, cot_ref,
+        qkv_ref, mixed_ref, denom_ref, low_ref, cot_out, rows_out,
+        ext_ref, half_ref, here, x_buf, *rest,
     ):
+        rows_ref, r_send, r_receive, r_store, cot_buf, c_send, c_receive, c_store = rest
         d, c, t = place_of()
-
-        def out(k):
-            return remote(
-                cut.at[beside(c, k)], wd_out.at[c], d_send, d_receive, k - 1, (d, beside(c, k), t)
-            )
-
-        def arrival(k):
-            there = wd_out.at[beside(c, k)]
-            return remote(there, there, d_send, d_receive, k - 1, (d, beside(c, k), t))
-
-        local = pltpu.make_async_copy(cut.at[c], wd_out.at[c], here.at[0])
-        met = [(d, beside(c, k), t) for k in (1, 2, 3)] + [(d, c, 1 - t)]
+        loaded = pltpu.make_async_copy(x_ref, x_buf, here.at[0])
+        loaded.start()
+        low_half = pltpu.make_async_copy(x_buf, rows_out.at[:, :part_width], here.at[1])
+
+        met = around()
         say(met)
-        for b in range(4):
-            part = columns(d_ref, None, b * units, units)
-            if units < filled:
-                part = jnp.concatenate([part, jnp.zeros((held, filled - units), F32)], axis=1)
-            cut[b] = part.astype(BF16)
-        mine = pl.multiple_of((2 * c + t) * own, own)
+        mine = pl.ds(pl.multiple_of((2 * c + t) * own, own), own)
+        rows_ref[mine, :] = own_ref[...]
+        cot_buf[mine, :] = cot_ref[pl.ds(pl.multiple_of(t * own, own), own), :part_width]
         hear(len(met))
-        rows_ref[pl.ds(mine, own), :] = cot_ref[
-            pl.ds(pl.multiple_of(t * own, own), own), : width // 2
-        ]
+
+        def first_half():
+            loaded.wait()
+
+            @pl.loop(0, tokens // BLOCK)
+            def _(n):
+                rows = pl.ds(pl.multiple_of(n * BLOCK, BLOCK), BLOCK)
+                half_ref[rows, :wide] = dot(x_buf[rows, :], w_ref[:part_width, :wide], 1, 0)
+                half_ref[rows, wide:] = dot(x_buf[rows, :], w_ref[:part_width, 2 * wide :], 1, 0)
+
+            low_half.start()
+
+        def second_half(start):
+            rows = pl.ds(start, own)
+            values = (
+                half_ref[rows, :wide] + dot(rows_ref[rows, :], w_ref[part_width:, :wide], 1, 0)
+            ).astype(BF16)
+            qkv_ref[rows, :wide] = values
+            qkv_ref[rows, wide:] = (
+                half_ref[rows, wide:] + dot(rows_ref[rows, :], w_ref[part_width:, 2 * wide :], 1, 0)
+            ).astype(BF16)
+            for h in range(heads):
+                ext_ref[rows, 2 * h * DV : (2 * h + 1) * DV] = values[:, h * DV : (h + 1) * DV]
+                ext_ref[rows, (2 * h + 1) * DV : (2 * h + 2) * DV] = jnp.ones((own, DV), BF16)
+
+        begun = []
+
+        def cot_begin():
+            begun.extend(gather_begin(cot_buf, c_send, c_receive))
+
+        gather_rows(
+            rows_ref, rows_out.at[:, part_width:], r_send, r_receive, r_store, second_half, first_half,
+            late=cot_begin,
+        )
 
         def blocks(first, last):
             @pl.loop(first, last)
@@ -1095,46 +1176,34 @@
                     i, qkv_ref, ext_ref, row_ref, col_ref, mixed_ref, denom_ref, low_ref, heads
                 )
 
-        def early():
-            local.start()
-            for k in (3, 1, 2):
-                out(k).start()
-
-            @pl.loop(0, tokens // BLOCK)
-            def _(n):
-                rows = pl.ds(pl.multiple_of(n * BLOCK, BLOCK), BLOCK)
-                values = dot(x_ref[rows, :], w_ref[:, :wide], 1, 0).astype(BF16)
-                qkv_ref[rows, :wide] = values
-                qkv_ref[rows, wide:] = dot(x_ref[rows, :], w_ref[:, 2 * wide :], 1, 0).astype(BF16)
-                for h in range(heads):
-                    ext_ref[rows, 2 * h * DV : (2 * h + 1) * DV] = values[:, h * DV : (h + 1) * DV]
-                    ext_ref[rows, (2 * h + 1) * DV : (2 * h + 2) * DV] = jnp.ones((BLOCK, DV), BF16)
-
         gather_rows(
-            rows_ref, rows_out, send, receive, store, early=early,
-            middle=lambda: blocks(0, tokens // BLOCK // 2),
-            late=lambda: blocks(tokens // BLOCK // 2, tokens // BLOCK),
+            cot_buf, cot_out, c_send, c_receive, c_store, begun=begun,
+            early=lambda: blocks(0, tokens // BLOCK // 2),
+            middle=lambda: blocks(tokens // BLOCK // 2, tokens // BLOCK - 1),
+            late=lambda: blocks(tokens // BLOCK - 1, tokens // BLOCK),
         )
-        local.wait()
-        for k in (1, 2, 3):
-            arrival(k).wait_recv()
-            out(k).wait_send()
+        low_half.wait()
 
     vmem, hbm = pl.BlockSpec(memory_space=pltpu.VMEM), pl.BlockSpec(memory_space=pl.ANY)
     return call(
-        kernel, "attend", 2, (rows_one, w_attn, seg_rows, seg_cols, cot, w_down),
+        kernel, "attend", 2, (rows_low, own_high, w_attn, seg_rows, seg_cols, cot),
         [
             jax.ShapeDtypeStruct((tokens, wide + 2 * narrow), BF16),
             jax.ShapeDtypeStruct((tokens, wide), F32),
             jax.ShapeDtypeStruct((tokens, heads), F32),
             jax.ShapeDtypeStruct((tokens, wide), BF16),
-            jax.ShapeDtypeStruct((tokens, width // 2), BF16),
-            jax.ShapeDtypeStruct((4, held, filled), BF16),
+            jax.ShapeDtypeStruct((tokens, part_width), BF16),
+            jax.ShapeDtypeStruct((tokens, 2 * part_width), BF16),
         ],
-        [pltpu.VMEM((tokens, 2 * wide), BF16), pltpu.VMEM((4, held, filled), BF16)]
-        + gather_scratch(tokens, width // 2) + sems(3) + [pltpu.SemaphoreType.DMA((1,))],
-        None,
-        [vmem] * 4 + [hbm, hbm],
+        [
+            pltpu.VMEM((tokens, 2 * wide), BF16),
+            pltpu.VMEM((tokens, wide + 2 * narrow), F32),
+            pltpu.SemaphoreType.DMA((2,)),
+            pltpu.VMEM((tokens, part_width), BF16),
+        ]
+        + gather_scratch(tokens, part_width) + gather_scratch(tokens, part_width),
+        [hbm] + [vmem] * 5,
+        [vmem] * 4 + [hbm] * 2,
     )
 
 
@@ -1585,7 +1654,7 @@
         bufs, (s_send, s_receive, t_send, t_receive) = rest[:6], rest[6:10]
         (
             came_deep, sums, parts_a, parts_b, scalar, back_ref, one_buf, load,
-            d_send, d_receive, p_send, p_receive, local,
+            d_send, d_receive, p_send, p_receive, local, x_buf, gm_buf, gate_buf, up_buf, in_buf, large,
         ) = rest[10:]
         d, c, t = place_of()
         hand_on, landed = exchange(
@@ -1598,6 +1667,18 @@
             return pltpu.make_async_copy(one_ref.at[:, part], one_buf.at[slot], load.at[slot])
 
         fetch(0).start()
+        mine = pl.ds(pl.multiple_of(t * own, own), own)
+        loads = (
+            pltpu.make_async_copy(x_ref.at[mine], x_buf, large.at[0]),
+            pltpu.make_async_copy(gm_ref, gm_buf, large.at[1]),
+        )
+        stores = (
+            pltpu.make_async_copy(gate_buf, gg_ref, large.at[2]),
+            pltpu.make_async_copy(up_buf, gu_ref, large.at[3]),
+            pltpu.make_async_copy(in_buf, out_ref.at[mine], large.at[4]),
+        )
+        for copy in loads:
+            copy.start()
         met = (
             around()
             + [(d, beside(c, 3), t)]
@@ -1644,8 +1725,8 @@
             for b in range(4):
                 whole = parts_b[b].astype(F32)
                 for ref, first, rest_of in (
-                    (gg_ref, 0, 2 * main),
-                    (gu_ref, main, main + units),
+                    (gate_buf, 0, 2 * main),
+                    (up_buf, main, main + units),
                 ):
                     s = whole[:, first : first + main]
                     if main < units:
@@ -1653,26 +1734,30 @@
                     ref[:, b * units : (b + 1) * units] = s * gain_two
             scalar[0, 1] = as_row(
                 (
-                    jnp.sum(gg_ref[...] * wg_ref[...].astype(F32), axis=1, keepdims=True)
-                    + jnp.sum(gu_ref[...] * wu_ref[...].astype(F32), axis=1, keepdims=True)
+                    jnp.sum(gate_buf[...] * wg_ref[...].astype(F32), axis=1, keepdims=True)
+                    + jnp.sum(up_buf[...] * wu_ref[...].astype(F32), axis=1, keepdims=True)
                 )
                 / gain_two
             )
+            stores[0].start()
+            stores[1].start()
             for m in range(deep - 1):
                 deeper(m).wait_recv()
-            mine = pl.ds(pl.multiple_of(d * group, group), group)
-            total = back_ref[mine, :].astype(F32)
+            kept_rows = pl.ds(pl.multiple_of(d * group, group), group)
+            total = back_ref[kept_rows, :].astype(F32)
             for m in range(deep - 1):
                 total = total + came_deep[m].astype(F32)
             sums[...] = total.astype(BF16)
             hand_on(0)
 
         e_one = scatter_rows(terms, bufs, s_send, s_receive, lambda: hear(len(met)), fill)
-        scale, hat = norm_parts(x_ref[pl.ds(pl.multiple_of(t * own, own), own), :].astype(F32))
-        place = out_ref.at[pl.ds(pl.multiple_of(t * own, own), own)]
-        place[...] = gm_ref[...] + norm_back(e_one, hat, scale)
-        copy = remote(place, place, t_send, t_receive, 0, (d, c, 1 - t))
+        for copy in loads:
+            copy.wait()
+        scale, hat = norm_parts(x_buf[...].astype(F32))
+        in_buf[...] = gm_buf[...] + norm_back(e_one, hat, scale)
+        copy = remote(in_buf, out_ref.at[mine], t_send, t_receive, 0, (d, c, 1 - t))
         copy.start()
+        stores[2].start()
         landed(0)
         gain_one = gain_ref[...]
 
@@ -1701,6 +1786,8 @@
         remote(there, there, t_send, t_receive, 0, (d, c, 1 - t)).wait_recv()
         for m in range(deep - 1):
             deeper(m).wait_send()
+        for copy in stores:
+            copy.wait()
 
     w_q, w_k, w_v, w_gate, w_up = weights
     vmem, hbm = pl.BlockSpec(memory_space=pltpu.VMEM), pl.BlockSpec(memory_space=pl.ANY)
@@ -1721,8 +1808,18 @@
             pltpu.VMEM((2, tokens, group), BF16),
             pltpu.SemaphoreType.DMA((2,)),
         ]
-        + sems(deep - 1) + sems(6) + [pltpu.SemaphoreType.DMA((2,))],
-        [vmem] * 4 + [hbm] * 2 + [vmem] * 7,
+        + sems(deep - 1) + sems(6)
+        + [
+            pltpu.SemaphoreType.DMA((2,)),
+            pltpu.VMEM((own, width), BF16),
+            pltpu.VMEM((own, width), F32),
+            pltpu.VMEM(w_gate.shape, F32),
+            pltpu.VMEM(w_up.shape, F32),
+            pltpu.VMEM((own, width), F32),
+            pltpu.SemaphoreType.DMA((5,)),
+        ],
+        [vmem] * 2 + [hbm] * 4 + [vmem] * 7,
+        [hbm] + [vmem] * 3 + [hbm] * 2 + [vmem] * 2,
         flops=2 * tokens * width * g_qkv.shape[1],
     )
 
@@ -1747,10 +1844,10 @@
     x, cot_block = activations[0], cotangent[0]
     gain_one = attn_gain.astype(F32)[:, None]
     gain_two = mlp_gain.astype(F32)[:, None]
-    rows_one, segments, w_attn, cut_both = front(
+    rows_low, own_high, segments, w_attn, cut_both, cut_down = front(
         x,
         seg_ids,
-        (q_weight, k_weight, v_weight, o_weight, gate_weight, up_weight),
+        (q_weight, k_weight, v_weight, o_weight, gate_weight, up_weight, down_weight),
         (gain_one, gain_two),
         tokens,
         heads,
@@ -1758,9 +1855,10 @@
     w_attn = w_attn.reshape(-1, w_attn.shape[3])
     w_both = lax.all_gather(cut_both, "dp", axis=0, tiled=True).reshape(-1, cut_both.shape[2])
     seg_rows, seg_cols = segments.reshape(tokens, 1), segments.reshape(1, tokens)
-    qkv, mixed, denom, heads_out, cot_low, cut_down = attend(
-        rows_one, w_attn, seg_rows, seg_cols, cot_block, down_weight, heads
-    )
+    qkv, mixed, denom, heads_out, cot_low, rows_one = attend(
+        rows_low, own_high, w_attn, seg_rows, seg_cols, cot_block, heads
+    )
+    cut_down, heads_out = lax.optimization_barrier((cut_down, heads_out))
     w_down = lax.all_gather(cut_down, "dp", axis=0, tiled=True).reshape(-1, cut_down.shape[2])
     middle, rows_two = to_middle(heads_out, w_attn, x)
     hidden, slope, silu, cot_high, back_down = gate_up(rows_two, w_both, cot_block, cot_low)

time: 539 us -> 528 us (0.980)
  waiting for transfers between devices: 14.4 us -> 3.58 us
    all_gather x1, waiting for transfers between devices: 11.9 us -> 1.04 us  [plane_shards(): lax.all_gather(cut_down, 'dp', axis=0, tiled=True)]
  transfers between devices with their start and end apart: 4 -> 4, of which waited for: 2 -> 2; matrix products, arithmetic and copies ran while one was open for 0% -> 0% of each run, Pallas kernels for 64% -> 67%
where the time goes in v5:
time: 528 us; the launch traced here: 520 us
  Pallas kernels  485 us (92%)
  local copies, waits for them, and re-layouts  15.8 us (3%)
  between operations  14.1 us (3%)
    pallas_call x7, Pallas kernels, call(): pl.pallas_call(kernel, in_specs=spaces or [vmem] * len(arrays), out_specs...  457 us
    pallas_call x1, Pallas kernels, feed_forward(): pl.pallas_call(kernel, in_specs=[hbm] * 6, out_specs=[hbm] * 2, out_shape...  27.4 us
    unnamed x33, local copies, waits for them, and re-layouts  12.3 us
  transfers between devices with their start and end apart: 4, of which 2 were waited for; matrix products, arithmetic and copies ran while one was open for 0% of the time, Pallas kernels for 67%

profile of v5, /device:TPU:0, one launch (start us, length us, event | category | flops | bytes accessed | tf_op | source)
XLA Modules:
  0.0 520.2 jit_solution(16095501347943978356)
XLA Ops:
  7.2 0.0 all-gather.3.cloned.1.call-start
  7.2 0.7 bitcast_convert_fusion.1
  7.9 0.7 bitcast_convert_fusion
  8.5 0.7 copy.34.two_ref.gain_two_ref
  9.3 0.7 copy.33.one_ref.gain_ref
  10.0 63.1 %front.1 = (bf16[2048,1024]{1,0:T(8,128)(2,1)}, bf16[256,1024]{1,0:T(8,128)(2,1)}, s32[4,1,512]{2,1,0:T(1,128)}, bf16[4,4,128,576]{3,2,1,0:T(8,128)(2,1)}, bf16[...) custom-call(bf16[512,2048]{1,0:T(8,128)(2,1)} %bitcast.22, s32[1,1,512]{2,1,0:T(1,128)} %bitcast.33, ...), custom_call_target="tpu_custom_call" | custom-call | bytes 4852736 | tf_op jit(solution)/shard_map/front/pallas_call | solution.py:664
  73.1 0.0 all-gather.3.cloned.1.call-update
  73.1 0.0 all-gather.5.cloned.1.call-start
  73.2 2.0 copy.35.row_ref
  75.2 45.7 %attend.1 = (bf16[2048,320]{1,0:T(8,128)(2,1)}, f32[2048,256]{1,0:T(8,128)}, f32[2048,2]{1,0:T(8,128)}, bf16[2048,256]{1,0:T(8,128)(2,1)}, bf16[2048,1024]{1,0:T(8,128)(2,1)}, /*index=5*/bf16[2048,2048]{1,0:T(8,128)(2,1)}) custom-call(bf16[2048,1024]{1,0:T(8,128)(2,1)} %get-tuple-element.50.x_ref, bf16[256,1024]{1,0:T(8,128)(2,1)} %get-tuple-element.51.own_ref, ...), custom_call_target="tpu_custom_call" | custom-call | bytes 9191424 | tf_op jit(solution)/shard_map/attend/pallas_call | solution.py:664
  120.9 0.0 all-gather.5.cloned.1.call-update
  121.0 0.5 reduce-scatter.3.cloned.1.call-start
  121.5 81.2 %to_middle.1 = (f32[256,2048]{1,0:T(8,128)}, bf16[2048,2048]{1,0:T(8,128)(2,1)}) custom-call(bf16[2048,256]{1,0:T(8,128)(2,1)} %get-tuple-element.57.h_ref, bf16[2048,576]{1,0:T(8,128)(2,1)} %bitcast.19, bf16[512,2048]{1,0:T(8,128)(2,1)} %bitcast.23), custom_call_target="tpu_custom_call" | custom-call | flops 2147483648 | bytes 5505024 | tf_op jit(solution)/shard_map/to_middle/pallas_call | solution.py:664
  202.7 0.0 all-gather.3.cloned.1.call-done
  202.7 39.5 %gate_up.1 = (bf16[2048,704]{1,0:T(8,128)(2,1)}, bf16[2048,704]{1,0:T(8,128)(2,1)}, bf16[2048,704]{1,0:T(8,128)(2,1)}, bf16[2048,1024]{1,0:T(8,128)(2,1)}, bf16[2048,704]{1,0:T(8,128)(2,1)}) custom-call(bf16[2048,2048]{1,0:T(8,128)(2,1)} %get-tuple-element.58.x_ref.two_ref, bf16[2048,1408]{1,0:T(8,128)(2,1)} %bitcast.34, bf16[512,2048]{1,0:T(8,128)(2,1)} %bitcast.28, ...), custom_call_target="tpu_custom_call" | custom-call | flops 11811160064 | bytes 20447232 | tf_op jit(solution)/shard_map/gate_up/pallas_call | solution.py:664
  242.2 0.0 reduce-scatter.3.cloned.1.call-update
  242.3 0.0 reduce-scatter.5.cloned.1.call-start
  242.3 1.0 all-gather.5.cloned.1.call-done
  243.4 27.4 %feed_forward.1 = (bf16[2048,1408]{1,0:T(8,128)(2,1)}, bf16[2048,1408]{1,0:T(8,128)(2,1)}) custom-call(bf16[2048,704]{1,0:T(8,128)(2,1)} %get-tuple-element.61.slope_ref, bf16[2048,704]{1,0:T(8,128)(2,1)} %get-tuple-element.62.silu_ref, bf16[2048,1024]{1,0:T(8,128)(2,1)} %get-tuple-element.60.low_ref, bf16[2048,1024]{1,0:T(8,128)(2,1)} %get-tuple-element.63.high_ref, ...), custom_call_target="tpu_custom_call" | custom-call | flops 17716740096 | bytes 36962304 | tf_op jit(solution)/shard_map/feed_forward/pallas_call | solution.py:1487
  270.8 0.0 reduce-scatter.5.cloned.1.call-update
  270.8 92.5 %to_branch.1 = (f32[256,2048]{1,0:T(8,128)}, bf16[2048,2048]{1,0:T(8,128)(2,1)}, bf16[2048,256]{1,0:T(8,128)(2,1)}, bf16[2048,2048]{1,0:T(8,128)(2,1)}) custom-call(bf16[2048,1408]{1,0:T(8,128)(2,1)} %get-tuple-element.65.g_ref, bf16[2048,1408]{1,0:T(8,128)(2,1)} %bitcast.35, f32[256,2048]{1,0:T(8,128)} %get-tuple-element.66.mid_ref, ...), custom_call_target="tpu_custom_call" | custom-call | flops 16106127360 | bytes 24117248 | tf_op jit(solution)/shard_map/to_branch/pallas_call | solution.py:664
  363.3 0.0 reduce-scatter.3.cloned.1.call-done.down_ref
  363.3 60.2 %attend_back.1 = (bf16[2048,320]{1,0:T(8,128)(2,1)}, bf16[512,2048]{1,0:T(8,128)(2,1)}, f32[128,1024]{1,0:T(8,128)}, f32[128,2816]{1,0:T(8,128)}) custom-call(bf16[2048,320]{1,0:T(8,128)(2,1)} %get-tuple-element.54.x_ref, bf16[2048,256]{1,0:T(8,128)(2,1)} %get-tuple-element.68.gm_ref, f32[2048,256]{1,0:T(8,128)} %get-tuple-element.69.m_ref, ...), custom_call_target="tpu_custom_call" | custom-call | bytes 25133056 | tf_op jit(solution)/shard_map/attend_back/pallas_call | solution.py:664
  423.5 2.4 reduce-scatter.5.cloned.1.call-done.both_ref
  425.9 75.2 %to_input.1 = (f32[512,2048]{1,0:T(8,128)}, f32[128,128]{1,0:T(8,128)}, f32[128,128]{1,0:T(8,128)}, f32[128,1024]{1,0:T(8,128)}, f32[128,2816]{1,0:T(8,128)}, /*...) custom-call(bf16[2048,320]{1,0:T(8,128)(2,1)} %get-tuple-element.75.g_ref, bf16[2048,576]{1,0:T(8,128)(2,1)} %bitcast.21, ...), custom_call_target="tpu_custom_call" | custom-call | flops 2684354560 | bytes 19465216 | tf_op jit(solution)/shard_map/to_input/pallas_call | solution.py:664
  501.2 0.0 copy-start
  501.2 0.0 copy-done.1
  501.2 1.3 copy.50
  502.5 1.6 copy-done
  504.1 0.0 copy-start.4
  504.1 2.1 copy.51
  506.3 0.0 copy-done.8
  506.3 0.6 copy.52
  506.9 0.0 copy-done.7
  506.9 0.6 copy.53
  507.5 0.0 copy-done.6
  507.5 0.8 copy.54
  508.3 0.0 copy-done.5
  508.3 0.8 copy.55
  509.1 0.0 copy-done.4
  509.1 1.1 copy.56
  510.2 0.0 copy-done.3
  510.2 1.1 copy.57
  511.3 0.0 copy-done.2
  511.3 1.1 copy.58
  512.4 0.0 copy-done.10
  512.5 0.5 copy.59
  513.0 0.5 copy.60
  (10 shorter events, 0.0 us)
Async XLA Ops:
  7.2 195.5 %all-gather.3.cloned.1.call-start = ((), (), s32[]{:S(2)}) async-start(), calls=%async_computation.2 | async-start | bytes 7208960 | tf_op jit(solution)/shard_map/all_gather | solution.py:1856
  73.1 170.2 %all-gather.5.cloned.1.call-start = ((), (), s32[]{:S(2)}) async-start(), calls=%async_computation.3 | async-start | bytes 3932160 | tf_op jit(solution)/shard_map/all_gather | solution.py:1862
  121.0 242.3 %reduce-scatter.3.cloned.1.call-start = ((), (), s32[]{:S(2)}) async-start(), calls=%async_computation.4 | async-start | bytes 3932160 | tf_op jit(solution)/shard_map/reduce_scatter | solution.py:1865
  242.3 183.6 %reduce-scatter.5.cloned.1.call-start = ((), (), s32[]{:S(2)}) async-start(), calls=%async_computation.5 | async-start | bytes 7208960 | tf_op jit(solution)/shard_map/reduce_scatter | solution.py:1867
  425.9 75.3 %copy-start.1 = (bf16[512,2048]{1,0:T(8,128)(2,1)S(1)}, bf16[512,2048]{1,0:T(8,128)(2,1)}, u32[]{:S(2)}) copy-start(bf16[512,2048]{1,0:T(8,128)(2,1)} %get-tuple-element.74) | copy-start | bytes 6291460
  501.2 2.9 copy-start
  504.1 2.2 copy-start.8
  504.1 2.8 copy-start.7
  504.1 3.4 copy-start.6
  504.1 4.2 copy-start.5
  504.1 5.0 copy-start.4
  506.3 4.0 copy-start.3
  509.1 2.2 copy-start.2
  510.2 2.2 copy-start.10
  510.2 2.7 copy-start.9
Sparse Core Ops, SparseCore 0:
  73.2 106.6 all-gather.2
  181.5 61.7 all-gather.4
  245.7 58.8 reduce-scatter.2
  306.8 119.1 reduce-scatter.4

commit v6 on v5

--- a/solution.py
+++ b/solution.py
@@ -871,27 +871,30 @@
 
 
 def attend_back(
-    qkv, g_mixed, mixed, denom, seg_rows, seg_cols, branch, heads_out, out_terms, middle, sum_down, heads
+    qkv, g_mixed, mixed, denom, seg_rows, seg_cols, out_terms, middle, sum_down, heads
 ):
-    tokens, width = branch.shape
+    tokens, width = out_terms.shape
     wide, narrow = heads * DV, heads * F
     blocks = tokens // BLOCK
-    deep = lax.axis_size("dp")
-    group = width // deep
     own = tokens // 8
     held, units = sum_down.shape[0] // 4, sum_down.shape[1]
 
     def kernel(
-        x_ref, gm_ref, m_ref, d_ref, row_ref, col_ref, br_ref, h_ref, term_ref, mid_ref, down_ref,
-        g_ref, out_ref, go_ref, gd_ref,
-        gq_ref, numer_ref, gden_ref, key_ref, back_ref, came, br_buf, load, send, receive,
-        term_buf, term_load, sums, parts_o, parts_d, p_send, p_receive, local, *rest,
+        x_ref, gm_ref, m_ref, d_ref, row_ref, col_ref, term_ref, mid_ref, down_ref,
+        g_ref, out_ref, gd_ref,
+        gq_ref, numer_ref, gden_ref, key_ref, gm_buf, m_buf, mid_buf, here_buf, large,
+        term_buf, term_load, parts_d, p_send, p_receive, local, *rest,
     ):
         bufs, (s_send, s_receive, t_send, t_receive) = rest[:6], rest[6:]
         d, c, t = place_of()
-        hand_on, landed = exchange(
-            ((sums, parts_o), (down_ref, parts_d)), held, p_send, p_receive, local
+        hand_on, landed = exchange(((down_ref, parts_d),), held, p_send, p_receive, local)
+        mine = pl.ds(pl.multiple_of(t * own, own), own)
+        loads = (
+            pltpu.make_async_copy(gm_ref, gm_buf, large.at[0]),
+            pltpu.make_async_copy(m_ref, m_buf, large.at[1]),
+            pltpu.make_async_copy(mid_ref, mid_buf, large.at[2]),
         )
+        stored = pltpu.make_async_copy(here_buf, out_ref.at[mine], large.at[3])
 
         def fetch_terms(i):
             part = pl.ds(pl.multiple_of(2 * scatter_order(i) * own, 2 * own), 2 * own)
@@ -900,46 +903,21 @@
 
         fetch_terms(0).start()
 
-        def fetch(n):
-            part = pl.ds(pl.multiple_of(depth(d, n + 1) * group, group), group)
-            slot = lax.rem(n, 2)
-            return pltpu.make_async_copy(br_ref.at[:, part], br_buf.at[slot], load.at[slot])
-
-        def deeper(n):
-            return remote(
-                back_ref.at[n], came.at[n], send, receive, n, (depth(d, n + 1), c, t)
-            )
-
-        fetch(0).start()
-        met = (
-            around()
-            + [(d, beside(c, 3), t)]
-            + [(depth(d, k), c, t) for k in range(1, deep)]
-        )
+        for copy in loads:
+            copy.start()
+        met = around() + [(d, beside(c, 3), t)]
         say(met)
 
-        def plane(n, carry):
-            @pl.when(n < deep - 1)
-            def _():
-                fetch(n + 1).start()
-
-            fetch(n).wait()
-            back_ref[n] = dot(br_buf[lax.rem(n, 2)], h_ref[...], 0, 0).astype(BF16)
-
-            @pl.when(n < deep - 1)
-            def _():
-                deeper(n).start()
-
-            return carry
-
         def prepare():
+            loads[0].wait()
+            loads[1].wait()
             gq_ref[...] = jnp.zeros_like(gq_ref)
             for h in range(heads):
                 part = pl.ds(h * DV, DV)
-                gm = gm_ref[:, part].astype(F32)
+                gm = gm_buf[:, part].astype(F32)
                 inverse = 1.0 / d_ref[:, h : h + 1]
                 numer_ref[:, part] = (gm * inverse).astype(BF16)
-                down = -jnp.sum(gm * m_ref[:, part], axis=1, keepdims=True) * inverse
+                down = -jnp.sum(gm * m_buf[:, part], axis=1, keepdims=True) * inverse
                 gden_ref[h : h + 1, :] = jnp.transpose(
                     jnp.broadcast_to(down, (tokens, 128)), (1, 0)
                 )[:1]
@@ -1004,48 +982,34 @@
 
         def fill(n):
             if n == 0:
-                lax.fori_loop(0, deep, plane, 0)
-                hand_on(1)
                 prepare()
                 pl.loop(0, 1)(one_block)
             else:
                 pl.loop(1, blocks)(one_block)
+                hand_on(0)
 
         moved = scatter_rows(terms, bufs, s_send, s_receive, lambda: hear(len(met)), fill)
-        here = out_ref.at[pl.ds(pl.multiple_of(t * own, own), own)]
-        here[...] = (mid_ref[...] + moved).astype(BF16)
-        copy = remote(here, here, t_send, t_receive, 0, (d, c, 1 - t))
+        loads[2].wait()
+        here_buf[...] = (mid_buf[...] + moved).astype(BF16)
+        copy = remote(here_buf, out_ref.at[mine], t_send, t_receive, 0, (d, c, 1 - t))
         copy.start()
+        stored.start()
         g_ref[:, wide : wide + narrow] = jnp.transpose(gq_ref[...], (1, 0)).astype(BF16)
-        total = back_ref[deep - 1].astype(F32)
-        for n in range(deep - 1):
-            deeper(n).wait_recv()
-            total = total + came[n].astype(F32)
-        sums[...] = total.astype(BF16)
-        hand_on(0)
-        landed(1)
+        landed(0)
         for b in range(4):
             gd_ref[:, b * units : (b + 1) * units] = parts_d[b].astype(F32)
-        landed(0)
-        for b in range(4):
-            go_ref[:, b * wide : (b + 1) * wide] = parts_o[b].astype(F32)
-        for n in range(deep - 1):
-            deeper(n).wait_send()
         copy.wait_send()
         there = out_ref.at[pl.ds(pl.multiple_of((1 - t) * own, own), own)]
         remote(there, there, t_send, t_receive, 0, (d, c, 1 - t)).wait_recv()
+        stored.wait()
 
     vmem, hbm = pl.BlockSpec(memory_space=pltpu.VMEM), pl.BlockSpec(memory_space=pl.ANY)
     return call(
         kernel, "attend_back", 7,
-        (
-            qkv, g_mixed, mixed, denom, seg_rows, seg_cols, branch, heads_out, out_terms, middle,
-            sum_down,
-        ),
+        (qkv, g_mixed, mixed, denom, seg_rows, seg_cols, out_terms, middle, sum_down),
         [
             jax.ShapeDtypeStruct(qkv.shape, BF16),
             jax.ShapeDtypeStruct((2 * own, width), BF16),
-            jax.ShapeDtypeStruct((held, 4 * wide), F32),
             jax.ShapeDtypeStruct((held, 4 * units), F32),
         ],
         [
@@ -1053,21 +1017,19 @@
             pltpu.VMEM((tokens, wide), BF16),
             pltpu.VMEM((8, tokens), F32),
             pltpu.VMEM((2 * narrow, tokens), BF16),
-            pltpu.VMEM((deep, group, wide), BF16),
-            pltpu.VMEM((deep - 1, group, wide), BF16),
-            pltpu.VMEM((2, tokens, group), BF16),
+            pltpu.VMEM(g_mixed.shape, BF16),
+            pltpu.VMEM(mixed.shape, F32),
+            pltpu.VMEM(middle.shape, F32),
+            pltpu.VMEM((own, width), BF16),
+            pltpu.SemaphoreType.DMA((4,)),
+            pltpu.VMEM((2, 2 * own, width), BF16),
             pltpu.SemaphoreType.DMA((2,)),
-        ]
-        + sems(deep - 1)
-        + [pltpu.VMEM((2, 2 * own, width), BF16), pltpu.SemaphoreType.DMA((2,))]
-        + [
-            pltpu.VMEM((group, wide), BF16),
-            pltpu.VMEM((4, held, wide), BF16),
             pltpu.VMEM((4, held, units), BF16),
         ]
-        + sems(6) + [pltpu.SemaphoreType.DMA((2,))]
+        + sems(3) + [pltpu.SemaphoreType.DMA((1,))]
         + scatter_scratch(own, width) + sems(SCATTER_COPIES) + sems(1),
-        [vmem] * 6 + [hbm, vmem, hbm, vmem, hbm],
+        [vmem, hbm, hbm, vmem, vmem, vmem, hbm, hbm, hbm],
+        [vmem, hbm, vmem],
     )
 
 
@@ -1212,27 +1174,44 @@
     own = tokens // 8
     wide = heads_out.shape[1]
 
-    def kernel(h_ref, w_ref, x_ref, mid_ref, rows_out, *rest):
+    def kernel(h_ref, w_ref, x_ref, mid_ref, rows_out, w_buf, x_buf, mid_buf, large, *rest):
         bufs, (s_send, s_receive, rows_ref, g_send, g_receive, store) = rest[:6], rest[6:]
         d, c, t = place_of()
+        mine = pl.ds(pl.multiple_of(t * own, own), own)
+        weights = pltpu.make_async_copy(w_ref.at[:, wide : 2 * wide], w_buf, large.at[0])
+        loaded = pltpu.make_async_copy(x_ref.at[mine], x_buf, large.at[1])
+        stored = pltpu.make_async_copy(mid_buf, mid_ref, large.at[2])
+        weights.start()
+        loaded.start()
         say(around())
+        weights.wait()
 
         def terms(i, start):
-            return [(h_ref[pl.ds(start, 2 * own), :], w_ref, slice(wide, 2 * wide))]
+            return [(h_ref[pl.ds(start, 2 * own), :], w_buf, slice(None))]
 
         total = scatter_rows(terms, bufs, s_send, s_receive, lambda: hear(3))
-        middle = total + x_ref[pl.ds(pl.multiple_of(t * own, own), own), :].astype(F32)
-        mid_ref[...] = middle
+        loaded.wait()
+        middle = total + x_buf[...].astype(F32)
+        mid_buf[...] = middle
+        stored.start()
         _, hat = norm_parts(middle)
         rows_ref[pl.ds(pl.multiple_of((2 * c + t) * own, own), own), :] = hat.astype(BF16)
         gather_rows(rows_ref, rows_out, g_send, g_receive, store)
-
+        stored.wait()
+
+    vmem, hbm = pl.BlockSpec(memory_space=pltpu.VMEM), pl.BlockSpec(memory_space=pl.ANY)
     return call(
         kernel, "to_middle", 3, (heads_out, w_attn, x),
         [jax.ShapeDtypeStruct((own, width), F32), jax.ShapeDtypeStruct((tokens, width), BF16)],
-        scatter_scratch(own, width) + sems(SCATTER_COPIES) + gather_scratch(tokens, width),
-        None,
-        [pl.BlockSpec(memory_space=pltpu.VMEM), pl.BlockSpec(memory_space=pl.ANY)],
+        [
+            pltpu.VMEM((width, wide), BF16),
+            pltpu.VMEM((own, width), BF16),
+            pltpu.VMEM((own, width), F32),
+            pltpu.SemaphoreType.DMA((3,)),
+        ]
+        + scatter_scratch(own, width) + sems(SCATTER_COPIES) + gather_scratch(tokens, width),
+        [vmem, hbm, hbm],
+        [hbm, hbm],
         flops=2 * tokens * width * heads_out.shape[1],
     )
 
@@ -1522,10 +1501,18 @@
 
     def kernel(
         g_ref, w_ref, mid_ref, cot_ref, o_ref, hid_ref, d_ref, gm_ref, rows_out, mix_ref, term_ref,
-        g_buf, w_buf, hid_buf, d_buf, term_buf, load, term_store, *rest,
+        g_buf, w_buf, hid_buf, d_buf, term_buf, load, term_store,
+        mid_buf, cot_buf, o_buf, gm_buf, large, *rest,
     ):
         bufs, (s_send, s_receive, rows_ref, g_send, g_receive, store) = rest[:6], rest[6:]
         d, c, t = place_of()
+        mine = pl.ds(pl.multiple_of(t * own, own), own)
+        loads = (
+            pltpu.make_async_copy(mid_ref, mid_buf, large.at[0]),
+            pltpu.make_async_copy(cot_ref.at[mine], cot_buf, large.at[1]),
+            pltpu.make_async_copy(o_ref.at[:, wide : 2 * wide], o_buf, large.at[2]),
+        )
+        stored = pltpu.make_async_copy(gm_buf, gm_ref, large.at[3])
 
         def fetch(i):
             part = pl.ds(pl.multiple_of(2 * scatter_order(i) * own, 2 * own), 2 * own)
@@ -1539,6 +1526,8 @@
         weights.wait()
         down = pltpu.make_async_copy(d_ref, d_buf, load.at[3])
         down.start()
+        for copy in loads:
+            copy.start()
         pltpu.make_async_copy(
             hid_ref.at[pl.ds(0, BLOCK)], hid_buf, load.at[4]
         ).start()
@@ -1553,16 +1542,17 @@
             return [(g_buf[lax.rem(i, 2)], w_buf, slice(None))]
 
         total = scatter_rows(terms, bufs, s_send, s_receive, lambda: hear(3))
-        scale, hat = norm_parts(mid_ref[...])
-        g_middle = cot_ref[pl.ds(pl.multiple_of(t * own, own), own), :].astype(F32) + norm_back(
-            total, hat, scale
-        )
-        gm_ref[...] = g_middle
+        for copy in loads:
+            copy.wait()
+        scale, hat = norm_parts(mid_buf[...])
+        g_middle = cot_buf[...].astype(F32) + norm_back(total, hat, scale)
+        gm_buf[...] = g_middle
+        stored.start()
         rows_ref[pl.ds(pl.multiple_of((2 * c + t) * own, own), own), :] = g_middle.astype(BF16)
 
         def mix(start):
             mix_ref[pl.ds(start, own), :] = dot(
-                rows_ref[pl.ds(start, own), :], o_ref[:, wide : 2 * wide], 1, 0
+                rows_ref[pl.ds(start, own), :], o_buf[...], 1, 0
             ).astype(BF16)
 
         def block(i):
@@ -1603,6 +1593,7 @@
             lambda: out_terms(blocks - 1, blocks),
         )
         term_given(blocks - 1).wait()
+        stored.wait()
 
     vmem, hbm = pl.BlockSpec(memory_space=pltpu.VMEM), pl.BlockSpec(memory_space=pl.ANY)
     return call(
@@ -1621,10 +1612,15 @@
             pltpu.VMEM((BLOCK, width), BF16),
             pltpu.SemaphoreType.DMA((5,)),
             pltpu.SemaphoreType.DMA((1,)),
+            pltpu.VMEM((own, width), F32),
+            pltpu.VMEM((own, width), BF16),
+            pltpu.VMEM((width, wide), BF16),
+            pltpu.VMEM((own, width), F32),
+            pltpu.SemaphoreType.DMA((4,)),
         ]
         + scatter_scratch(own, width) + sems(SCATTER_COPIES) + gather_scratch(tokens, width),
-        [hbm, hbm, vmem, vmem, vmem, hbm, hbm],
-        [vmem, hbm, vmem, hbm],
+        [hbm] * 7,
+        [hbm, hbm, vmem, hbm],
         flops=4 * tokens * width * (g_both.shape[1] // 2 + wide),
     )
 
@@ -1633,7 +1629,9 @@
     return jnp.transpose(jnp.broadcast_to(column, (column.shape[0], 128)), (1, 0))[:8]
 
 
-def to_input(g_qkv, w_attn, x, g_middle, rows_one, sum_both, weights, gains, heads):
+def to_input(
+    g_qkv, w_attn, x, g_middle, rows_one, branch, heads_out, sum_both, weights, gains, heads
+):
     tokens, width = g_qkv.shape[0], x.shape[1]
     own = tokens // 8
     deep = lax.axis_size("dp")
@@ -1646,25 +1644,50 @@
     main = units // 128 * 128
 
     def kernel(
-        g_ref, w_ref, x_ref, gm_ref, one_ref, both_ref,
+        g_ref, w_ref, x_ref, gm_ref, one_ref, br_ref, h_ref, both_ref,
         wq_ref, wk_ref, wv_ref, wg_ref, wu_ref, gain_ref, gain_two_ref,
-        out_ref, gq_ref, gk_ref, gv_ref, gg_ref, gu_ref, row_ref, row_two_ref,
+        out_ref, gq_ref, gk_ref, gv_ref, go_ref, gg_ref, gu_ref, row_ref, row_two_ref,
         *rest,
     ):
         bufs, (s_send, s_receive, t_send, t_receive) = rest[:6], rest[6:10]
         (
-            came_deep, sums, parts_a, parts_b, scalar, back_ref, one_buf, load,
-            d_send, d_receive, p_send, p_receive, local, x_buf, gm_buf, gate_buf, up_buf, in_buf, large,
+            came_deep, came_out, sums, sums_out, parts_a, parts_o, parts_b, scalar, back_ref, back_out,
+            cols, load, d_send, d_receive, p_send, p_receive, local, x_buf, gm_buf, in_buf, gate_buf,
+            up_buf, large,
         ) = rest[10:]
         d, c, t = place_of()
         hand_on, landed = exchange(
-            ((sums, parts_a), (both_ref, parts_b)), held, p_send, p_receive, local
+            ((sums, parts_a), (both_ref, parts_b), (sums_out, parts_o)), held, p_send, p_receive, local
         )
 
-        def fetch(n):
-            part = pl.ds(pl.multiple_of(depth(d, n + 1) * group, group), group)
-            slot = lax.rem(n, 2)
-            return pltpu.make_async_copy(one_ref.at[:, part], one_buf.at[slot], load.at[slot])
+        def fetch(j):
+            part = pl.ds(pl.multiple_of(depth(d, j % deep + 1) * group, group), group)
+            source = br_ref if j < deep else one_ref
+            return pltpu.make_async_copy(source.at[:, part], cols.at[j % 2], load.at[j % 2])
+
+        def deeper(j):
+            n = j % deep
+            source, target = (back_out, came_out) if j < deep else (back_ref, came_deep)
+            return remote(
+                source.at[n], target.at[n], d_send, d_receive, j, (depth(d, n + 1), c, t)
+            )
+
+        def plane(j):
+            n = j % deep
+            if j + 1 < 2 * deep:
+                fetch(j + 1).start()
+            fetch(j).wait()
+            if j < deep:
+                back_out[n] = dot(cols[j % 2], h_ref[...], 0, 0).astype(BF16)
+            else:
+                back_ref[n] = dot(cols[j % 2], g_ref[...], 0, 0).astype(BF16)
+
+        def sum_of(back, came, first):
+            total = back[deep - 1].astype(F32)
+            for n in range(deep - 1):
+                deeper(first + n).wait_recv()
+                total = total + came[n].astype(F32)
+            return total.astype(BF16)
 
         fetch(0).start()
         mine = pl.ds(pl.multiple_of(t * own, own), own)
@@ -1672,10 +1695,10 @@
             pltpu.make_async_copy(x_ref.at[mine], x_buf, large.at[0]),
             pltpu.make_async_copy(gm_ref, gm_buf, large.at[1]),
         )
-        stores = (
-            pltpu.make_async_copy(gate_buf, gg_ref, large.at[2]),
-            pltpu.make_async_copy(up_buf, gu_ref, large.at[3]),
-            pltpu.make_async_copy(in_buf, out_ref.at[mine], large.at[4]),
+        stored = pltpu.make_async_copy(in_buf, out_ref.at[mine], large.at[2])
+        wide_stores = (
+            pltpu.make_async_copy(gate_buf, gg_ref, large.at[3]),
+            pltpu.make_async_copy(up_buf, gu_ref, large.at[4]),
         )
         for copy in loads:
             copy.start()
@@ -1686,27 +1709,14 @@
         )
         say(met)
 
-        def deeper(n):
-            rows = pl.ds(pl.multiple_of(depth(d, n + 1) * group, group), group)
-            return remote(
-                back_ref.at[rows], came_deep.at[n], d_send, d_receive, n, (depth(d, n + 1), c, t)
-            )
-
-        def plane(n, carry):
-            rows = pl.ds(pl.multiple_of(depth(d, n + 1) * group, group), group)
-
-            @pl.when(n < deep - 1)
-            def _():
-                fetch(n + 1).start()
-
-            fetch(n).wait()
-            back_ref[rows, :] = dot(one_buf[lax.rem(n, 2)], g_ref[...], 0, 0).astype(BF16)
-
-            @pl.when(n < deep - 1)
-            def _():
-                deeper(n).start()
-
-            return carry
+        early = deep // 2
+        for j in range(early):
+            plane(j)
+
+        def enter():
+            hear(len(met))
+            for j in range(early):
+                deeper(j).start()
 
         def terms(i, start):
             part = pl.ds(start, 2 * own)
@@ -1718,53 +1728,46 @@
         def fill(n):
             if n == 0:
                 hand_on(1)
-                lax.fori_loop(0, deep, plane, 0)
+                for j in range(early, 2 * deep):
+                    plane(j)
+                    if j % deep != deep - 1:
+                        deeper(j).start()
                 return
             landed(1)
-            gain_two = gain_two_ref[...]
-            for b in range(4):
-                whole = parts_b[b].astype(F32)
-                for ref, first, rest_of in (
-                    (gate_buf, 0, 2 * main),
-                    (up_buf, main, main + units),
-                ):
-                    s = whole[:, first : first + main]
+            whole = [parts_b[b].astype(F32) for b in range(4)]
+            term = jnp.zeros((held, 1), F32)
+            for ref, weight, first, rest_of in (
+                (gate_buf, wg_ref, 0, 2 * main),
+                (up_buf, wu_ref, main, main + units),
+            ):
+                pieces = []
+                for b in range(4):
+                    pieces.append(whole[b][:, first : first + main])
                     if main < units:
-                        s = jnp.concatenate([s, whole[:, rest_of : rest_of + units - main]], axis=1)
-                    ref[:, b * units : (b + 1) * units] = s * gain_two
-            scalar[0, 1] = as_row(
-                (
-                    jnp.sum(gate_buf[...] * wg_ref[...].astype(F32), axis=1, keepdims=True)
-                    + jnp.sum(up_buf[...] * wu_ref[...].astype(F32), axis=1, keepdims=True)
-                )
-                / gain_two
-            )
-            stores[0].start()
-            stores[1].start()
-            for m in range(deep - 1):
-                deeper(m).wait_recv()
-            kept_rows = pl.ds(pl.multiple_of(d * group, group), group)
-            total = back_ref[kept_rows, :].astype(F32)
-            for m in range(deep - 1):
-                total = total + came_deep[m].astype(F32)
-            sums[...] = total.astype(BF16)
-            hand_on(0)
-
-        e_one = scatter_rows(terms, bufs, s_send, s_receive, lambda: hear(len(met)), fill)
+                        pieces.append(whole[b][:, rest_of : rest_of + units - main])
+                s = jnp.concatenate(pieces, axis=1)
+                term = term + jnp.sum(s * weight[...].astype(F32), axis=1, keepdims=True)
+                ref[...] = s * gain_two_ref[...]
+            for copy in wide_stores:
+                copy.start()
+            scalar[0, 1] = as_row(term)
+
+        e_one = scatter_rows(terms, bufs, s_send, s_receive, enter, fill)
         for copy in loads:
             copy.wait()
         scale, hat = norm_parts(x_buf[...].astype(F32))
         in_buf[...] = gm_buf[...] + norm_back(e_one, hat, scale)
         copy = remote(in_buf, out_ref.at[mine], t_send, t_receive, 0, (d, c, 1 - t))
         copy.start()
-        stores[2].start()
+        stored.start()
+        sums_out[...] = sum_of(back_out, came_out, 0)
+        hand_on(2)
+        sums[...] = sum_of(back_ref, came_deep, deep)
+        hand_on(0)
+        landed(2)
+        for b in range(4):
+            go_ref[:, b * wide : (b + 1) * wide] = parts_o[b].astype(F32)
         landed(0)
-        gain_one = gain_ref[...]
-
-        def owned(start, count):
-            return jnp.concatenate(
-                [parts_a[b][:, start : start + count].astype(F32) for b in range(4)], axis=1
-            )
 
         term_one = jnp.zeros((held, 1), F32)
         for ref, weight, start, count in (
@@ -1772,9 +1775,11 @@
             (gq_ref, wq_ref, wide, narrow),
             (gk_ref, wk_ref, wide + narrow, narrow),
         ):
-            s = owned(start, count)
+            s = jnp.concatenate(
+                [parts_a[b][:, start : start + count].astype(F32) for b in range(4)], axis=1
+            )
             term_one = term_one + jnp.sum(s * weight[...].astype(F32), axis=1, keepdims=True)
-            ref[...] = s * gain_one
+            ref[...] = s * gain_ref[...]
         scalar[0, 0] = as_row(term_one)
         swap = remote(scalar.at[0], scalar.at[1], t_send, t_receive, 1, (d, c, 1 - t))
         swap.start()
@@ -1784,42 +1789,49 @@
         copy.wait_send()
         there = out_ref.at[pl.ds(pl.multiple_of((1 - t) * own, own), own)]
         remote(there, there, t_send, t_receive, 0, (d, c, 1 - t)).wait_recv()
-        for m in range(deep - 1):
-            deeper(m).wait_send()
-        for copy in stores:
+        for n in range(deep - 1):
+            deeper(n).wait_send()
+            deeper(deep + n).wait_send()
+        stored.wait()
+        for copy in wide_stores:
             copy.wait()
 
     w_q, w_k, w_v, w_gate, w_up = weights
     vmem, hbm = pl.BlockSpec(memory_space=pltpu.VMEM), pl.BlockSpec(memory_space=pl.ANY)
     return call(
         kernel, "to_input", 6,
-        (g_qkv, w_attn, x, g_middle, rows_one, sum_both) + tuple(weights) + tuple(gains),
+        (g_qkv, w_attn, x, g_middle, rows_one, branch, heads_out, sum_both) + tuple(weights)
+        + tuple(gains),
         [jax.ShapeDtypeStruct((2 * own, width), F32)]
-        + [jax.ShapeDtypeStruct(w.shape, F32) for w in weights]
+        + [jax.ShapeDtypeStruct(w.shape, F32) for w in (w_q, w_k, w_v, w_v, w_gate, w_up)]
         + [jax.ShapeDtypeStruct((1, held), F32)] * 2,
         scatter_scratch(own, width) + sems(SCATTER_COPIES) + sems(2)
         + [
             pltpu.VMEM((deep - 1, group, across), BF16),
+            pltpu.VMEM((deep - 1, group, wide), BF16),
             pltpu.VMEM((group, across), BF16),
+            pltpu.VMEM((group, wide), BF16),
             pltpu.VMEM((4, held, across), BF16),
+            pltpu.VMEM((4, held, wide), BF16),
             pltpu.VMEM((4, held, both), BF16),
             pltpu.VMEM((2, 2, 8, held), F32),
-            pltpu.VMEM((width, across), BF16),
+            pltpu.VMEM((deep, group, across), BF16),
+            pltpu.VMEM((deep, group, wide), BF16),
             pltpu.VMEM((2, tokens, group), BF16),
             pltpu.SemaphoreType.DMA((2,)),
         ]
-        + sems(deep - 1) + sems(6)
+        + sems(2 * deep) + sems(9)
         + [
-            pltpu.SemaphoreType.DMA((2,)),
+            pltpu.SemaphoreType.DMA((3,)),
             pltpu.VMEM((own, width), BF16),
+            pltpu.VMEM((own, width), F32),
             pltpu.VMEM((own, width), F32),
             pltpu.VMEM(w_gate.shape, F32),
             pltpu.VMEM(w_up.shape, F32),
-            pltpu.VMEM((own, width), F32),
             pltpu.SemaphoreType.DMA((5,)),
         ],
-        [vmem] * 2 + [hbm] * 4 + [vmem] * 7,
-        [hbm] + [vmem] * 3 + [hbm] * 2 + [vmem] * 2,
+        [vmem] * 2 + [hbm] * 4 + [vmem, hbm] + [vmem] * 7,
+        [hbm] + [vmem] * 4 + [hbm] * 2 + [vmem] * 2,
         flops=2 * tokens * width * g_qkv.shape[1],
     )
 
@@ -1868,26 +1880,17 @@
     g_middle, branch, g_mixed, out_terms = to_branch(
         g_both, w_both, middle, cot_block, w_attn, heads * DV, hidden, w_down
     )
-    g_qkv, out, s_o, s_down = attend_back(
-        qkv,
-        g_mixed,
-        mixed,
-        denom,
-        seg_rows,
-        seg_cols,
-        branch,
-        heads_out,
-        out_terms,
-        middle,
-        sum_down,
-        heads,
-    )
-    g_input, s_q, s_k, s_v, s_gate, s_up, attn_row, mlp_row = to_input(
+    g_qkv, out, s_down = attend_back(
+        qkv, g_mixed, mixed, denom, seg_rows, seg_cols, out_terms, middle, sum_down, heads
+    )
+    g_input, s_q, s_k, s_v, s_o, s_gate, s_up, attn_row, mlp_row = to_input(
         g_qkv,
         w_attn,
         x,
         g_middle,
         rows_one,
+        branch,
+        heads_out,
         sum_both,
         (q_weight, k_weight, v_weight, gate_weight, up_weight),
         (gain_one, gain_two),

time: 528 us -> 515 us (0.975)
  Pallas kernels: 485 us -> 473 us
    pallas_call x7, Pallas kernels: 457 us -> 446 us  [call(): pl.pallas_call(kernel, in_specs=spaces or [vmem] * len(arrays), out_specs...]
  transfers between devices with their start and end apart: 4 -> 4, of which waited for: 2 -> 1; matrix products, arithmetic and copies ran while one was open for 0% -> 0% of each run, Pallas kernels for 67% -> 66%
where the time goes in v6:
time: 515 us; the launch traced here: 507 us
  Pallas kernels  473 us (92%)
  local copies, waits for them, and re-layouts  15.8 us (3%)
  between operations  14.1 us (3%)
    pallas_call x7, Pallas kernels, call(): pl.pallas_call(kernel, in_specs=spaces or [vmem] * len(arrays), out_specs...  446 us
    pallas_call x1, Pallas kernels, feed_forward(): pl.pallas_call(kernel, in_specs=[hbm] * 6, out_specs=[hbm] * 2, out_shape...  27.4 us
    unnamed x33, local copies, waits for them, and re-layouts  12.3 us
  transfers between devices with their start and end apart: 4, of which 1 were waited for; matrix products, arithmetic and copies ran while one was open for 0% of the time, Pallas kernels for 66%

profile of v6, /device:TPU:0, one launch (start us, length us, event | category | flops | bytes accessed | tf_op | source)
XLA Modules:
  0.0 507.2 jit_solution(2644483494909369462)
XLA Ops:
  7.2 0.0 all-gather.3.cloned.1.call-start
  7.2 0.7 bitcast_convert_fusion.1
  7.9 0.7 bitcast_convert_fusion
  8.5 0.7 copy.34.two_ref.gain_two_ref
  9.3 0.7 copy.33.one_ref.gain_ref
  10.0 63.1 %front.1 = (bf16[2048,1024]{1,0:T(8,128)(2,1)}, bf16[256,1024]{1,0:T(8,128)(2,1)}, s32[4,1,512]{2,1,0:T(1,128)}, bf16[4,4,128,576]{3,2,1,0:T(8,128)(2,1)}, bf16[...) custom-call(bf16[512,2048]{1,0:T(8,128)(2,1)} %bitcast.22, s32[1,1,512]{2,1,0:T(1,128)} %bitcast.33, ...), custom_call_target="tpu_custom_call" | custom-call | bytes 4852736 | tf_op jit(solution)/shard_map/front/pallas_call | solution.py:664
  73.1 0.0 all-gather.3.cloned.1.call-update
  73.1 0.0 all-gather.5.cloned.1.call-start
  73.2 2.0 copy.35.row_ref
  75.2 45.7 %attend.1 = (bf16[2048,320]{1,0:T(8,128)(2,1)}, f32[2048,256]{1,0:T(8,128)}, f32[2048,2]{1,0:T(8,128)}, bf16[2048,256]{1,0:T(8,128)(2,1)}, bf16[2048,1024]{1,0:T(8,128)(2,1)}, /*index=5*/bf16[2048,2048]{1,0:T(8,128)(2,1)}) custom-call(bf16[2048,1024]{1,0:T(8,128)(2,1)} %get-tuple-element.50.x_ref, bf16[256,1024]{1,0:T(8,128)(2,1)} %get-tuple-element.51.own_ref, ...), custom_call_target="tpu_custom_call" | custom-call | bytes 9191424 | tf_op jit(solution)/shard_map/attend/pallas_call | solution.py:664
  120.9 0.0 all-gather.5.cloned.1.call-update
  121.0 0.5 reduce-scatter.3.cloned.1.call-start
  121.5 79.9 %to_middle.1 = (f32[256,2048]{1,0:T(8,128)}, bf16[2048,2048]{1,0:T(8,128)(2,1)}) custom-call(bf16[2048,256]{1,0:T(8,128)(2,1)} %get-tuple-element.57.h_ref, bf16[2048,576]{1,0:T(8,128)(2,1)} %bitcast.19, bf16[512,2048]{1,0:T(8,128)(2,1)} %bitcast.23), custom_call_target="tpu_custom_call" | custom-call | flops 2147483648 | bytes 5505024 | tf_op jit(solution)/shard_map/to_middle/pallas_call | solution.py:664
  201.3 0.0 all-gather.3.cloned.1.call-done
  201.4 39.6 %gate_up.1 = (bf16[2048,704]{1,0:T(8,128)(2,1)}, bf16[2048,704]{1,0:T(8,128)(2,1)}, bf16[2048,704]{1,0:T(8,128)(2,1)}, bf16[2048,1024]{1,0:T(8,128)(2,1)}, bf16[2048,704]{1,0:T(8,128)(2,1)}) custom-call(bf16[2048,2048]{1,0:T(8,128)(2,1)} %get-tuple-element.58.x_ref.two_ref, bf16[2048,1408]{1,0:T(8,128)(2,1)} %bitcast.34, bf16[512,2048]{1,0:T(8,128)(2,1)} %bitcast.28, ...), custom_call_target="tpu_custom_call" | custom-call | flops 11811160064 | bytes 20447232 | tf_op jit(solution)/shard_map/gate_up/pallas_call | solution.py:664
  241.0 0.0 reduce-scatter.3.cloned.1.call-update
  241.0 0.0 reduce-scatter.5.cloned.1.call-start
  241.1 2.3 all-gather.5.cloned.1.call-done
  243.4 27.4 %feed_forward.1 = (bf16[2048,1408]{1,0:T(8,128)(2,1)}, bf16[2048,1408]{1,0:T(8,128)(2,1)}) custom-call(bf16[2048,704]{1,0:T(8,128)(2,1)} %get-tuple-element.61.slope_ref, bf16[2048,704]{1,0:T(8,128)(2,1)} %get-tuple-element.62.silu_ref, bf16[2048,1024]{1,0:T(8,128)(2,1)} %get-tuple-element.60.low_ref, bf16[2048,1024]{1,0:T(8,128)(2,1)} %get-tuple-element.63.high_ref, ...), custom_call_target="tpu_custom_call" | custom-call | flops 17716740096 | bytes 36962304 | tf_op jit(solution)/shard_map/feed_forward/pallas_call | solution.py:1466
  270.8 0.0 reduce-scatter.5.cloned.1.call-update
  270.8 88.8 %to_branch.1 = (f32[256,2048]{1,0:T(8,128)}, bf16[2048,2048]{1,0:T(8,128)(2,1)}, bf16[2048,256]{1,0:T(8,128)(2,1)}, bf16[2048,2048]{1,0:T(8,128)(2,1)}) custom-call(bf16[2048,1408]{1,0:T(8,128)(2,1)} %get-tuple-element.65.g_ref, bf16[2048,1408]{1,0:T(8,128)(2,1)} %bitcast.35, f32[256,2048]{1,0:T(8,128)} %get-tuple-element.66.mid_ref, ...), custom_call_target="tpu_custom_call" | custom-call | flops 16106127360 | bytes 24117248 | tf_op jit(solution)/shard_map/to_branch/pallas_call | solution.py:664
  359.6 0.0 reduce-scatter.3.cloned.1.call-done.down_ref
  359.6 52.8 %attend_back.1 = (bf16[2048,320]{1,0:T(8,128)(2,1)}, bf16[512,2048]{1,0:T(8,128)(2,1)}, f32[128,2816]{1,0:T(8,128)}) custom-call(bf16[2048,320]{1,0:T(8,128)(2,1)} %get-tuple-element.54.x_ref, bf16[2048,256]{1,0:T(8,128)(2,1)} %get-tuple-element.68.gm_ref, f32[2048,256]{1,0:T(8,128)} %get-tuple-element.69.m_ref, f32[2048,2]{1,0:T(8,128)} %get-tuple-element.70.d_ref, ...), custom_call_target="tpu_custom_call" | custom-call | bytes 15695872 | tf_op jit(solution)/shard_map/attend_back/pallas_call | solution.py:664
  412.4 0.0 reduce-scatter.5.cloned.1.call-done.both_ref
  412.4 0.0 copy-start.1
  412.4 75.7 %to_input.1 = (f32[512,2048]{1,0:T(8,128)}, f32[128,128]{1,0:T(8,128)}, f32[128,128]{1,0:T(8,128)}, f32[128,1024]{1,0:T(8,128)}, f32[128,1024]{1,0:T(8,128)}, /*...) custom-call(bf16[2048,320]{1,0:T(8,128)(2,1)} %get-tuple-element.74.g_ref, ...), custom_call_target="tpu_custom_call" | custom-call | flops 2684354560 | bytes 28902400 | tf_op jit(solution)/shard_map/to_input/pallas_call | solution.py:664
  488.2 0.0 copy-start
  488.2 0.0 copy-done.1
  488.2 1.3 copy.50
  489.5 1.6 copy-done
  491.1 0.0 copy-start.4
  491.1 2.1 copy.51
  493.3 0.0 copy-done.8
  493.3 0.6 copy.52
  493.9 0.0 copy-done.7
  493.9 0.6 copy.53
  494.5 0.0 copy-done.6
  494.5 0.8 copy.54
  495.3 0.0 copy-done.5
  495.3 0.8 copy.55
  496.1 0.0 copy-done.4
  496.1 1.1 copy.56
  497.2 0.0 copy-done.3
  497.2 1.1 copy.57
  498.3 1.1 copy.58
  499.4 0.5 copy.59
  500.0 0.0 copy-done.9
  500.0 0.5 copy.60
  (10 shorter events, 0.0 us)
Async XLA Ops:
  7.2 194.2 %all-gather.3.cloned.1.call-start = ((), (), s32[]{:S(2)}) async-start(), calls=%async_computation.2 | async-start | bytes 7208960 | tf_op jit(solution)/shard_map/all_gather | solution.py:1868
  73.1 170.2 %all-gather.5.cloned.1.call-start = ((), (), s32[]{:S(2)}) async-start(), calls=%async_computation.3 | async-start | bytes 3932160 | tf_op jit(solution)/shard_map/all_gather | solution.py:1874
  121.0 238.7 %reduce-scatter.3.cloned.1.call-start = ((), (), s32[]{:S(2)}) async-start(), calls=%async_computation.4 | async-start | bytes 3932160 | tf_op jit(solution)/shard_map/reduce_scatter | solution.py:1877
  241.0 171.4 %reduce-scatter.5.cloned.1.call-start = ((), (), s32[]{:S(2)}) async-start(), calls=%async_computation.5 | async-start | bytes 7208960 | tf_op jit(solution)/shard_map/reduce_scatter | solution.py:1879
  412.4 75.8 %copy-start.1 = (bf16[512,2048]{1,0:T(8,128)(2,1)S(1)}, bf16[512,2048]{1,0:T(8,128)(2,1)}, u32[]{:S(2)}) copy-start(bf16[512,2048]{1,0:T(8,128)(2,1)} %get-tuple-element.73) | copy-start | bytes 6291460
  488.2 2.9 copy-start
  491.1 2.2 copy-start.8
  491.1 2.8 copy-start.7
  491.1 3.4 copy-start.6
  491.1 4.2 copy-start.5
  491.1 5.0 copy-start.4
  493.3 4.0 copy-start.3
  496.1 2.2 copy-start.2
  497.2 2.2 copy-start.10
  497.2 2.7 copy-start.9
Sparse Core Ops, SparseCore 0:
  73.2 106.6 all-gather.2
  181.5 61.7 all-gather.4
  245.7 58.8 reduce-scatter.2
  306.8 102.2 reduce-scatter.4

commit v7 on v6

--- a/solution.py
+++ b/solution.py
@@ -517,6 +517,9 @@
     return hand_on, landed
 
 
+PARTS = 2
+
+
 def scatter_order(i):
     c = lax.axis_index("ctx")
     across = 3 - i
@@ -533,11 +536,11 @@
 
     def link(k, n):
         return remote(
-            over.at[k, n], came.at[k, n], send, receive, 8 + 2 * k + n, to_x if k % 2 == 0 else to_y
+            over.at[k, n], came.at[k, n], send, receive, PARTS * (4 + k) + n, to_x if k % 2 == 0 else to_y
         )
 
     def core(i, n):
-        return remote(to_core.at[lax.rem(i, 2), n], from_core.at[i, n], send, receive, 2 * i + n, to_t)
+        return remote(to_core.at[lax.rem(i, 2), n], from_core.at[i, n], send, receive, PARTS * i + n, to_t)
 
     def total(i, h, n, *extra):
         out = kept[i % 3, n, pl.ds(h * half, half), :]
@@ -573,52 +576,61 @@
         return pl.multiple_of(2 * scatter_order(i) * own, 2 * own)
 
     pairs = terms(0, begin(0))
-    product(pairs, 0, 0)
-    enter()
-    core(0, 0).start()
-    product(pairs, 0, 1)
-    core(0, 1).start()
-    for n in (0, 1):
-        joined(0, n)
-        go(0, 0, 0, n)
-        go(1, 0, 1, n)
+    for n in range(PARTS):
+        product(pairs, 0, n)
+        if n == 0:
+            enter()
+        core(0, n).start()
+        if n > 0:
+            joined(0, n - 1)
+            go(0, 0, 0, n - 1)
+            go(1, 0, 1, n - 1)
+    joined(0, PARTS - 1)
+    go(0, 0, 0, PARTS - 1)
+    go(1, 0, 1, PARTS - 1)
 
     def step(i, carry):
         pairs = terms(i, begin(i))
 
         @pl.when(i >= 2)
         def _():
-            for n in (0, 1):
+            for n in range(PARTS):
                 core(i - 2, n).wait_send()
 
-        for n in (0, 1):
+        product(pairs, i, 0)
+        core(i, 0).start()
+
+        @pl.when(i == 2)
+        def _():
+            for n in range(PARTS):
+                joined(1, n)
+                go(3, 1, 1, n)
+
+        @pl.when(i == 3)
+        def _():
+            for n in range(PARTS):
+                joined(2, n)
+                go(2, 2, 0, n)
+
+        for n in range(1, PARTS):
             product(pairs, i, n)
             core(i, n).start()
 
-        @pl.when(i == 2)
-        def _():
-            for n in (0, 1):
-                joined(1, n)
-                go(3, 1, 1, n)
-
         return carry
 
     lax.fori_loop(1, 4, step, 0)
-    for n in (0, 1):
-        joined(2, n)
-        go(2, 2, 0, n)
     if fill is not None:
         fill(0)
-    for n in (0, 1):
+    for n in range(PARTS):
         link(0, n).wait_recv()
         link(1, n).wait_recv()
         go(4, 2, 1, n, 1)
         go(5, 1, 0, n, 0)
-    for n in (0, 1):
+    for n in range(PARTS):
         joined(3, n)
     if fill is not None:
         fill(1)
-    for n in (0, 1):
+    for n in range(PARTS):
         for k in (2, 3, 4, 5):
             link(k, n).wait_recv()
         core(2, n).wait_send()
@@ -628,23 +640,23 @@
     return jnp.concatenate(
         [
             jnp.concatenate([total(3, 0, n, 2, 5), total(3, 1, n, 3, 4)], axis=0)
-            for n in (0, 1)
+            for n in range(PARTS)
         ],
         axis=1,
     )
 
 
-SCATTER_COPIES = 20
+SCATTER_COPIES = 10 * PARTS
 
 
 def scatter_scratch(own, width):
-    tile = width // 2
+    tile = width // PARTS
     return [
-        pltpu.VMEM((2, 2, own, tile), BF16),
-        pltpu.VMEM((4, 2, own, tile), BF16),
-        pltpu.VMEM((3, 2, own, tile), F32),
-        pltpu.VMEM((6, 2, own // 2, tile), BF16),
-        pltpu.VMEM((6, 2, own // 2, tile), BF16),
+        pltpu.VMEM((2, PARTS, own, tile), BF16),
+        pltpu.VMEM((4, PARTS, own, tile), BF16),
+        pltpu.VMEM((3, PARTS, own, tile), F32),
+        pltpu.VMEM((6, PARTS, own // 2, tile), BF16),
+        pltpu.VMEM((6, PARTS, own // 2, tile), BF16),
         pltpu.VMEM((2 * own, tile), F32),
     ]
 
@@ -683,6 +695,10 @@
     return lax.rem(d + k, lax.axis_size("dp"))
 
 
+def as_column(row):
+    return jnp.transpose(jnp.broadcast_to(row, (128, row.shape[1])), (1, 0))[:, :1]
+
+
 def columns(ref, gain, start, count):
     low = start // 128 * 128
     high = -(-(start + count) // 128) * 128
@@ -692,8 +708,46 @@
     return value[:, start - low : start - low + count]
 
 
-def whole_tiles(count):
-    return -(-count // 128) * 128
+def packed_down(held, units):
+    return units // 128 * held + (held // 2 if units % 128 else 0)
+
+
+def down_scratch(w_down, units):
+    return [
+        pltpu.VMEM((w_down.shape[0], w_down.shape[1] * 128 // units, -(-units // 128) * 128), BF16),
+        pltpu.VMEM((w_down.shape[0], w_down.shape[1] * 64 // units, 128), BF16),
+        pltpu.SemaphoreType.DMA((-(-units // 128),)),
+    ]
+
+
+def load_down(w_ref, w_buf, rest_buf, load, units):
+    held = w_buf.shape[1]
+    tiles = units // 128
+    copies = [
+        pltpu.make_async_copy(
+            w_ref.at[:, n * held : (n + 1) * held], w_buf.at[:, :, n * 128 : (n + 1) * 128], load.at[n]
+        )
+        for n in range(tiles)
+    ]
+    if units % 128:
+        copies.append(pltpu.make_async_copy(w_ref.at[:, tiles * held :], rest_buf, load.at[tiles]))
+
+    def finish():
+        for copy in copies:
+            copy.wait()
+        if units % 128:
+            w_buf[:, : held // 2, tiles * 128 : units] = rest_buf[:, :, :64]
+            w_buf[:, held // 2 :, tiles * 128 : units] = rest_buf[:, :, 64:]
+
+    for copy in copies:
+        copy.start()
+    return finish
+
+
+def down_rows(w_buf, first, last, units):
+    held = w_buf.shape[1]
+    rows = w_buf[first // held : last // held, :, :units]
+    return rows.reshape(last - first, units)
 
 
 def front(x, seg, weights, gains, tokens, heads):
@@ -705,7 +759,7 @@
     main = units // 128 * 128
     packed = 2 * wide + 2 * narrow
     part_width = width // 2
-    filled = whole_tiles(units)
+    down_shape = (4, packed_down(held, units), 128)
     line = {
         0: (((0, 2),), ((0, 1),), ()),
         1: (((1, 0),), ((1, 2), (1, 3)), ((3, 0),)),
@@ -774,7 +828,7 @@
             for slot, (s, to) in enumerate(first + then + on):
                 shard(slot, s, to).wait_send()
 
-        one, two = one_ref[...], two_ref[...]
+        one, two = as_column(one_ref[...].astype(F32)), as_column(two_ref[...].astype(F32))
         met = (
             [(d, beside(c, k), t) for k in (1, 2, 3)]
             + [(d, c, 1 - t)]
@@ -816,10 +870,15 @@
                 for k in (3, 1, 2):
                     out(n, k).start()
             for b in range(4):
-                part = columns(d_ref, None, b * units, units)
-                if units < filled:
-                    part = jnp.concatenate([part, jnp.zeros((held, filled - units), F32)], axis=1)
-                cut_d[b] = part.astype(BF16)
+                for n in range(units // 128):
+                    cut_d[b, n * held : (n + 1) * held, :] = columns(
+                        d_ref, None, b * units + n * 128, 128
+                    ).astype(BF16)
+                if main < units:
+                    part = columns(d_ref, None, b * units + main, units - main)
+                    cut_d[b, units // 128 * held :, :] = jnp.concatenate(
+                        [part[: held // 2], part[held // 2 :]], axis=1
+                    ).astype(BF16)
             local(3).start()
             for k in (3, 1, 2):
                 out(3, k).start()
@@ -849,12 +908,12 @@
             jax.ShapeDtypeStruct((4,) + seg.shape, seg.dtype),
             jax.ShapeDtypeStruct((deep, 4, held, packed), BF16),
             jax.ShapeDtypeStruct((4, held, 2 * units), BF16),
-            jax.ShapeDtypeStruct((4, held, filled), BF16),
+            jax.ShapeDtypeStruct(down_shape, BF16),
         ],
         [
             pltpu.VMEM((4, held, packed), BF16),
             pltpu.VMEM((4, held, 2 * units), BF16),
-            pltpu.VMEM((4, held, filled), BF16),
+            pltpu.VMEM(down_shape, BF16),
         ]
         + gather_scratch(tokens, part_width) + sems(12) + sems(deep) + [pltpu.SemaphoreType.DMA((4,))],
         [vmem, hbm] + [vmem] * 9,
@@ -1374,7 +1433,8 @@
 
     def kernel(
         slope_ref, silu_ref, low_ref, high_ref, d_ref, two_ref, g_out, grad_ref,
-        slope_buf, silu_buf, low_buf, high_buf, d_buf, g_ref, here, g_store, cols, out, load, store,
+        slope_buf, silu_buf, low_buf, high_buf, d_buf, rest_buf, d_load, g_ref, here, g_store, cols,
+        out, load, store,
     ):
         def rows(i):
             return pl.ds(pl.multiple_of(i * BLOCK, BLOCK), BLOCK)
@@ -1406,12 +1466,11 @@
             slot = lax.rem(n, 2)
             return pltpu.make_async_copy(out.at[slot], grad_ref.at[part], store.at[slot])
 
-        weights = pltpu.make_async_copy(d_ref, d_buf, load.at[2])
-        weights.start()
+        weights_there = load_down(d_ref, d_buf, rest_buf, d_load, units)
         for copy in fetch(0):
             copy.start()
         wanted(0).start()
-        weights.wait()
+        weights_there()
 
         @pl.loop(0, count)
         def _(i):
@@ -1424,8 +1483,8 @@
 
             for copy in fetch(i):
                 copy.wait()
-            g_hidden = dot(low_buf[slot], d_buf[:part_width, :units], 1, 0) + dot(
-                high_buf[slot], d_buf[part_width:, :units], 1, 0
+            g_hidden = dot(low_buf[slot], down_rows(d_buf, 0, part_width, units), 1, 0) + dot(
+                high_buf[slot], down_rows(d_buf, part_width, width, units), 1, 0
             )
             gg = g_hidden * slope_buf[slot].astype(F32)
             gu = g_hidden * silu_buf[slot].astype(F32)
@@ -1476,7 +1535,7 @@
             pltpu.VMEM((2, BLOCK, units), BF16),
             pltpu.VMEM((2, BLOCK, part_width), BF16),
             pltpu.VMEM((2, BLOCK, part_width), BF16),
-            pltpu.VMEM(w_down.shape, BF16),
+            *down_scratch(w_down, units),
             pltpu.VMEM((tokens, 2 * units), BF16),
             pltpu.SemaphoreType.DMA((4, 2)),
             pltpu.SemaphoreType.DMA((count,)),
@@ -1501,7 +1560,7 @@
 
     def kernel(
         g_ref, w_ref, mid_ref, cot_ref, o_ref, hid_ref, d_ref, gm_ref, rows_out, mix_ref, term_ref,
-        g_buf, w_buf, hid_buf, d_buf, term_buf, load, term_store,
+        g_buf, w_buf, hid_buf, d_buf, rest_buf, d_load, term_buf, load, term_store,
         mid_buf, cot_buf, o_buf, gm_buf, large, *rest,
     ):
         bufs, (s_send, s_receive, rows_ref, g_send, g_receive, store) = rest[:6], rest[6:]
@@ -1524,8 +1583,7 @@
         fetch(0).start()
         say(around())
         weights.wait()
-        down = pltpu.make_async_copy(d_ref, d_buf, load.at[3])
-        down.start()
+        down_there = load_down(d_ref, d_buf, rest_buf, d_load, units)
         for copy in loads:
             copy.start()
         pltpu.make_async_copy(
@@ -1575,16 +1633,15 @@
 
                 for n in (0, 1):
                     columns = slice(n * tile, (n + 1) * tile)
-                    term_buf[:, columns] = dot(
-                        hid_buf[...], d_buf[columns, :units], 1, 1
-                    ).astype(BF16)
+                    matrix = down_rows(d_buf, n * tile, (n + 1) * tile, units)
+                    term_buf[:, columns] = dot(hid_buf[...], matrix, 1, 1).astype(BF16)
                 term_given(i).start()
 
                 @pl.when(i + 1 < tokens // BLOCK)
                 def _():
                     hidden_of(i + 1).start()
 
-        down.wait()
+        down_there()
         blocks = tokens // BLOCK
         gather_rows(
             rows_ref, rows_out, g_send, g_receive, store, mix,
@@ -1608,7 +1665,7 @@
             pltpu.VMEM((2, 2 * own, g_both.shape[1]), BF16),
             pltpu.VMEM(w_both.shape, BF16),
             pltpu.VMEM((BLOCK, units), BF16),
-            pltpu.VMEM(w_down.shape, BF16),
+            *down_scratch(w_down, units),
             pltpu.VMEM((BLOCK, width), BF16),
             pltpu.SemaphoreType.DMA((5,)),
             pltpu.SemaphoreType.DMA((1,)),
@@ -1747,7 +1804,7 @@
                         pieces.append(whole[b][:, rest_of : rest_of + units - main])
                 s = jnp.concatenate(pieces, axis=1)
                 term = term + jnp.sum(s * weight[...].astype(F32), axis=1, keepdims=True)
-                ref[...] = s * gain_two_ref[...]
+                ref[...] = s * as_column(gain_two_ref[...].astype(F32))
             for copy in wide_stores:
                 copy.start()
             scalar[0, 1] = as_row(term)
@@ -1769,6 +1826,7 @@
             go_ref[:, b * wide : (b + 1) * wide] = parts_o[b].astype(F32)
         landed(0)
 
+        gain_one = as_column(gain_ref[...].astype(F32))
         term_one = jnp.zeros((held, 1), F32)
         for ref, weight, start, count in (
             (gv_ref, wv_ref, 0, wide),
@@ -1779,7 +1837,7 @@
                 [parts_a[b][:, start : start + count].astype(F32) for b in range(4)], axis=1
             )
             term_one = term_one + jnp.sum(s * weight[...].astype(F32), axis=1, keepdims=True)
-            ref[...] = s * gain_ref[...]
+            ref[...] = s * gain_one
         scalar[0, 0] = as_row(term_one)
         swap = remote(scalar.at[0], scalar.at[1], t_send, t_receive, 1, (d, c, 1 - t))
         swap.start()
@@ -1854,8 +1912,7 @@
     heads = q_weight.shape[1] // F // parts
     tokens = activations.shape[1] * parts
     x, cot_block = activations[0], cotangent[0]
-    gain_one = attn_gain.astype(F32)[:, None]
-    gain_two = mlp_gain.astype(F32)[:, None]
+    gain_one, gain_two = attn_gain[None], mlp_gain[None]
     rows_low, own_high, segments, w_attn, cut_both, cut_down = front(
         x,
         seg_ids,
@@ -1871,7 +1928,7 @@
         rows_low, own_high, w_attn, seg_rows, seg_cols, cot_block, heads
     )
     cut_down, heads_out = lax.optimization_barrier((cut_down, heads_out))
-    w_down = lax.all_gather(cut_down, "dp", axis=0, tiled=True).reshape(-1, cut_down.shape[2])
+    w_down = lax.all_gather(cut_down, "dp", axis=0, tiled=True)
     middle, rows_two = to_middle(heads_out, w_attn, x)
     hidden, slope, silu, cot_high, back_down = gate_up(rows_two, w_both, cot_block, cot_low)
     sum_down = lax.psum_scatter(back_down, "dp", scatter_dimension=0, tiled=True)
@@ -1912,8 +1969,10 @@
 
 
 def layer(*arrays):
-    heads = arrays[3].shape[1] // F
-    plan = shards if heads % lax.axis_size("ctx") else plane_shards
+    heads, units = arrays[3].shape[1] // F, arrays[7].shape[1]
+    fits = lax.axis_size("ctx") == 4 and lax.axis_size("tp") == 2
+    fits = fits and heads % 4 == 0 and units % 256 == 0
+    plan = plane_shards if fits else shards
     return plan(*arrays)
 
 

time: 515 us -> 507 us (0.984)
  transfers between devices with their start and end apart: 4 -> 4, of which waited for: 1 -> 0; matrix products, arithmetic and copies ran while one was open for 0% -> 0% of each run, Pallas kernels for 66% -> 66%
where the time goes in v7:
time: 507 us; the launch traced here: 500 us
  Pallas kernels  471 us (93%)
  local copies, waits for them, and re-layouts  14.3 us (3%)
  between operations  14.1 us (3%)
    pallas_call x7, Pallas kernels, call(): pl.pallas_call(kernel, in_specs=spaces or [vmem] * len(arrays), out_specs...  443 us
    pallas_call x1, Pallas kernels, feed_forward(): pl.pallas_call(kernel, in_specs=[hbm] * 6, out_specs=[hbm] * 2, out_shape...  27.3 us
    unnamed x33, local copies, waits for them, and re-layouts  12.3 us
  transfers between devices with their start and end apart: 4, of which 0 were waited for; matrix products, arithmetic and copies ran while one was open for 0% of the time, Pallas kernels for 66%

profile of v7, /device:TPU:0, one launch (start us, length us, event | category | flops | bytes accessed | tf_op | source)
XLA Modules:
  0.0 499.8 jit_solution(18313267499517783266)
XLA Ops:
  7.2 0.0 all-gather.3.cloned.1.call-start
  7.2 63.2 %front.1 = (bf16[2048,1024]{1,0:T(8,128)(2,1)}, bf16[256,1024]{1,0:T(8,128)(2,1)}, s32[4,1,512]{2,1,0:T(1,128)}, bf16[4,4,128,576]{3,2,1,0:T(8,128)(2,1)}, bf16[...) custom-call(bf16[512,2048]{1,0:T(8,128)(2,1)} %bitcast.17, s32[1,1,512]{2,1,0:T(1,128)} %bitcast.28, ...), custom_call_target="tpu_custom_call" | custom-call | bytes 4852224 | tf_op jit(solution)/shard_map/front/pallas_call | solution.py:676
  70.4 0.0 all-gather.3.cloned.1.call-update
  70.4 0.0 all-gather.5.cloned.1.call-start
  70.5 2.0 copy.25.row_ref
  72.5 45.7 %attend.1 = (bf16[2048,320]{1,0:T(8,128)(2,1)}, f32[2048,256]{1,0:T(8,128)}, f32[2048,2]{1,0:T(8,128)}, bf16[2048,256]{1,0:T(8,128)(2,1)}, bf16[2048,1024]{1,0:T(8,128)(2,1)}, /*index=5*/bf16[2048,2048]{1,0:T(8,128)(2,1)}) custom-call(bf16[2048,1024]{1,0:T(8,128)(2,1)} %get-tuple-element.50.x_ref, bf16[256,1024]{1,0:T(8,128)(2,1)} %get-tuple-element.51.own_ref, ...), custom_call_target="tpu_custom_call" | custom-call | bytes 9191424 | tf_op jit(solution)/shard_map/attend/pallas_call | solution.py:676
  118.2 0.0 all-gather.5.cloned.1.call-update
  118.2 0.5 reduce-scatter.3.cloned.1.call-start
  118.8 79.9 %to_middle.1 = (f32[256,2048]{1,0:T(8,128)}, bf16[2048,2048]{1,0:T(8,128)(2,1)}) custom-call(bf16[2048,256]{1,0:T(8,128)(2,1)} %get-tuple-element.57.h_ref, bf16[2048,576]{1,0:T(8,128)(2,1)} %bitcast.14, bf16[512,2048]{1,0:T(8,128)(2,1)} %bitcast.18), custom_call_target="tpu_custom_call" | custom-call | flops 2147483648 | bytes 5505024 | tf_op jit(solution)/shard_map/to_middle/pallas_call | solution.py:676
  198.6 0.0 all-gather.3.cloned.1.call-done
  198.7 39.6 %gate_up.1 = (bf16[2048,704]{1,0:T(8,128)(2,1)}, bf16[2048,704]{1,0:T(8,128)(2,1)}, bf16[2048,704]{1,0:T(8,128)(2,1)}, bf16[2048,1024]{1,0:T(8,128)(2,1)}, bf16[2048,704]{1,0:T(8,128)(2,1)}) custom-call(bf16[2048,2048]{1,0:T(8,128)(2,1)} %get-tuple-element.58.x_ref.two_ref, bf16[2048,1408]{1,0:T(8,128)(2,1)} %bitcast.33, bf16[512,2048]{1,0:T(8,128)(2,1)} %bitcast.23, ...), custom_call_target="tpu_custom_call" | custom-call | flops 11811160064 | bytes 20447232 | tf_op jit(solution)/shard_map/gate_up/pallas_call | solution.py:676
  238.3 0.0 reduce-scatter.3.cloned.1.call-update
  238.3 0.0 reduce-scatter.5.cloned.1.call-start
  238.4 0.0 all-gather.5.cloned.1.call-done.d_ref
  238.4 27.3 %feed_forward.1 = (bf16[2048,1408]{1,0:T(8,128)(2,1)}, bf16[2048,1408]{1,0:T(8,128)(2,1)}) custom-call(bf16[2048,704]{1,0:T(8,128)(2,1)} %get-tuple-element.61.slope_ref, bf16[2048,704]{1,0:T(8,128)(2,1)} %get-tuple-element.62.silu_ref, bf16[2048,1024]{1,0:T(8,128)(2,1)} %get-tuple-element.60.low_ref, bf16[2048,1024]{1,0:T(8,128)(2,1)} %get-tuple-element.63.high_ref, ...), custom_call_target="tpu_custom_call" | custom-call | flops 17716740096 | bytes 36962304 | tf_op jit(solution)/shard_map/feed_forward/pallas_call | solution.py:1525
  265.7 0.0 reduce-scatter.5.cloned.1.call-update
  265.7 86.9 %to_branch.1 = (f32[256,2048]{1,0:T(8,128)}, bf16[2048,2048]{1,0:T(8,128)(2,1)}, bf16[2048,256]{1,0:T(8,128)(2,1)}, bf16[2048,2048]{1,0:T(8,128)(2,1)}) custom-call(bf16[2048,1408]{1,0:T(8,128)(2,1)} %get-tuple-element.65.g_ref, bf16[2048,1408]{1,0:T(8,128)(2,1)} %bitcast.34, f32[256,2048]{1,0:T(8,128)} %get-tuple-element.66.mid_ref, ...), custom_call_target="tpu_custom_call" | custom-call | flops 16106127360 | bytes 23855104 | tf_op jit(solution)/shard_map/to_branch/pallas_call | solution.py:676
  352.6 0.0 reduce-scatter.3.cloned.1.call-done.down_ref
  352.6 52.0 %attend_back.1 = (bf16[2048,320]{1,0:T(8,128)(2,1)}, bf16[512,2048]{1,0:T(8,128)(2,1)}, f32[128,2816]{1,0:T(8,128)}) custom-call(bf16[2048,320]{1,0:T(8,128)(2,1)} %get-tuple-element.54.x_ref, bf16[2048,256]{1,0:T(8,128)(2,1)} %get-tuple-element.68.gm_ref, f32[2048,256]{1,0:T(8,128)} %get-tuple-element.69.m_ref, f32[2048,2]{1,0:T(8,128)} %get-tuple-element.70.d_ref, ...), custom_call_target="tpu_custom_call" | custom-call | bytes 15695872 | tf_op jit(solution)/shard_map/attend_back/pallas_call | solution.py:676
  404.6 0.0 reduce-scatter.5.cloned.1.call-done.both_ref
  404.6 0.0 copy-start.1
  404.6 76.1 %to_input.1 = (f32[512,2048]{1,0:T(8,128)}, f32[128,128]{1,0:T(8,128)}, f32[128,128]{1,0:T(8,128)}, f32[128,1024]{1,0:T(8,128)}, f32[128,1024]{1,0:T(8,128)}, /*...) custom-call(bf16[2048,320]{1,0:T(8,128)(2,1)} %get-tuple-element.74.g_ref, ...), custom_call_target="tpu_custom_call" | custom-call | flops 2684354560 | bytes 28901888 | tf_op jit(solution)/shard_map/to_input/pallas_call | solution.py:676
  480.8 0.0 copy-start
  480.8 0.0 copy-done.1
  480.8 1.3 copy.38
  482.1 1.6 copy-done
  483.7 0.0 copy-start.8
  483.7 0.0 copy-start.7
  483.7 0.0 copy-start.4
  483.7 2.1 copy.39
  485.9 0.0 copy-done.8
  485.9 0.6 copy.40
  486.5 0.0 copy-done.7
  486.5 0.6 copy.41
  487.1 0.0 copy-done.6
  487.1 0.8 copy.42
  487.9 0.0 copy-done.5
  487.9 0.8 copy.43
  488.7 0.0 copy-done.4
  488.7 1.1 copy.44
  489.8 0.0 copy-done.3
  489.8 1.1 copy.45
  490.9 0.0 copy-done.2
  490.9 1.1 copy.46
  492.0 0.0 copy-done.10
  492.0 0.5 copy.47
  492.6 0.0 copy-done.9
  492.6 0.5 copy.48
  (6 shorter events, 0.0 us)
Async XLA Ops:
  7.2 191.5 %all-gather.3.cloned.1.call-start = ((), (), s32[]{:S(2)}) async-start(), calls=%async_computation.2 | async-start | bytes 7208960 | tf_op jit(solution)/shard_map/all_gather | solution.py:1925
  70.4 167.9 %all-gather.5.cloned.1.call-start = ((), (), s32[]{:S(2)}) async-start(), calls=%async_computation.3 | async-start | bytes 3604480 | tf_op jit(solution)/shard_map/all_gather | solution.py:1931
  118.2 234.4 %reduce-scatter.3.cloned.1.call-start = ((), (), s32[]{:S(2)}) async-start(), calls=%async_computation.4 | async-start | bytes 3932160 | tf_op jit(solution)/shard_map/reduce_scatter | solution.py:1934
  238.3 166.3 %reduce-scatter.5.cloned.1.call-start = ((), (), s32[]{:S(2)}) async-start(), calls=%async_computation.5 | async-start | bytes 7208960 | tf_op jit(solution)/shard_map/reduce_scatter | solution.py:1936
  404.6 76.2 %copy-start.1 = (bf16[512,2048]{1,0:T(8,128)(2,1)S(1)}, bf16[512,2048]{1,0:T(8,128)(2,1)}, u32[]{:S(2)}) copy-start(bf16[512,2048]{1,0:T(8,128)(2,1)} %get-tuple-element.73) | copy-start | bytes 6291460
  480.8 2.9 copy-start
  483.7 2.2 copy-start.8
  483.7 2.8 copy-start.7
  483.7 3.4 copy-start.6
  483.7 4.2 copy-start.5
  483.7 5.0 %copy-start.4 = (f32[128,2816]{1,0:T(8,128)S(1)}, f32[128,2816]{1,0:T(8,128)}, u32[]{:S(2)}) copy-start(f32[128,2816]{1,0:T(8,128)} %get-tuple-element.106) | copy-start | bytes 4325380
  485.9 4.0 copy-start.3
  488.7 2.2 copy-start.2
  489.8 2.2 copy-start.10
  489.8 2.7 copy-start.9
Sparse Core Ops, SparseCore 0:
  70.6 106.6 all-gather.2
  178.8 57.4 all-gather.4
  238.6 58.9 reduce-scatter.2
  299.8 102.2 reduce-scatter.4

commit v8 on v7

--- a/solution.py
+++ b/solution.py
@@ -1772,6 +1772,7 @@
 
         def enter():
             hear(len(met))
+            hand_on(1)
             for j in range(early):
                 deeper(j).start()
 
@@ -1784,7 +1785,6 @@
 
         def fill(n):
             if n == 0:
-                hand_on(1)
                 for j in range(early, 2 * deep):
                     plane(j)
                     if j % deep != deep - 1:

time: 507 us -> 506 us (level)
  transfers between devices with their start and end apart: 4 -> 4, of which waited for: 0 -> 0; matrix products, arithmetic and copies ran while one was open for 0% -> 0% of each run, Pallas kernels for 66% -> 67%
where the time goes in v8:
time: 506 us; the launch traced here: 498 us
  Pallas kernels  469 us (93%)
  local copies, waits for them, and re-layouts  14.3 us (3%)
  between operations  14.1 us (3%)
    pallas_call x7, Pallas kernels, call(): pl.pallas_call(kernel, in_specs=spaces or [vmem] * len(arrays), out_specs...  441 us
    pallas_call x1, Pallas kernels, feed_forward(): pl.pallas_call(kernel, in_specs=[hbm] * 6, out_specs=[hbm] * 2, out_shape...  27.3 us
    unnamed x33, local copies, waits for them, and re-layouts  12.3 us
  transfers between devices with their start and end apart: 4, of which 0 were waited for; matrix products, arithmetic and copies ran while one was open for 0% of the time, Pallas kernels for 67%

profile of v8, /device:TPU:0, one launch (start us, length us, event | category | flops | bytes accessed | tf_op | source)
XLA Modules:
  0.0 497.8 jit_solution(1216746261183675385)
XLA Ops:
  7.2 0.0 all-gather.3.cloned.1.call-start
  7.2 63.2 %front.1 = (bf16[2048,1024]{1,0:T(8,128)(2,1)}, bf16[256,1024]{1,0:T(8,128)(2,1)}, s32[4,1,512]{2,1,0:T(1,128)}, bf16[4,4,128,576]{3,2,1,0:T(8,128)(2,1)}, bf16[...) custom-call(bf16[512,2048]{1,0:T(8,128)(2,1)} %bitcast.17, s32[1,1,512]{2,1,0:T(1,128)} %bitcast.28, ...), custom_call_target="tpu_custom_call" | custom-call | bytes 4852224 | tf_op jit(solution)/shard_map/front/pallas_call | solution.py:676
  70.4 0.0 all-gather.3.cloned.1.call-update
  70.4 0.0 all-gather.5.cloned.1.call-start
  70.5 2.0 copy.25.row_ref
  72.5 45.7 %attend.1 = (bf16[2048,320]{1,0:T(8,128)(2,1)}, f32[2048,256]{1,0:T(8,128)}, f32[2048,2]{1,0:T(8,128)}, bf16[2048,256]{1,0:T(8,128)(2,1)}, bf16[2048,1024]{1,0:T(8,128)(2,1)}, /*index=5*/bf16[2048,2048]{1,0:T(8,128)(2,1)}) custom-call(bf16[2048,1024]{1,0:T(8,128)(2,1)} %get-tuple-element.50.x_ref, bf16[256,1024]{1,0:T(8,128)(2,1)} %get-tuple-element.51.own_ref, ...), custom_call_target="tpu_custom_call" | custom-call | bytes 9191424 | tf_op jit(solution)/shard_map/attend/pallas_call | solution.py:676
  118.2 0.0 all-gather.5.cloned.1.call-update
  118.2 0.5 reduce-scatter.3.cloned.1.call-start
  118.8 79.9 %to_middle.1 = (f32[256,2048]{1,0:T(8,128)}, bf16[2048,2048]{1,0:T(8,128)(2,1)}) custom-call(bf16[2048,256]{1,0:T(8,128)(2,1)} %get-tuple-element.57.h_ref, bf16[2048,576]{1,0:T(8,128)(2,1)} %bitcast.14, bf16[512,2048]{1,0:T(8,128)(2,1)} %bitcast.18), custom_call_target="tpu_custom_call" | custom-call | flops 2147483648 | bytes 5505024 | tf_op jit(solution)/shard_map/to_middle/pallas_call | solution.py:676
  198.6 0.0 all-gather.3.cloned.1.call-done
  198.7 39.6 %gate_up.1 = (bf16[2048,704]{1,0:T(8,128)(2,1)}, bf16[2048,704]{1,0:T(8,128)(2,1)}, bf16[2048,704]{1,0:T(8,128)(2,1)}, bf16[2048,1024]{1,0:T(8,128)(2,1)}, bf16[2048,704]{1,0:T(8,128)(2,1)}) custom-call(bf16[2048,2048]{1,0:T(8,128)(2,1)} %get-tuple-element.58.x_ref.two_ref, bf16[2048,1408]{1,0:T(8,128)(2,1)} %bitcast.33, bf16[512,2048]{1,0:T(8,128)(2,1)} %bitcast.23, ...), custom_call_target="tpu_custom_call" | custom-call | flops 11811160064 | bytes 20447232 | tf_op jit(solution)/shard_map/gate_up/pallas_call | solution.py:676
  238.3 0.0 reduce-scatter.3.cloned.1.call-update
  238.3 0.0 reduce-scatter.5.cloned.1.call-start
  238.4 0.0 all-gather.5.cloned.1.call-done.d_ref
  238.4 27.3 %feed_forward.1 = (bf16[2048,1408]{1,0:T(8,128)(2,1)}, bf16[2048,1408]{1,0:T(8,128)(2,1)}) custom-call(bf16[2048,704]{1,0:T(8,128)(2,1)} %get-tuple-element.61.slope_ref, bf16[2048,704]{1,0:T(8,128)(2,1)} %get-tuple-element.62.silu_ref, bf16[2048,1024]{1,0:T(8,128)(2,1)} %get-tuple-element.60.low_ref, bf16[2048,1024]{1,0:T(8,128)(2,1)} %get-tuple-element.63.high_ref, ...), custom_call_target="tpu_custom_call" | custom-call | flops 17716740096 | bytes 36962304 | tf_op jit(solution)/shard_map/feed_forward/pallas_call | solution.py:1525
  265.7 0.0 reduce-scatter.5.cloned.1.call-update
  265.7 86.9 %to_branch.1 = (f32[256,2048]{1,0:T(8,128)}, bf16[2048,2048]{1,0:T(8,128)(2,1)}, bf16[2048,256]{1,0:T(8,128)(2,1)}, bf16[2048,2048]{1,0:T(8,128)(2,1)}) custom-call(bf16[2048,1408]{1,0:T(8,128)(2,1)} %get-tuple-element.65.g_ref, bf16[2048,1408]{1,0:T(8,128)(2,1)} %bitcast.34, f32[256,2048]{1,0:T(8,128)} %get-tuple-element.66.mid_ref, ...), custom_call_target="tpu_custom_call" | custom-call | flops 16106127360 | bytes 23855104 | tf_op jit(solution)/shard_map/to_branch/pallas_call | solution.py:676
  352.6 0.0 reduce-scatter.3.cloned.1.call-done.down_ref
  352.6 52.0 %attend_back.1 = (bf16[2048,320]{1,0:T(8,128)(2,1)}, bf16[512,2048]{1,0:T(8,128)(2,1)}, f32[128,2816]{1,0:T(8,128)}) custom-call(bf16[2048,320]{1,0:T(8,128)(2,1)} %get-tuple-element.54.x_ref, bf16[2048,256]{1,0:T(8,128)(2,1)} %get-tuple-element.68.gm_ref, f32[2048,256]{1,0:T(8,128)} %get-tuple-element.69.m_ref, f32[2048,2]{1,0:T(8,128)} %get-tuple-element.70.d_ref, ...), custom_call_target="tpu_custom_call" | custom-call | bytes 15695872 | tf_op jit(solution)/shard_map/attend_back/pallas_call | solution.py:676
  404.6 0.0 reduce-scatter.5.cloned.1.call-done.both_ref
  404.6 0.0 copy-start.1
  404.6 74.1 %to_input.1 = (f32[512,2048]{1,0:T(8,128)}, f32[128,128]{1,0:T(8,128)}, f32[128,128]{1,0:T(8,128)}, f32[128,1024]{1,0:T(8,128)}, f32[128,1024]{1,0:T(8,128)}, /*...) custom-call(bf16[2048,320]{1,0:T(8,128)(2,1)} %get-tuple-element.74.g_ref, ...), custom_call_target="tpu_custom_call" | custom-call | flops 2684354560 | bytes 28901888 | tf_op jit(solution)/shard_map/to_input/pallas_call | solution.py:676
  478.8 0.0 copy-start
  478.8 0.0 copy-done.1
  478.8 1.3 copy.38
  480.1 1.6 copy-done
  481.7 0.0 copy-start.7
  481.7 0.0 copy-start.6
  481.7 0.0 copy-start.4
  481.7 2.1 copy.39
  483.9 0.0 copy-done.8
  483.9 0.6 copy.40
  484.5 0.0 copy-done.7
  484.5 0.6 copy.41
  485.1 0.0 copy-done.6
  485.1 0.8 copy.42
  485.9 0.0 copy-done.5
  485.9 0.8 copy.43
  486.7 0.0 copy-done.4
  486.7 1.1 copy.44
  487.8 0.0 copy-done.3
  487.8 1.1 copy.45
  488.9 0.0 copy-done.2
  488.9 1.1 copy.46
  490.0 0.0 copy-done.10
  490.0 0.5 copy.47
  490.6 0.0 copy-done.9
  490.6 0.5 copy.48
  (6 shorter events, 0.0 us)
Async XLA Ops:
  7.2 191.5 %all-gather.3.cloned.1.call-start = ((), (), s32[]{:S(2)}) async-start(), calls=%async_computation.2 | async-start | bytes 7208960 | tf_op jit(solution)/shard_map/all_gather | solution.py:1925
  70.4 167.9 %all-gather.5.cloned.1.call-start = ((), (), s32[]{:S(2)}) async-start(), calls=%async_computation.3 | async-start | bytes 3604480 | tf_op jit(solution)/shard_map/all_gather | solution.py:1931
  118.2 234.4 %reduce-scatter.3.cloned.1.call-start = ((), (), s32[]{:S(2)}) async-start(), calls=%async_computation.4 | async-start | bytes 3932160 | tf_op jit(solution)/shard_map/reduce_scatter | solution.py:1934
  238.3 166.3 %reduce-scatter.5.cloned.1.call-start = ((), (), s32[]{:S(2)}) async-start(), calls=%async_computation.5 | async-start | bytes 7208960 | tf_op jit(solution)/shard_map/reduce_scatter | solution.py:1936
  404.6 74.2 %copy-start.1 = (bf16[512,2048]{1,0:T(8,128)(2,1)S(1)}, bf16[512,2048]{1,0:T(8,128)(2,1)}, u32[]{:S(2)}) copy-start(bf16[512,2048]{1,0:T(8,128)(2,1)} %get-tuple-element.73) | copy-start | bytes 6291460
  478.8 2.9 copy-start
  481.7 2.2 copy-start.8
  481.7 2.8 copy-start.7
  481.7 3.4 copy-start.6
  481.7 4.2 copy-start.5
  481.7 5.0 %copy-start.4 = (f32[128,2816]{1,0:T(8,128)S(1)}, f32[128,2816]{1,0:T(8,128)}, u32[]{:S(2)}) copy-start(f32[128,2816]{1,0:T(8,128)} %get-tuple-element.106) | copy-start | bytes 4325380
  483.9 4.0 copy-start.3
  486.7 2.2 copy-start.2
  487.8 2.2 copy-start.10
  487.8 2.7 copy-start.9
Sparse Core Ops, SparseCore 0:
  70.6 106.6 all-gather.2
  178.8 57.4 all-gather.4
  238.6 58.9 reduce-scatter.2
  299.8 102.2 reduce-scatter.4

commit v9 on v8

--- a/solution.py
+++ b/solution.py
@@ -1044,8 +1044,9 @@
                 prepare()
                 pl.loop(0, 1)(one_block)
             else:
-                pl.loop(1, blocks)(one_block)
+                pl.loop(1, blocks - 1)(one_block)
                 hand_on(0)
+                one_block(blocks - 1)
 
         moved = scatter_rows(terms, bufs, s_send, s_receive, lambda: hear(len(met)), fill)
         loads[2].wait()

time: 506 us -> 515 us (1.018)
  Pallas kernels: 469 us -> 476 us
    pallas_call x1, Pallas kernels: 27.3 us -> 35.2 us  [feed_forward(): pl.pallas_call(kernel, in_specs=[hbm] * 6, out_specs=[hbm] * 2, out_shape...]
where the time goes in v9:
time: 515 us; the launch traced here: 505 us
  Pallas kernels  476 us (92%)
  local copies, waits for them, and re-layouts  14.3 us (3%)
  between operations  14.1 us (3%)
    pallas_call x7, Pallas kernels, call(): pl.pallas_call(kernel, in_specs=spaces or [vmem] * len(arrays), out_specs...  441 us
    pallas_call x1, Pallas kernels, feed_forward(): pl.pallas_call(kernel, in_specs=[hbm] * 6, out_specs=[hbm] * 2, out_shape...  35.2 us
    unnamed x33, local copies, waits for them, and re-layouts  12.3 us
  transfers between devices with their start and end apart: 4, of which 0 were waited for; matrix products, arithmetic and copies ran while one was open for 0% of the time, Pallas kernels for 67%

profile of v9, /device:TPU:0, one launch (start us, length us, event | category | flops | bytes accessed | tf_op | source)
XLA Modules:
  0.0 505.0 jit_solution(7305499408433922369)
XLA Ops:
  7.2 0.0 all-gather.3.cloned.1.call-start
  7.2 63.2 %front.1 = (bf16[2048,1024]{1,0:T(8,128)(2,1)}, bf16[256,1024]{1,0:T(8,128)(2,1)}, s32[4,1,512]{2,1,0:T(1,128)}, bf16[4,4,128,576]{3,2,1,0:T(8,128)(2,1)}, bf16[...) custom-call(bf16[512,2048]{1,0:T(8,128)(2,1)} %bitcast.17, s32[1,1,512]{2,1,0:T(1,128)} %bitcast.28, ...), custom_call_target="tpu_custom_call" | custom-call | bytes 4852224 | tf_op jit(solution)/shard_map/front/pallas_call | solution.py:676
  70.4 0.0 all-gather.3.cloned.1.call-update
  70.4 0.0 all-gather.5.cloned.1.call-start
  70.5 2.0 copy.25.row_ref
  72.5 45.7 %attend.1 = (bf16[2048,320]{1,0:T(8,128)(2,1)}, f32[2048,256]{1,0:T(8,128)}, f32[2048,2]{1,0:T(8,128)}, bf16[2048,256]{1,0:T(8,128)(2,1)}, bf16[2048,1024]{1,0:T(8,128)(2,1)}, /*index=5*/bf16[2048,2048]{1,0:T(8,128)(2,1)}) custom-call(bf16[2048,1024]{1,0:T(8,128)(2,1)} %get-tuple-element.50.x_ref, bf16[256,1024]{1,0:T(8,128)(2,1)} %get-tuple-element.51.own_ref, ...), custom_call_target="tpu_custom_call" | custom-call | bytes 9191424 | tf_op jit(solution)/shard_map/attend/pallas_call | solution.py:676
  118.2 0.0 all-gather.5.cloned.1.call-update
  118.2 0.3 reduce-scatter.3.cloned.1.call-start
  118.5 79.9 %to_middle.1 = (f32[256,2048]{1,0:T(8,128)}, bf16[2048,2048]{1,0:T(8,128)(2,1)}) custom-call(bf16[2048,256]{1,0:T(8,128)(2,1)} %get-tuple-element.57.h_ref, bf16[2048,576]{1,0:T(8,128)(2,1)} %bitcast.14, bf16[512,2048]{1,0:T(8,128)(2,1)} %bitcast.18), custom_call_target="tpu_custom_call" | custom-call | flops 2147483648 | bytes 5505024 | tf_op jit(solution)/shard_map/to_middle/pallas_call | solution.py:676
  198.4 0.0 all-gather.3.cloned.1.call-done
  198.4 39.6 %gate_up.1 = (bf16[2048,704]{1,0:T(8,128)(2,1)}, bf16[2048,704]{1,0:T(8,128)(2,1)}, bf16[2048,704]{1,0:T(8,128)(2,1)}, bf16[2048,1024]{1,0:T(8,128)(2,1)}, bf16[2048,704]{1,0:T(8,128)(2,1)}) custom-call(bf16[2048,2048]{1,0:T(8,128)(2,1)} %get-tuple-element.58.x_ref.two_ref, bf16[2048,1408]{1,0:T(8,128)(2,1)} %bitcast.33, bf16[512,2048]{1,0:T(8,128)(2,1)} %bitcast.23, ...), custom_call_target="tpu_custom_call" | custom-call | flops 11811160064 | bytes 20447232 | tf_op jit(solution)/shard_map/gate_up/pallas_call | solution.py:676
  238.1 0.0 reduce-scatter.3.cloned.1.call-update
  238.1 0.0 reduce-scatter.5.cloned.1.call-start
  238.1 0.0 all-gather.5.cloned.1.call-done.d_ref
  238.2 35.2 %feed_forward.1 = (bf16[2048,1408]{1,0:T(8,128)(2,1)}, bf16[2048,1408]{1,0:T(8,128)(2,1)}) custom-call(bf16[2048,704]{1,0:T(8,128)(2,1)} %get-tuple-element.61.slope_ref, bf16[2048,704]{1,0:T(8,128)(2,1)} %get-tuple-element.62.silu_ref, bf16[2048,1024]{1,0:T(8,128)(2,1)} %get-tuple-element.60.low_ref, bf16[2048,1024]{1,0:T(8,128)(2,1)} %get-tuple-element.63.high_ref, ...), custom_call_target="tpu_custom_call" | custom-call | flops 17716740096 | bytes 36962304 | tf_op jit(solution)/shard_map/feed_forward/pallas_call | solution.py:1526
  273.3 0.0 reduce-scatter.5.cloned.1.call-update
  273.4 86.6 %to_branch.1 = (f32[256,2048]{1,0:T(8,128)}, bf16[2048,2048]{1,0:T(8,128)(2,1)}, bf16[2048,256]{1,0:T(8,128)(2,1)}, bf16[2048,2048]{1,0:T(8,128)(2,1)}) custom-call(bf16[2048,1408]{1,0:T(8,128)(2,1)} %get-tuple-element.65.g_ref, bf16[2048,1408]{1,0:T(8,128)(2,1)} %bitcast.34, f32[256,2048]{1,0:T(8,128)} %get-tuple-element.66.mid_ref, ...), custom_call_target="tpu_custom_call" | custom-call | flops 16106127360 | bytes 23855104 | tf_op jit(solution)/shard_map/to_branch/pallas_call | solution.py:676
  360.0 0.0 reduce-scatter.3.cloned.1.call-done.down_ref
  360.0 52.0 %attend_back.1 = (bf16[2048,320]{1,0:T(8,128)(2,1)}, bf16[512,2048]{1,0:T(8,128)(2,1)}, f32[128,2816]{1,0:T(8,128)}) custom-call(bf16[2048,320]{1,0:T(8,128)(2,1)} %get-tuple-element.54.x_ref, bf16[2048,256]{1,0:T(8,128)(2,1)} %get-tuple-element.68.gm_ref, f32[2048,256]{1,0:T(8,128)} %get-tuple-element.69.m_ref, f32[2048,2]{1,0:T(8,128)} %get-tuple-element.70.d_ref, ...), custom_call_target="tpu_custom_call" | custom-call | bytes 15695872 | tf_op jit(solution)/shard_map/attend_back/pallas_call | solution.py:676
  412.0 0.0 reduce-scatter.5.cloned.1.call-done.both_ref
  412.0 0.0 copy-start.1
  412.1 73.9 %to_input.1 = (f32[512,2048]{1,0:T(8,128)}, f32[128,128]{1,0:T(8,128)}, f32[128,128]{1,0:T(8,128)}, f32[128,1024]{1,0:T(8,128)}, f32[128,1024]{1,0:T(8,128)}, /*...) custom-call(bf16[2048,320]{1,0:T(8,128)(2,1)} %get-tuple-element.74.g_ref, ...), custom_call_target="tpu_custom_call" | custom-call | flops 2684354560 | bytes 28901888 | tf_op jit(solution)/shard_map/to_input/pallas_call | solution.py:676
  486.0 0.0 copy-start
  486.0 0.0 copy-done.1
  486.0 1.3 copy.38
  487.3 1.6 copy-done
  488.9 0.0 copy-start.7
  488.9 0.0 copy-start.6
  488.9 0.0 copy-start.4
  488.9 2.1 copy.39
  491.1 0.0 copy-done.8
  491.1 0.6 copy.40
  491.7 0.0 copy-done.7
  491.7 0.6 copy.41
  492.3 0.0 copy-done.6
  492.3 0.8 copy.42
  493.1 0.0 copy-done.5
  493.1 0.8 copy.43
  493.9 0.0 copy-done.4
  493.9 1.1 copy.44
  495.0 0.0 copy-done.3
  495.0 1.1 copy.45
  496.1 0.0 copy-done.2
  496.2 1.1 copy.46
  497.3 0.0 copy-done.10
  497.3 0.5 copy.47
  497.8 0.0 copy-done.9
  497.8 0.5 copy.48
  (6 shorter events, 0.0 us)
Async XLA Ops:
  7.2 191.2 %all-gather.3.cloned.1.call-start = ((), (), s32[]{:S(2)}) async-start(), calls=%async_computation.2 | async-start | bytes 7208960 | tf_op jit(solution)/shard_map/all_gather | solution.py:1926
  70.4 167.7 %all-gather.5.cloned.1.call-start = ((), (), s32[]{:S(2)}) async-start(), calls=%async_computation.3 | async-start | bytes 3604480 | tf_op jit(solution)/shard_map/all_gather | solution.py:1932
  118.2 241.8 %reduce-scatter.3.cloned.1.call-start = ((), (), s32[]{:S(2)}) async-start(), calls=%async_computation.4 | async-start | bytes 3932160 | tf_op jit(solution)/shard_map/reduce_scatter | solution.py:1935
  238.1 173.9 %reduce-scatter.5.cloned.1.call-start = ((), (), s32[]{:S(2)}) async-start(), calls=%async_computation.5 | async-start | bytes 7208960 | tf_op jit(solution)/shard_map/reduce_scatter | solution.py:1937
  412.0 73.9 %copy-start.1 = (bf16[512,2048]{1,0:T(8,128)(2,1)S(1)}, bf16[512,2048]{1,0:T(8,128)(2,1)}, u32[]{:S(2)}) copy-start(bf16[512,2048]{1,0:T(8,128)(2,1)} %get-tuple-element.73) | copy-start | bytes 6291460
  486.0 2.9 copy-start
  488.9 2.2 copy-start.8
  488.9 2.8 copy-start.7
  488.9 3.4 copy-start.6
  488.9 4.2 copy-start.5
  488.9 5.0 copy-start.4
  491.1 4.0 copy-start.3
  493.9 2.2 copy-start.2
  495.0 2.2 copy-start.10
  495.0 2.7 copy-start.9
Sparse Core Ops, SparseCore 0:
  70.6 106.6 all-gather.2
  178.8 57.4 all-gather.4
  238.6 58.9 reduce-scatter.2
  299.8 102.2 reduce-scatter.4
